TPU v7x, 32 devices: a whole 2x2x4 slice. The times are simulated.
32 devices in a mesh: grp: 8 (over z, core), tp: 4 (over y, x).
Axes of the slice: x: 2, y: 2, z: 4, core: 2. Of those that a mesh axis runs over, the one named last changes fastest.
Arguments:
- tokens: bfloat16 [8192, 8192], P(('grp', 'tp')), may hold values from -6 to 6
- frozen_weight: bfloat16 [8192, 10240], P(None, 'tp'), may hold values from -0.0625 to 0.0625
- down_weight: bfloat16 [32, 64, 8192], P('grp', None, 'tp'), may hold values from -0.0625 to 0.0625
- up_weight: bfloat16 [32, 64, 10240], P('grp', None, 'tp'), may hold values from -0.75 to 0.75
- adapter_storage_slot: int32 [32], replicated, may hold values from 0 to 31, as said below
- adapter_of_block: int32 [64], replicated, may hold values from 0 to 31, as said below
Outputs:
- qkv: bfloat16 [8192, 10240], P('grp', 'tp')
Inputs may be any that keep to these rules, and one draw needn't show every extreme that they name: `adapter_storage_slot`: each slot is named by exactly one adapter; an adapter with slot s is stored by group s // 4. `adapter_of_block`: the 8 blocks of one group, blocks g * 8 to (g + 1) * 8 - 1, name adapters stored by 8 different groups.
All inputs are finite; a program needn't handle non-finite values.
Results may differ from a plain program's by a relative error of at most 0.0029.
Values may be sent and summed in bfloat16 or wider, within the bound.
No kernel may reach another device: no remote copies, remote signals or barrier semaphores. Data moves between devices by JAX's collectives and lax.ppermute only.
A program may use at most 128 MiB of HBM per device.

v0:
```python
import jax
import jax.numpy as jnp
from jax import lax
from jax.sharding import PartitionSpec as P

BLOCK = 128


adapter_scale = 0.5


def local(tokens, frozen_weight, down_weight, up_weight, adapter_storage_slot, adapter_of_block):
    group_count = lax.axis_size("grp")
    tp_count = lax.axis_size("tp")
    group = lax.axis_index("grp")
    member = lax.axis_index("tp")
    local_rows, width = tokens.shape
    group_rows = local_rows * tp_count
    blocks_here = group_rows // BLOCK
    loaded_here = down_weight.shape[0]
    rank_columns = down_weight.shape[1]
    column_slice = up_weight.shape[2]
    slot_numbers = jnp.take(adapter_storage_slot, adapter_of_block, axis=0)
    owners = slot_numbers // loaded_here
    offsets = slot_numbers % loaded_here
    my_owners = lax.dynamic_slice_in_dim(owners, group * blocks_here, blocks_here)
    owner_grid = owners.reshape(group_count, blocks_here)
    offset_grid = offsets.reshape(group_count, blocks_here)
    owned_here = owner_grid == group
    select_slot = jnp.sum(jnp.where(owned_here, offset_grid, 0), axis=1)
    available = jnp.any(owned_here, axis=1)
    departing_down = jnp.where(
        available[:, None, None], jnp.take(down_weight, select_slot, axis=0), 0
    )
    departing_up = jnp.where(available[:, None, None], jnp.take(up_weight, select_slot, axis=0), 0)
    arrived_a, arrived_b = (
        lax.all_to_all(departing_down, "grp", split_axis=0, concat_axis=0, tiled=True),
        lax.all_to_all(departing_up, "grp", split_axis=0, concat_axis=0, tiled=True),
    )
    down_tile = jnp.take(arrived_a, my_owners, axis=0)
    up_tile = jnp.take(arrived_b, my_owners, axis=0)
    whole_a = lax.all_gather(down_tile, "tp", axis=2, tiled=True)
    span_rows = min(local_rows, BLOCK)
    pieces_here = local_rows // span_rows
    first_block = member * local_rows // BLOCK
    local_a = lax.dynamic_slice_in_dim(whole_a, first_block, pieces_here, 0)
    shrink_local = jnp.einsum(
        "pnd,prd->pnr",
        tokens.reshape(pieces_here, span_rows, width),
        local_a,
        preferred_element_type=jnp.float32,
    )
    shrink_local = shrink_local.astype(jnp.bfloat16).reshape(local_rows, rank_columns)
    shrink = lax.all_gather(shrink_local, "tp", axis=0, tiled=True)
    frozen_rows = jnp.dot(
        lax.all_gather(tokens, "tp", axis=0, tiled=True),
        frozen_weight,
        preferred_element_type=jnp.float32,
    )
    update_rows = jnp.einsum(
        "bnr,brc->bnc",
        shrink.reshape(blocks_here, BLOCK, rank_columns),
        up_tile,
        preferred_element_type=jnp.float32,
    )
    update_rows = update_rows.reshape(group_rows, column_slice)
    return (frozen_rows + adapter_scale * update_rows).astype(jnp.bfloat16)


def solution(mesh):
    placed = (
        P(("grp", "tp"), None),
        P(None, "tp"),
        P("grp", None, "tp"),
        P("grp", None, "tp"),
        P(),
        P(),
    )
    return jax.shard_map(
        local, mesh=mesh, in_specs=placed, out_specs=P("grp", "tp"), check_vma=False
    )
```

profile of v0, /device:TPU:0, one launch (start us, length us, event | category | flops | bytes accessed | tf_op | source)
XLA Modules:
  0.0 380.7 jit_solution(7864684759658232207)
XLA Ops:
  6.5 0.0 copy-start
  6.5 0.8 compare_select_fusion.3
  7.3 1.4 gather_fusion
  8.7 0.7 and_select_fusion
  9.4 0.1 select_n.103
  9.5 0.1 fusion.22
  9.6 0.1 fusion.16
  9.8 1.9 gather_fusion.1
  11.7 1.6 select_select_fusion.1
  13.3 6.3 %all-to-all-start = ((bf16[8,64,2048]{2,1,0:T(8,128)(2,1)}), bf16[8,64,2048]{2,1,0:T(8,128)(2,1)S(1)}, u32[]{:S(2)}, u32[]{:S(2)}) async-start(bf16[8,64,2048]{2,1,0:T(8,128)(2,1)} %select_select_fusion.1), calls=%async_computation | async-start | bytes 4194304 | tf_op jit(solution)/shard_map/all_to_all | solution.py:37
  19.6 0.0 all-gather.5.cloned.1.call-start
  19.7 0.1 compare_and_fusion.1
  19.8 48.9 %all-to-all-done = bf16[8,64,2048]{2,1,0:T(8,128)(2,1)S(1)} async-done(((bf16[8,64,2048]{2,1,0:T(8,128)(2,1)}), bf16[8,64,2048]{2,1,0:T(8,128)(2,1)S(1)}, u32[]{:S(2)}, u32[]{:S(2)}) %all-to-all-start) | async-done | bytes 2097184 | tf_op jit(solution)/shard_map/all_to_all | solution.py:37
  68.7 2.0 gather_fusion.2
  70.7 3.2 broadcast_select_fusion
  73.9 0.0 all-gather.5.cloned.1.call-update
  74.0 0.0 all-gather.3.cloned.1.call-start
  74.0 0.7 all-gather.3.cloned.1.call-update
  74.7 0.0 copy-done
  74.7 2.2 gather_fusion.3
  76.9 3.6 select_select_fusion
  80.5 4.5 %all-to-all-start.1 = ((bf16[8,64,2560]{2,1,0:T(8,128)(2,1)}), bf16[8,64,2560]{2,1,0:T(8,128)(2,1)}, u32[]{:S(2)}, u32[]{:S(2)}) async-start(bf16[8,64,2560]{2,1,0:T(8,128)(2,1)} %select_select_fusion), calls=%async_computation.1 | async-start | bytes 5242880 | tf_op jit(solution)/shard_map/all_to_all | solution.py:38
  85.0 60.3 %all-to-all-done.1 = bf16[8,64,2560]{2,1,0:T(8,128)(2,1)} async-done(((bf16[8,64,2560]{2,1,0:T(8,128)(2,1)}), bf16[8,64,2560]{2,1,0:T(8,128)(2,1)}, u32[]{:S(2)}, u32[]{:S(2)}) %all-to-all-start.1) | async-done | bytes 2621472 | tf_op jit(solution)/shard_map/all_to_all | solution.py:38
  145.3 3.9 %gather_fusion.4 = bf16[8,64,2560]{2,1,0:T(8,128)(2,1)} fusion(bf16[8,64,2560]{2,1,0:T(8,128)(2,1)} %all-to-all-done.1, s32[1024]{0:T(1024)S(1)} %pad_clamp_fusion), kind=kCustom, calls=%fused_computation.4 | custom fusion | bytes 5242912 | tf_op jit(solution)/shard_map/jit(_take)/gather | solution.py:41
  149.2 11.4 %all-gather.5.cloned.1.call-done = bf16[8,64,8192]{2,1,0:T(8,128)(2,1)} async-done(((bf16[8,64,2048]{2,1,0:T(8,128)(2,1)}), bf16[8,64,8192]{2,1,0:T(8,128)(2,1)}) %all-gather.5.cloned.1.call-update) | async-done | bytes 8388624 | tf_op jit(solution)/shard_map/all_gather | solution.py:42
  160.6 0.0 copy-start.2
  160.6 4.5 %fusion.9 = bf16[2,8,8,128]{3,2,1,0:T(8,128)(2,1)S(1)} fusion(bf16[2,128,8192]{2,1,0:T(8,128)(2,1)} %bitcast.25, bf16[8,64,8192]{2,1,0:T(8,128)(2,1)} %all-gather.5.cloned.1.call-done, s32[]{:T(128)S(6)} %select_n.113), kind=kOutput, calls=%fused_computation.17 | convolution fusion | flops 268451840 | bytes 6324228 | tf_op jit(solution)/shard_map/pnd,prd->pnr/dot_general | solution.py:47
  165.2 8.9 %all_gather.11 = bf16[1024,64]{0,1:T(8,128)(2,1)S(1)} all-gather(bf16[256,64]{0,1:T(8,128)(2,1)S(1)} %bitcast.26), channel_id=1, replica_groups=mesh['grp'=8,'tp'=4] {'tp'}, dimensions={0}, use_global_device_ids=true | all-gather | bytes 163840 | tf_op jit(solution)/shard_map/all_gather | solution.py:54
  174.1 0.0 copy-done.2
  174.1 6.2 %convolution_multiply_fusion = f32[8,128,2560]{2,1,0:T(8,128)} fusion(bf16[8,64,2560]{2,1,0:T(8,128)(2,1)S(1)} %copy-done.2, pred[8]{0:T(512)(128)(4,1)S(1)} %get-tuple-element.5, bf16[1024,64]{0,1:T(8,128)(2,1)S(1)} %all_gather.11), kind=kOutput, calls=%fused_computation.7 | convolution fusion | flops 339476480 | bytes 13238280 | tf_op jit(solution)/shard_map/bnr,brc->bnc/dot_general | solution.py:60
  180.4 139.6 %all-gather.3.cloned.1.call-done = bf16[1024,8192]{1,0:T(8,128)(2,1)} async-done(((bf16[256,8192]{1,0:T(8,128)(2,1)}), bf16[1024,8192]{1,0:T(8,128)(2,1)}) %all-gather.3.cloned.1.call-update) | async-done | bytes 16777232 | tf_op jit(solution)/shard_map/all_gather | solution.py:56
  319.9 0.0 copy-start.1
  319.9 53.9 %fusion = bf16[1024,2560]{1,0:T(8,128)(2,1)} fusion(f32[8,128,2560]{2,1,0:T(8,128)} %convolution_multiply_fusion, bf16[1024,8192]{1,0:T(8,128)(2,1)} %all-gather.3.cloned.1.call-done, bf16[8192,2560]{1,0:T(8,128)(2,1)} %param.7), kind=kOutput, calls=%fused_computation.6 | convolution fusion | flops 42954915840 | bytes 74448896 | tf_op jit(solution)/shard_map/dot_general | solution.py:55
  373.9 0.0 copy-done.1
  (6 shorter events, 0.0 us)
Async XLA Ops:
  6.5 68.2 %copy-start = (bf16[4,64,2560]{2,1,0:T(8,128)(2,1)S(1)}, bf16[4,64,2560]{2,1,0:T(8,128)(2,1)}, u32[]{:S(2)}) copy-start(bf16[4,64,2560]{2,1,0:T(8,128)(2,1)} %param.9) | copy-start | bytes 3932164
  13.3 55.4 %all-to-all-start = ((bf16[8,64,2048]{2,1,0:T(8,128)(2,1)}), bf16[8,64,2048]{2,1,0:T(8,128)(2,1)S(1)}, u32[]{:S(2)}, u32[]{:S(2)}) async-start(bf16[8,64,2048]{2,1,0:T(8,128)(2,1)} %select_select_fusion.1), calls=%async_computation | async-start | bytes 4194304 | tf_op jit(solution)/shard_map/all_to_all | solution.py:37
  19.6 141.0 %all-gather.5.cloned.1.call-start = ((), (), s32[]{:S(2)}) async-start(), calls=%async_computation.3 | async-start | bytes 10485760 | tf_op jit(solution)/shard_map/all_gather | solution.py:42
  74.0 246.0 %all-gather.3.cloned.1.call-start = ((), (), s32[]{:S(2)}) async-start(), calls=%async_computation.2 | async-start | bytes 20971520 | tf_op jit(solution)/shard_map/all_gather | solution.py:56
  80.5 64.8 %all-to-all-start.1 = ((bf16[8,64,2560]{2,1,0:T(8,128)(2,1)}), bf16[8,64,2560]{2,1,0:T(8,128)(2,1)}, u32[]{:S(2)}, u32[]{:S(2)}) async-start(bf16[8,64,2560]{2,1,0:T(8,128)(2,1)} %select_select_fusion), calls=%async_computation.1 | async-start | bytes 5242880 | tf_op jit(solution)/shard_map/all_to_all | solution.py:38
  160.6 13.5 %copy-start.2 = (bf16[8,64,2560]{2,1,0:T(8,128)(2,1)S(1)}, bf16[8,64,2560]{2,1,0:T(8,128)(2,1)}, u32[]{:S(2)}) copy-start(bf16[8,64,2560]{2,1,0:T(8,128)(2,1)} %gather_fusion.4) | copy-start | bytes 7864324
  319.9 53.9 %copy-start.1 = (bf16[4,64,2560]{2,1,0:T(8,128)(2,1)S(1)}, bf16[4,64,2560]{2,1,0:T(8,128)(2,1)}, u32[]{:S(2)}) copy-start(bf16[4,64,2560]{2,1,0:T(8,128)(2,1)} %param.9) | copy-start | bytes 3932164
Sparse Core Ops, SparseCore 0:
  74.1 86.5 all-gather.4
  162.5 157.4 all-gather.2
where the time goes:
time: 381 us
  waiting for transfers between devices  261 us (69%)
  matrix products  64.7 us (17%)
  between operations  13.5 us (4%)
  local copies, waits for them, and re-layouts  11.6 us (3%)
  starting transfers between devices  10.9 us (3%)
  other arithmetic  10.2 us (3%)
  blocking collectives  8.94 us (2%)
    all_gather x1, waiting for transfers between devices, local(): lax.all_gather(tokens, 'tp', axis=0, tiled=True)  140 us
    all_to_all x1, waiting for transfers between devices, local(): lax.all_to_all(departing_up, 'grp', split_axis=0, concat_axis=0, tiled=True)  60.3 us
    dot_general x1, matrix products, local(): jnp.dot(lax.all_gather(tokens, 'tp', axis=0, tiled=True), frozen_weight,...  53.9 us
    all_to_all x1, waiting for transfers between devices, local(): lax.all_to_all(departing_down, 'grp', split_axis=0, concat_axis=0, tiled=...  48.9 us
    all_gather x1, waiting for transfers between devices, local(): whole_a = lax.all_gather(down_tile, 'tp', axis=2, tiled=True)  11.4 us
    all_gather x1, blocking collectives, local(): shrink = lax.all_gather(shrink_local, 'tp', axis=0, tiled=True)  8.94 us
  transfers between devices with their start and end apart: 4, of which 4 were waited for; matrix products, arithmetic and copies ran while one was open for 5% of the time, Pallas kernels for 0%

commit v1 on v0

v1 whole, which is shorter than its diff:
```python
import functools

import jax
import jax.numpy as jnp
from jax import lax
from jax.experimental import pallas as pl
from jax.experimental.pallas import tpu as pltpu
from jax.sharding import PartitionSpec as P

BLOCK = 128
MIB = 1 << 20

adapter_scale = 0.5


def tile_of(columns, most):
    return max(t for t in range(128, most + 1, 128) if columns % t == 0)


def pick_kernel(index_ref, source_ref, out_ref):
    out_ref[...] = source_ref[...]


def pick(source, index):
    count, block = index.shape[0], (1,) + source.shape[1:]
    return pl.pallas_call(
        pick_kernel,
        grid_spec=pltpu.PrefetchScalarGridSpec(
            num_scalar_prefetch=1,
            grid=(count,),
            in_specs=[pl.BlockSpec(block, lambda i, index: (index[i], 0, 0))],
            out_specs=pl.BlockSpec(block, lambda i, index: (i, 0, 0)),
        ),
        out_shape=jax.ShapeDtypeStruct((count,) + source.shape[1:], source.dtype),
        cost_estimate=pl.CostEstimate(
            flops=0, bytes_accessed=2 * count * source[0].size * 2, transcendentals=0
        ),
        name="pick_panels",
    )(index, source)


class Piece:
    def __init__(self, array, at=None):
        self.array, self.at = array, at

    def value(self):
        return self.array if self.at is None else self.array[self.at]


def gather_refs(pieces):
    arrays = []
    places = []
    for piece in pieces:
        for number, array in enumerate(arrays):
            if array is piece.array:
                break
        else:
            number = len(arrays)
            arrays.append(piece.array)
        places.append((number, piece.at))
    return arrays, places


def read(refs, place):
    number, at = place
    return refs[number][...] if at is None else refs[number][at]


def whole_spec(array):
    zeros = (0,) * array.ndim
    return pl.BlockSpec(array.shape, lambda n, *_: zeros)


def project_kernel(places, slices, with_total, order_ref, owner_ref, *refs):
    refs = list(refs)
    arrays = refs[: places["arrays"]]
    weights = refs[places["arrays"] : places["arrays"] + slices]
    rest = refs[places["arrays"] + slices :]
    half = weights[0].shape[0] // 2
    rows = places["rows"]
    out_ref = rest[-1]
    for number, pairs in enumerate(rows):
        total = None
        for weight, (first, second) in zip(weights, pairs):
            part = jnp.dot(read(arrays, first), weight[:half], preferred_element_type=jnp.float32)
            part += jnp.dot(read(arrays, second), weight[half:], preferred_element_type=jnp.float32)
            total = part if total is None else total + part
        if with_total:
            total_ref, shrink_ref, *panels = rest[:-2]
            total += total_ref[...]
            for block, panel in enumerate(panels):
                update = jnp.dot(
                    shrink_ref[:, block * panel.shape[1] : (block + 1) * panel.shape[1]],
                    panel[0],
                    preferred_element_type=jnp.float32,
                )
                span = pl.ds(block * BLOCK, BLOCK)
                out_ref[span, :] = (
                    total[block * BLOCK : (block + 1) * BLOCK] + adapter_scale * update
                ).astype(out_ref.dtype)
        else:
            out_ref[number] = total


def project(rows, order, weight, tile, total=None, shrink=None, panels=None, owner=None, out=None, name=None):
    flat = [piece for pairs in rows for pair in pairs for piece in pair]
    arrays, places = gather_refs(flat)
    slices = len(rows[0])
    grid_places, position = [], 0
    for pairs in rows:
        grid_places.append([(places[position + 2 * i], places[position + 2 * i + 1]) for i in range(len(pairs))])
        position += 2 * len(pairs)
    row_count, half = arrays[0].shape[-2:]
    columns = weight.shape[1]
    width = 2 * half
    in_specs = [whole_spec(a) for a in arrays]
    operands = list(arrays)
    for i in range(slices):
        in_specs.append(pl.BlockSpec((width, tile), lambda n, order, owner, i=i: (order[i], n)))
        operands.append(weight)
    aliases = {}
    if total is None:
        owner = order
        out_shape = jax.ShapeDtypeStruct((len(rows), row_count, columns), jnp.float32)
        out_spec = pl.BlockSpec((len(rows), row_count, tile), lambda n, *_: (0, 0, n))
    else:
        in_specs += [pl.BlockSpec((None, row_count, tile), lambda n, *_: (0, 0, n)), whole_spec(shrink)]
        operands += [total, shrink]
        for block in range(row_count // BLOCK):
            in_specs.append(
                pl.BlockSpec(
                    (1, panels.shape[1], tile), lambda n, order, owner, b=block: (owner[b], 0, n)
                )
            )
            operands.append(panels)
        in_specs.append(pl.BlockSpec(memory_space=pl.ANY))
        operands.append(out)
        aliases = {2 + len(operands) - 1: 0}
        out_shape = jax.ShapeDtypeStruct(out.shape, out.dtype)
        out_spec = pl.BlockSpec((row_count, tile), lambda n, order, owner: (order[slices], n))
    flops = 2 * len(rows) * row_count * slices * width * columns
    moved = 2 * slices * width * columns + 2 * len(rows) * slices * row_count * width
    return pl.pallas_call(
        functools.partial(
            project_kernel,
            {"arrays": len(arrays), "rows": grid_places},
            slices,
            total is not None,
        ),
        grid_spec=pltpu.PrefetchScalarGridSpec(
            num_scalar_prefetch=2,
            grid=(columns // tile,),
            in_specs=in_specs,
            out_specs=out_spec,
        ),
        out_shape=out_shape,
        input_output_aliases=aliases,
        cost_estimate=pl.CostEstimate(
            flops=flops,
            bytes_accessed=moved + 4 * len(rows) * row_count * columns,
            transcendentals=0,
        ),
        compiler_params=pltpu.CompilerParams(vmem_limit_bytes=56 * MIB),
        name=name,
    )(order, owner, *operands)


def shrink_kernel(places, count, owner_ref, *refs):
    arrays, panels_ref, out_ref = refs[:count], refs[count], refs[count + 1]
    rank = panels_ref.shape[1]
    nt = (((1,), (1,)), ((), ()))
    for number, (first, second) in enumerate(places):
        one, two = read(arrays, first), read(arrays, second)
        half = one.shape[1]
        for block in range(one.shape[0] // BLOCK):
            panel = panels_ref[owner_ref[number * (one.shape[0] // BLOCK) + block]]
            span = slice(block * BLOCK, (block + 1) * BLOCK)
            out_ref[number, :, block * rank : (block + 1) * rank] = lax.dot_general(
                one[span], panel[:, :half], nt, preferred_element_type=jnp.float32
            ) + lax.dot_general(
                two[span], panel[:, half:], nt, preferred_element_type=jnp.float32
            )


def shrink_parts(pairs, panels, owner):
    arrays, places = gather_refs([piece for pair in pairs for piece in pair])
    places = [(places[2 * i], places[2 * i + 1]) for i in range(len(pairs))]
    row_count = arrays[0].shape[-2]
    rank = panels.shape[1]
    shape = (len(pairs), BLOCK, rank * (row_count // BLOCK))
    return pl.pallas_call(
        functools.partial(shrink_kernel, places, len(arrays)),
        grid_spec=pltpu.PrefetchScalarGridSpec(
            num_scalar_prefetch=1,
            grid=(1,),
            in_specs=[whole_spec(a) for a in arrays] + [whole_spec(panels)],
            out_specs=pl.BlockSpec(shape, lambda n, *_: (0, 0, 0)),
        ),
        out_shape=jax.ShapeDtypeStruct(shape, jnp.float32),
        cost_estimate=pl.CostEstimate(
            flops=8 * len(pairs) * row_count * panels.shape[2] * rank,
            bytes_accessed=2 * (len(pairs) * row_count * panels.shape[2] + panels.size),
            transcendentals=0,
        ),
        compiler_params=pltpu.CompilerParams(vmem_limit_bytes=56 * MIB),
        name="shrink_parts",
    )(owner, *arrays, panels)


def finish_kernel(order_ref, owner_ref, total_ref, shrink_ref, panel_ref, out_ref):
    rank = panel_ref.shape[1]
    blocks = shrink_ref.shape[2] // rank
    block = pl.program_id(0) % blocks
    shrink = shrink_ref[0, :, :rank]
    for other in range(1, blocks):
        shrink = jnp.where(block == other, shrink_ref[0, :, other * rank : (other + 1) * rank], shrink)
    update = jnp.dot(shrink, panel_ref[0], preferred_element_type=jnp.float32)
    out_ref[...] = (total_ref[0] + adapter_scale * update).astype(out_ref.dtype)


def finish(total, shrink, panels, place, owner, out, row_total):
    sets, row_count, columns = total.shape
    blocks = row_count // BLOCK
    rank = panels.shape[1]
    operands = [total, shrink, panels]
    return pl.pallas_call(
        finish_kernel,
        grid_spec=pltpu.PrefetchScalarGridSpec(
            num_scalar_prefetch=2,
            grid=(sets * blocks,),
            in_specs=[
                pl.BlockSpec((1, BLOCK, columns), lambda i, *_: (i // blocks, i % blocks, 0)),
                pl.BlockSpec((1, BLOCK, rank * blocks), lambda i, *_: (i // blocks, 0, 0)),
                pl.BlockSpec((1, rank, columns), lambda i, place, owner: (owner[i], 0, 0)),
            ],
            out_specs=pl.BlockSpec(
                (BLOCK, columns), lambda i, place, owner: (place[i // blocks] * blocks + i % blocks, 0)
            ),
        ),
        out_shape=jax.ShapeDtypeStruct((row_total, columns), jnp.bfloat16),
        cost_estimate=pl.CostEstimate(
            flops=8 * sets * row_count * rank * columns,
            bytes_accessed=6 * sets * row_count * columns,
            transcendentals=0,
        ),
        name="finish_rows",
    )(place, owner, *operands)


def square(tokens, frozen_weight, down_weight, up_weight, owners, select_slot):
    group = lax.axis_index("grp")
    member = lax.axis_index("tp")
    local_rows, width = tokens.shape
    blocks_own = local_rows // BLOCK
    blocks_here = 4 * blocks_own
    half = width // 8
    send = lambda x, m: lax.ppermute(x, "tp", [(i, i ^ m) for i in range(4)])
    exchange = lambda x: lax.all_to_all(x, "grp", split_axis=0, concat_axis=0, tiled=True)

    def cut(j, second):
        at = ((member ^ 3 ^ j) * 2 + second) * half
        return lax.dynamic_slice(tokens, (0, at), (local_rows, half))

    a = [cut(j, 0) for j in range(4)]
    b = [cut(j, 1) for j in range(4)]
    stack_a, stack_b = jnp.stack([a[0], a[2], a[3]]), jnp.stack([b[0], b[1], b[3]])

    xa, xb, ya, yb, da, db = {}, {}, {}, {}, {}, {}
    xa[0], yb[0] = Piece(send(a[0], 1)), Piece(send(b[0], 2))
    xa[2], yb[1] = Piece(send(a[2], 1)), Piece(send(b[1], 2))
    xb[2], ya[1] = Piece(send(b[2], 1)), Piece(send(a[1], 2))
    db[0], da[0] = Piece(send(yb[0].value(), 1)), Piece(send(xa[0].value(), 2))
    x_rest, y_rest = send(stack_b, 1), send(stack_a, 2)
    for place, j in enumerate((0, 1, 3)):
        xb[j] = Piece(x_rest, place)
    for place, j in enumerate((0, 2, 3)):
        ya[j] = Piece(y_rest, place)
    xa[1], yb[2] = Piece(send(a[1], 1)), Piece(send(b[2], 2))
    xa[3], yb[3] = Piece(send(a[3], 1)), Piece(send(b[3], 2))
    db[1], da[2] = Piece(send(yb[1].value(), 1)), Piece(send(xa[2].value(), 2))
    db[2], da[1] = Piece(send(yb[2].value(), 1)), Piece(send(xa[1].value(), 2))
    db[3], da[3] = Piece(send(yb[3].value(), 1)), Piece(send(xa[3].value(), 2))

    down_tile = exchange(pick(down_weight, select_slot))
    up_tile = exchange(pick(up_weight, select_slot))

    members = member ^ jnp.arange(4, dtype=jnp.int32)
    mine = lax.dynamic_slice_in_dim(owners, group * blocks_here, blocks_here).reshape(4, blocks_own)
    owner = jnp.take(mine, members, axis=0).reshape(-1)

    share = shrink_parts(
        [
            (Piece(a[3]), Piece(b[3])),
            (xa[2], xb[2]),
            (ya[1], yb[1]),
            (da[0], db[0]),
        ],
        down_tile,
        owner,
    )
    home = share[0] + send(share[1], 1) + send(share[2], 2) + send(share[3], 3)
    home = home.astype(jnp.bfloat16)
    shrink = [home] + [send(home, m) for m in (1, 2, 3)]

    slices = jnp.arange(4, dtype=jnp.int32)
    own = project(
        [[(Piece(a[j]), Piece(b[j])) for j in range(4)]],
        member ^ 3 ^ slices,
        frozen_weight,
        tile_of(frozen_weight.shape[1], 256),
        name="own_rows",
    )
    near = project(
        [[(xa[j], xb[j]) for j in range(4)], [(ya[j ^ 3], yb[j ^ 3]) for j in range(4)]],
        member ^ 2 ^ slices,
        frozen_weight,
        tile_of(frozen_weight.shape[1], 256),
        name="near_rows",
    )
    far = project(
        [[(da[j], db[j]) for j in range(3)]],
        member ^ slices,
        frozen_weight,
        tile_of(frozen_weight.shape[1], 256),
        name="far_rows",
    )
    totals = jnp.concatenate([own, near])
    out = finish(
        totals,
        jnp.stack(shrink[:3]),
        up_tile,
        members[:3],
        owner[: 3 * blocks_own],
        None,
        4 * local_rows,
    )
    return project(
        [[(da[3], db[3])]],
        jnp.stack([member ^ 3, member ^ 3]),
        frozen_weight,
        tile_of(frozen_weight.shape[1], 512),
        total=far,
        shrink=shrink[3],
        panels=up_tile,
        owner=owner[3 * blocks_own :],
        out=out,
        name="last_rows",
    )


def general(tokens, frozen_weight, down_weight, up_weight, owners, select_slot):
    tp_count = lax.axis_size("tp")
    group = lax.axis_index("grp")
    member = lax.axis_index("tp")
    local_rows, width = tokens.shape
    group_rows = local_rows * tp_count
    blocks_here = group_rows // BLOCK
    rank_columns = down_weight.shape[1]
    column_slice = up_weight.shape[2]
    my_owners = lax.dynamic_slice_in_dim(owners, group * blocks_here, blocks_here)
    arrived_a, arrived_b = (
        lax.all_to_all(
            jnp.take(panels, select_slot, axis=0), "grp", split_axis=0, concat_axis=0, tiled=True
        )
        for panels in (down_weight, up_weight)
    )
    down_tile = jnp.take(arrived_a, my_owners, axis=0)
    up_tile = jnp.take(arrived_b, my_owners, axis=0)
    whole_a = lax.all_gather(down_tile, "tp", axis=2, tiled=True)
    span_rows = min(local_rows, BLOCK)
    pieces_here = local_rows // span_rows
    first_block = member * local_rows // BLOCK
    local_a = lax.dynamic_slice_in_dim(whole_a, first_block, pieces_here, 0)
    shrink_local = jnp.einsum(
        "pnd,prd->pnr",
        tokens.reshape(pieces_here, span_rows, width),
        local_a,
        preferred_element_type=jnp.float32,
    )
    shrink_local = shrink_local.astype(jnp.bfloat16).reshape(local_rows, rank_columns)
    shrink = lax.all_gather(shrink_local, "tp", axis=0, tiled=True)
    frozen_rows = jnp.dot(
        lax.all_gather(tokens, "tp", axis=0, tiled=True),
        frozen_weight,
        preferred_element_type=jnp.float32,
    )
    update_rows = jnp.einsum(
        "bnr,brc->bnc",
        shrink.reshape(blocks_here, BLOCK, rank_columns),
        up_tile,
        preferred_element_type=jnp.float32,
    )
    update_rows = update_rows.reshape(group_rows, column_slice)
    return (frozen_rows + adapter_scale * update_rows).astype(jnp.bfloat16)


def local(tokens, frozen_weight, down_weight, up_weight, adapter_storage_slot, adapter_of_block):
    group_count = lax.axis_size("grp")
    group = lax.axis_index("grp")
    loaded_here = down_weight.shape[0]
    slot_numbers = jnp.take(adapter_storage_slot, adapter_of_block, axis=0)
    owners = slot_numbers // loaded_here
    offsets = slot_numbers % loaded_here
    owned_here = owners.reshape(group_count, -1) == group
    select_slot = jnp.sum(jnp.where(owned_here, offsets.reshape(group_count, -1), 0), axis=1)
    fits = lax.axis_size("tp") == 4 and tokens.shape[0] % BLOCK == 0
    way = square if fits else general
    return way(tokens, frozen_weight, down_weight, up_weight, owners, select_slot)


def solution(mesh):
    placed = (
        P(("grp", "tp"), None),
        P(None, "tp"),
        P("grp", None, "tp"),
        P("grp", None, "tp"),
        P(),
        P(),
    )
    return jax.shard_map(
        local, mesh=mesh, in_specs=placed, out_specs=P("grp", "tp"), check_vma=False
    )
```

time: 381 us -> 237 us (0.62)
  waiting for transfers between devices: 261 us -> 56.5 us
  Pallas kernels: 0 us -> 110 us
  matrix products: 64.7 us -> 0 us
  starting transfers between devices: 10.9 us -> 38.1 us
  between operations: 13.5 us -> 0.12 us
  blocking collectives: 8.94 us -> 0 us
  other arithmetic: 10.2 us -> 17.7 us
    all_gather x2 -> x0, waiting for transfers between devices: 151 us -> none  [the longest x1 140 us: local(): lax.all_gather(tokens, 'tp', axis=0, tiled=True)]
    pallas_call x0 -> x8, Pallas kernels: none -> 110 us  [the longest x4 82.8 us: project(): pl.pallas_call(functools.partial(project_kernel, {'arrays': len(arrays),...]
    all_to_all x2, waiting for transfers between devices: 109 us -> 1.53 us  [square(): lax.all_to_all(x, 'grp', split_axis=0, concat_axis=0, tiled=True)]
    dot_general x3 -> x0, matrix products: 64.7 us -> none  [the longest x1 53.9 us: local(): jnp.dot(lax.all_gather(tokens, 'tp', axis=0, tiled=True), frozen_weight,...]
    ppermute x0 -> x26, waiting for transfers between devices: none -> 55 us  [square(): send = lambda x, m: lax.ppermute(x, 'tp', [(i, i ^ m) for i in range(4)])]
    ppermute x0 -> x26, starting transfers between devices: none -> 28.6 us  [square(): send = lambda x, m: lax.ppermute(x, 'tp', [(i, i ^ m) for i in range(4)])]
    gather x4 -> x1, local copies, waits for them, and re-layouts: 10.1 us -> 0.56 us  [square(): owner = jnp.take(mine, members, axis=0).reshape(-1)]
    all_gather x1 -> x0, blocking collectives: 8.94 us -> none  [local(): shrink = lax.all_gather(shrink_local, 'tp', axis=0, tiled=True)]
  transfers between devices with their start and end apart: 4 -> 28, of which waited for: 4 -> 5; matrix products, arithmetic and copies ran while one was open for 5% -> 10% of each run, Pallas kernels for 0% -> 40%
where the time goes in v1:
time: 237 us; the launch traced here: 236 us
  Pallas kernels  110 us (46%)
  waiting for transfers between devices  56.5 us (24%)
  starting transfers between devices  38.1 us (16%)
  other arithmetic  17.7 us (7%)
  local copies, waits for them, and re-layouts  13.4 us (6%)
    pallas_call x4, Pallas kernels, project(): pl.pallas_call(functools.partial(project_kernel, {'arrays': len(arrays),...  82.8 us
    ppermute x26, waiting for transfers between devices, square(): send = lambda x, m: lax.ppermute(x, 'tp', [(i, i ^ m) for i in range(4)])  55 us
    ppermute x26, starting transfers between devices, square(): send = lambda x, m: lax.ppermute(x, 'tp', [(i, i ^ m) for i in range(4)])  28.6 us
    pallas_call x2, Pallas kernels, pick(): pl.pallas_call(pick_kernel, grid_spec=pltpu.PrefetchScalarGridSpec(num_sc...  12.9 us
    all_to_all x2, starting transfers between devices, square(): lax.all_to_all(x, 'grp', split_axis=0, concat_axis=0, tiled=True)  9.56 us
    pallas_call x1, Pallas kernels, finish(): pl.pallas_call(finish_kernel, grid_spec=pltpu.PrefetchScalarGridSpec(num_...  8.55 us
    concatenate x1, other arithmetic, square(): totals = jnp.concatenate([own, near])  6.65 us
    pallas_call x1, Pallas kernels, shrink_parts(): pl.pallas_call(functools.partial(shrink_kernel, places, len(arrays)), gri...  5.54 us
  transfers between devices with their start and end apart: 28, of which 5 were waited for; matrix products, arithmetic and copies ran while one was open for 10% of the time, Pallas kernels for 40%

profile of v1, /device:TPU:0, one launch (start us, length us, event | category | flops | bytes accessed | tf_op | source)
XLA Modules:
  0.0 235.7 jit_solution(2372318318480687668)
XLA Ops:
  0.0 0.7 compare_select_fusion.1
  0.7 0.8 gather_fusion
  1.5 0.7 and_select_fusion
  2.2 0.7 fusion.6.index_ref
  2.9 6.3 %pick_panels.2 = bf16[8,64,2048]{2,1,0:T(8,128)(2,1)} custom-call(s32[8]{0:T(128)} %fusion.6.index_ref, bf16[4,64,2048]{2,1,0:T(8,128)(2,1)} %source_ref.2), custom_call_target="tpu_custom_call" | custom-call | bytes 4194304 | tf_op jit(solution)/shard_map/pick_panels/pallas_call | solution.py:26
  9.2 5.9 %all-to-all-start = ((bf16[8,64,2048]{2,1,0:T(8,128)(2,1)}), bf16[8,64,2048]{2,1,0:T(8,128)(2,1)S(1)}, u32[]{:S(2)}, u32[]{:S(2)}) async-start(bf16[8,64,2048]{2,1,0:T(8,128)(2,1)} %pick_panels.2), calls=%async_computation | async-start | bytes 4194304 | tf_op jit(solution)/shard_map/all_to_all | solution.py:258
  15.1 4.0 %constant_dynamic-slice_fusion = (bf16[256,1024]{1,0:T(8,128)(2,1)}, bf16[256,1024]{1,0:T(8,128)(2,1)}, bf16[256,1024]{1,0:T(8,128)(2,1)}, bf16[256,1024]{1,0:T(...) fusion(bf16[256,8192]{1,0:T(8,128)(2,1)} %param.6, ...), kind=kLoop, calls=%fused_computation.30 | loop fusion | bytes 8388640 | tf_op jit(solution)/shard_map/dynamic_slice | solution.py:262
  19.1 1.5 collective-permute-start.4
  20.6 1.5 collective-permute-start.6
  23.2 1.5 collective-permute-start.16
  25.2 22.9 %own_rows.1 = f32[1,256,2560]{2,1,0:T(8,128)} custom-call(s32[4]{0:T(128)} %iota_xor_fusion.1.order_ref.owner_ref, s32[4]{0:T(128)} %iota_xor_fusion.1.order_ref.owner_ref, bf16[256,1024]{1,0:T(8,128)(2,1)} %copy-done.6, bf16[256,1024]{1,0:T(8,128)(2,1)} %get-tuple-element.10.refs_1_, bf16[256,1024]{1,0:T(8,128)(2,1)} %get-tuple-element.9.refs_2_, ...), custom_call_target="tpu_custom_call" | custom-call | flops 10737418240 | bytes 48758784 | tf_op jit(solution)/shard_map/own_rows/pallas_call | solution.py:143
  48.2 6.6 %pick_panels.3 = bf16[8,64,2560]{2,1,0:T(8,128)(2,1)} custom-call(s32[8]{0:T(128)} %fusion.6.index_ref, bf16[4,64,2560]{2,1,0:T(8,128)(2,1)} %source_ref.3), custom_call_target="tpu_custom_call" | custom-call | bytes 5242880 | tf_op jit(solution)/shard_map/pick_panels/pallas_call | solution.py:26
  55.4 1.6 collective-permute-start.14
  58.1 1.5 collective-permute-start.7
  60.1 2.5 %pad_maximum_fusion.1 = bf16[3,256,1024]{2,1,0:T(8,128)(2,1)} fusion(bf16[1,256,1024]{2,1,0:T(8,128)(2,1)S(1)} %bitcast.32, bf16[1,256,1024]{2,1,0:T(8,128)(2,1)} %bitcast.8, bf16[1,256,1024]{2,1,0:T(8,128)(2,1)} %bitcast.7), kind=kLoop, calls=%fused_computation.3 | loop fusion | flops 1572864 | bytes 3145728 | tf_op jit(solution)/shard_map/stack | solution.py:266
  62.7 1.5 all-to-all-done.refs_8_
  64.2 1.3 copy-done.5
  65.5 3.6 %all-to-all-start.1 = ((bf16[8,64,2560]{2,1,0:T(8,128)(2,1)}), bf16[8,64,2560]{2,1,0:T(8,128)(2,1)S(1)}, u32[]{:S(2)}, u32[]{:S(2)}) async-start(bf16[8,64,2560]{2,1,0:T(8,128)(2,1)} %pick_panels.3), calls=%async_computation.1 | async-start | bytes 5242880 | tf_op jit(solution)/shard_map/all_to_all | solution.py:258
  69.2 2.7 %pad_maximum_fusion.2 = bf16[3,256,1024]{2,1,0:T(8,128)(2,1)} fusion(bf16[1,256,1024]{2,1,0:T(8,128)(2,1)} %bitcast.33, bf16[1,256,1024]{2,1,0:T(8,128)(2,1)} %bitcast.11, bf16[1,256,1024]{2,1,0:T(8,128)(2,1)} %bitcast.34), kind=kLoop, calls=%fused_computation.4 | loop fusion | flops 1572864 | bytes 3145728 | tf_op jit(solution)/shard_map/stack | solution.py:266
  71.8 1.5 collective-permute-start.22
  73.3 1.5 collective-permute-start.23
  74.9 7.0 %collective-permute-done.5.refs_0_.refs_6_ = bf16[256,1024]{1,0:T(8,128)(2,1)} collective-permute-done((bf16[256,1024]{1,0:T(8,128)(2,1)}, bf16[256,1024]{1,0:T(8,128)(2,1)}, u32[]{:S(2)}, u32[]{:S(2)}) %collective-permute-start.5) | collective-permute-done | bytes 524320 | tf_op jit(solution)/shard_map/ppermute | solution.py:257
  81.9 1.6 collective-permute-start.13
  84.0 10.7 %collective-permute-done.11.refs_3_ = bf16[256,1024]{1,0:T(8,128)(2,1)} collective-permute-done((bf16[256,1024]{1,0:T(8,128)(2,1)}, bf16[256,1024]{1,0:T(8,128)(2,1)}, u32[]{:S(2)}, u32[]{:S(2)}) %collective-permute-start.11) | collective-permute-done | bytes 524320 | tf_op jit(solution)/shard_map/ppermute | solution.py:257
  96.3 0.7 slice.35.owner_ref
  97.5 0.7 pad_add_fusion.order_ref
  98.7 28.2 %collective-permute-done.13.refs_4_ = bf16[256,1024]{1,0:T(8,128)(2,1)} collective-permute-done((bf16[256,1024]{1,0:T(8,128)(2,1)}, bf16[256,1024]{1,0:T(8,128)(2,1)}, u32[]{:S(2)}, u32[]{:S(2)}) %collective-permute-start.13) | collective-permute-done | bytes 524320 | tf_op jit(solution)/shard_map/ppermute | solution.py:257
  126.8 1.6 collective-permute-start.17
  128.4 9.1 %collective-permute-done.15.refs_5_ = bf16[256,1024]{1,0:T(8,128)(2,1)} collective-permute-done((bf16[256,1024]{1,0:T(8,128)(2,1)}, bf16[256,1024]{1,0:T(8,128)(2,1)}, u32[]{:S(2)}, u32[]{:S(2)}) %collective-permute-start.15) | collective-permute-done | bytes 524320 | tf_op jit(solution)/shard_map/ppermute | solution.py:257
  138.1 1.5 collective-permute-start.2
  139.6 19.4 %far_rows.1.refs_3_ = f32[1,256,2560]{2,1,0:T(8,128)} custom-call(s32[4]{0:T(128)} %iota_xor_fusion.2.order_ref.owner_ref, s32[4]{0:T(128)} %iota_xor_fusion.2.order_ref.owner_ref, bf16[256,1024]{1,0:T(8,128)(2,1)} %collective-permute-done.5.refs_0_.refs_6_, bf16[256,1024]{1,0:T(8,128)(2,1)} %collective-permute-done.7.refs_1_.refs_7_, ...), custom_call_target="tpu_custom_call" | custom-call | flops 8053063680 | bytes 37224448 | tf_op jit(solution)/shard_map/far_rows/pallas_call | solution.py:143
  159.5 1.5 collective-permute-start.3
  161.0 0.8 copy-done.7
  161.8 5.5 %shrink_parts.1 = f32[4,128,128]{2,1,0:T(8,128)} custom-call(s32[8]{0:T(128)} %select_n.104.owner_ref, bf16[256,1024]{1,0:T(8,128)(2,1)} %get-tuple-element.13.refs_0_.refs_6_, bf16[256,1024]{1,0:T(8,128)(2,1)} %get-tuple-element.12.refs_1_.refs_7_, bf16[256,1024]{1,0:T(8,128)(2,1)} %collective-permute-done.12.refs_2_.refs_3_, ...), custom_call_target="tpu_custom_call" | custom-call | flops 1073741824 | bytes 6291456 | tf_op jit(solution)/shard_map/shrink_parts/pallas_call | solution.py:191
  167.3 0.9 slice_bitcast_fusion.2
  168.8 1.6 collective-permute-start.19
  170.4 1.3 collective-permute-start.20
  171.8 30.6 %near_rows.1 = f32[2,256,2560]{2,1,0:T(8,128)} custom-call(s32[4]{0:T(128)} %iota_xor_fusion.order_ref.owner_ref, s32[4]{0:T(128)} %iota_xor_fusion.order_ref.owner_ref, bf16[256,1024]{1,0:T(8,128)(2,1)} %collective-permute-done.4.refs_0_, bf16[3,256,1024]{2,1,0:T(8,128)(2,1)} %collective-permute-done.22.refs_1_, ...), custom_call_target="tpu_custom_call" | custom-call | flops 21474836480 | bytes 55574528 | tf_op jit(solution)/shard_map/near_rows/pallas_call | solution.py:143
  202.4 0.9 fusion.3
  203.8 1.8 collective-permute-start.25
  205.6 6.7 %pad_maximum_fusion.total_ref = f32[3,256,2560]{2,1,0:T(8,128)} fusion(f32[2,256,2560]{2,1,0:T(8,128)} %near_rows.1, f32[1,256,2560]{2,1,0:T(8,128)S(1)} %copy-done.3), kind=kLoop, calls=%fused_computation.2 | loop fusion | flops 1966080 | bytes 15728640 | tf_op jit(solution)/shard_map/concatenate | solution.py:327
  212.2 1.3 collective-permute-start.21
  213.5 0.7 pad_maximum_fusion.3.shrink_ref
  214.2 1.6 copy-done.2
  215.7 8.5 %finish_rows.1.refs_7_ = bf16[1024,2560]{1,0:T(8,128)(2,1)} custom-call(s32[3]{0:T(128)} %bitcast.39, s32[6]{0:T(128)} %slice.35.owner_ref, f32[3,256,2560]{2,1,0:T(8,128)} %pad_maximum_fusion.total_ref, bf16[3,128,128]{2,1,0:T(8,128)(2,1)} %pad_maximum_fusion.3.shrink_ref, bf16[8,64,2560]{2,1,0:T(8,128)(2,1)} %copy-done.2), custom_call_target="tpu_custom_call" | custom-call | flops 1006632960 | bytes 11796480 | tf_op jit(solution)/shard_map/finish_rows/pallas_call | solution.py:226
  224.3 0.8 copy-done.8
  225.1 0.6 copy-done.9
  225.7 10.0 %last_rows.1 = bf16[1024,2560]{1,0:T(8,128)(2,1)} custom-call(s32[2]{0:T(128)} %pad_add_fusion.order_ref, s32[2]{0:T(128)} %slice_bitcast_fusion.4.owner_ref, bf16[256,1024]{1,0:T(8,128)(2,1)} %collective-permute-done.1.refs_0_, bf16[256,1024]{1,0:T(8,128)(2,1)} %copy-done.8, bf16[8192,2560]{1,0:T(8,128)(2,1)} %refs_2_.1, ...), custom_call_target="tpu_custom_call", output_to_operand_aliasing={{}: (9, {})} | custom-call | flops 2684354560 | bytes 14155776 | tf_op jit(solution)/shard_map/last_rows/pallas_call | solution.py:143
  (63 shorter events, 9.5 us)
Async XLA Ops:
  0.0 0.7 copy-start
  9.2 55.0 %all-to-all-start = ((bf16[8,64,2048]{2,1,0:T(8,128)(2,1)}), bf16[8,64,2048]{2,1,0:T(8,128)(2,1)S(1)}, u32[]{:S(2)}, u32[]{:S(2)}) async-start(bf16[8,64,2048]{2,1,0:T(8,128)(2,1)} %pick_panels.2), calls=%async_computation | async-start | bytes 4194304 | tf_op jit(solution)/shard_map/all_to_all | solution.py:258
  19.1 6.0 %copy-start.6 = (bf16[256,1024]{1,0:T(8,128)(2,1)}, bf16[256,1024]{1,0:T(8,128)(2,1)S(1)}, u32[]{:S(2)}) copy-start(bf16[256,1024]{1,0:T(8,128)(2,1)S(1)} %get-tuple-element.11.refs_0_) | copy-start | bytes 1572868
  19.1 36.3 %collective-permute-start.4 = (bf16[256,1024]{1,0:T(8,128)(2,1)S(1)}, bf16[256,1024]{1,0:T(8,128)(2,1)}, u32[]{:S(2)}, u32[]{:S(2)}) collective-permute-start(bf16[256,1024]{1,0:T(8,128)(2,1)S(1)} %get-tuple-element.11.refs_0_), channel_id=1, source_target_pairs={{0,1},{1,0},{2,3},{3,2},{4,5},{5,4},{6,7},{7,6},{8,9},{9,8},{10,11... | collective-permute-start | bytes 1572872 | tf_op jit(solution)/shard_map/ppermute | solution.py:257
  20.6 36.4 %collective-permute-start.6 = (bf16[256,1024]{1,0:T(8,128)(2,1)}, bf16[256,1024]{1,0:T(8,128)(2,1)}, u32[]{:S(2)}, u32[]{:S(2)}) collective-permute-start(bf16[256,1024]{1,0:T(8,128)(2,1)} %get-tuple-element.10.refs_1_), channel_id=1, source_target_pairs={{0,2},{1,3},{2,0},{3,1},{4,6},{5,7},{6,4},{7,5},{8,10},{9,11},{10,... | collective-permute-start | bytes 1572872 | tf_op jit(solution)/shard_map/ppermute | solution.py:257
  22.2 35.4 %collective-permute-start.10 = (bf16[256,1024]{1,0:T(8,128)(2,1)}, bf16[256,1024]{1,0:T(8,128)(2,1)}, u32[]{:S(2)}, u32[]{:S(2)}) collective-permute-start(bf16[256,1024]{1,0:T(8,128)(2,1)} %get-tuple-element.8.refs_3_), channel_id=1, source_target_pairs={{0,2},{1,3},{2,0},{3,1},{4,6},{5,7},{6,4},{7,5},{8,10},{9,11},{10,... | collective-permute-start | bytes 1572872 | tf_op jit(solution)/shard_map/ppermute | solution.py:257
  22.7 35.4 %collective-permute-start.12 = (bf16[256,1024]{1,0:T(8,128)(2,1)}, bf16[256,1024]{1,0:T(8,128)(2,1)}, u32[]{:S(2)}, u32[]{:S(2)}) collective-permute-start(bf16[256,1024]{1,0:T(8,128)(2,1)} %get-tuple-element.14.refs_4_), channel_id=1, source_target_pairs={{0,1},{1,0},{2,3},{3,2},{4,5},{5,4},{6,7},{7,6},{8,9},{9,8},{10,11... | collective-permute-start | bytes 1572872 | tf_op jit(solution)/shard_map/ppermute | solution.py:257
  23.2 36.3 %collective-permute-start.16 = (bf16[256,1024]{1,0:T(8,128)(2,1)}, bf16[256,1024]{1,0:T(8,128)(2,1)}, u32[]{:S(2)}, u32[]{:S(2)}) collective-permute-start(bf16[256,1024]{1,0:T(8,128)(2,1)} %get-tuple-element.7.refs_5_), channel_id=1, source_target_pairs={{0,1},{1,0},{2,3},{3,2},{4,5},{5,4},{6,7},{7,6},{8,9},{9,8},{10,11... | collective-permute-start | bytes 1572872 | tf_op jit(solution)/shard_map/ppermute | solution.py:257
  48.1 12.0 %copy-start.4 = (bf16[256,1024]{1,0:T(8,128)(2,1)S(1)}, bf16[256,1024]{1,0:T(8,128)(2,1)}, u32[]{:S(2)}) copy-start(bf16[256,1024]{1,0:T(8,128)(2,1)} %get-tuple-element.12.refs_1_.refs_7_) | copy-start | bytes 1572868
  55.4 16.4 %collective-permute-start.14 = (bf16[256,1024]{1,0:T(8,128)(2,1)}, bf16[256,1024]{1,0:T(8,128)(2,1)}, u32[]{:S(2)}, u32[]{:S(2)}) collective-permute-start(bf16[256,1024]{1,0:T(8,128)(2,1)} %get-tuple-element.7.refs_5_), channel_id=1, source_target_pairs={{0,2},{1,3},{2,0},{3,1},{4,6},{5,7},{6,4},{7,5},{8,10},{9,11},{10,... | collective-permute-start | bytes 1572872 | tf_op jit(solution)/shard_map/ppermute | solution.py:257
  57.0 16.3 %collective-permute-start.8 = (bf16[256,1024]{1,0:T(8,128)(2,1)}, bf16[256,1024]{1,0:T(8,128)(2,1)}, u32[]{:S(2)}, u32[]{:S(2)}) collective-permute-start(bf16[256,1024]{1,0:T(8,128)(2,1)} %get-tuple-element.9.refs_2_), channel_id=1, source_target_pairs={{0,1},{1,0},{2,3},{3,2},{4,5},{5,4},{6,7},{7,6},{8,9},{9,8},{10,11... | collective-permute-start | bytes 1572872 | tf_op jit(solution)/shard_map/ppermute | solution.py:257
  57.6 24.3 %collective-permute-start.5 = (bf16[256,1024]{1,0:T(8,128)(2,1)}, bf16[256,1024]{1,0:T(8,128)(2,1)}, u32[]{:S(2)}, u32[]{:S(2)}) collective-permute-start(bf16[256,1024]{1,0:T(8,128)(2,1)} %collective-permute-done.4.refs_0_), channel_id=1, source_target_pairs={{0,2},{1,3},{2,0},{3,1},{4,6},{5,7},{6,4},{7,5},{8,10},{9,11},{10,... | collective-permute-start | bytes 1572872 | tf_op jit(solution)/shard_map/ppermute | solution.py:257
  58.1 25.4 %collective-permute-start.7 = (bf16[256,1024]{1,0:T(8,128)(2,1)}, bf16[256,1024]{1,0:T(8,128)(2,1)}, u32[]{:S(2)}, u32[]{:S(2)}) collective-permute-start(bf16[256,1024]{1,0:T(8,128)(2,1)} %collective-permute-done.6.refs_11_), channel_id=1, source_target_pairs={{0,1},{1,0},{2,3},{3,2},{4,5},{5,4},{6,7},{7,6},{8,9},{9,8},{10,11... | collective-permute-start | bytes 1572872 | tf_op jit(solution)/shard_map/ppermute | solution.py:257
  59.5 35.1 %collective-permute-start.11 = (bf16[256,1024]{1,0:T(8,128)(2,1)}, bf16[256,1024]{1,0:T(8,128)(2,1)}, u32[]{:S(2)}, u32[]{:S(2)}) collective-permute-start(bf16[256,1024]{1,0:T(8,128)(2,1)} %collective-permute-done.10.refs_5_.refs_10_), channel_id=1, source_target_pairs={{0,1},{1,0},{2,3},{3,2},{4,5},{5,4},{6,7},{7,6},{8,9},{9,8},{10,11... | collective-permute-start | bytes 1572872 | tf_op jit(solution)/shard_map/ppermute | solution.py:257
  64.2 1.3 copy-start.5
  65.5 148.6 %all-to-all-start.1 = ((bf16[8,64,2560]{2,1,0:T(8,128)(2,1)}), bf16[8,64,2560]{2,1,0:T(8,128)(2,1)S(1)}, u32[]{:S(2)}, u32[]{:S(2)}) async-start(bf16[8,64,2560]{2,1,0:T(8,128)(2,1)} %pick_panels.3), calls=%async_computation.1 | async-start | bytes 5242880 | tf_op jit(solution)/shard_map/all_to_all | solution.py:258
  71.8 97.0 %collective-permute-start.22 = (bf16[3,256,1024]{2,1,0:T(8,128)(2,1)}, bf16[3,256,1024]{2,1,0:T(8,128)(2,1)}, u32[]{:S(2)}, u32[]{:S(2)}) collective-permute-start(bf16[3,256,1024]{2,1,0:T(8,128)(2,1)} %pad_maximum_fusion.1), channel_id=1, source_target_pairs={{0,1},{1,0},{2,3},{3,2},{4,5},{5,4},{6,7},{7,6},{8,9},{9,8},{10,11... | collective-permute-start | bytes 4718600 | tf_op jit(solution)/shard_map/ppermute | solution.py:257
  73.3 97.1 %collective-permute-start.23 = (bf16[3,256,1024]{2,1,0:T(8,128)(2,1)}, bf16[3,256,1024]{2,1,0:T(8,128)(2,1)}, u32[]{:S(2)}, u32[]{:S(2)}) collective-permute-start(bf16[3,256,1024]{2,1,0:T(8,128)(2,1)} %pad_maximum_fusion.2), channel_id=1, source_target_pairs={{0,2},{1,3},{2,0},{3,1},{4,6},{5,7},{6,4},{7,5},{8,10},{9,11},{10,... | collective-permute-start | bytes 4718600 | tf_op jit(solution)/shard_map/ppermute | solution.py:257
  81.9 44.9 %collective-permute-start.13 = (bf16[256,1024]{1,0:T(8,128)(2,1)}, bf16[256,1024]{1,0:T(8,128)(2,1)}, u32[]{:S(2)}, u32[]{:S(2)}) collective-permute-start(bf16[256,1024]{1,0:T(8,128)(2,1)} %collective-permute-done.12.refs_2_.refs_3_), channel_id=1, source_target_pairs={{0,2},{1,3},{2,0},{3,1},{4,6},{5,7},{6,4},{7,5},{8,10},{9,11},{10,... | collective-permute-start | bytes 1572872 | tf_op jit(solution)/shard_map/ppermute | solution.py:257
  83.4 54.1 %collective-permute-start.15 = (bf16[256,1024]{1,0:T(8,128)(2,1)}, bf16[256,1024]{1,0:T(8,128)(2,1)}, u32[]{:S(2)}, u32[]{:S(2)}) collective-permute-start(bf16[256,1024]{1,0:T(8,128)(2,1)} %collective-permute-done.14.refs_8_), channel_id=1, source_target_pairs={{0,1},{1,0},{2,3},{3,2},{4,5},{5,4},{6,7},{7,6},{8,9},{9,8},{10,11... | collective-permute-start | bytes 1572872 | tf_op jit(solution)/shard_map/ppermute | solution.py:257
  94.7 43.4 %collective-permute-start.9 = (bf16[256,1024]{1,0:T(8,128)(2,1)}, bf16[256,1024]{1,0:T(8,128)(2,1)}, u32[]{:S(2)}, u32[]{:S(2)}) collective-permute-start(bf16[256,1024]{1,0:T(8,128)(2,1)} %collective-permute-done.8.refs_2_), channel_id=1, source_target_pairs={{0,2},{1,3},{2,0},{3,1},{4,6},{5,7},{6,4},{7,5},{8,10},{9,11},{10,... | collective-permute-start | bytes 1572872 | tf_op jit(solution)/shard_map/ppermute | solution.py:257
  126.8 34.1 %collective-permute-start.17 = (bf16[256,1024]{1,0:T(8,128)(2,1)}, bf16[256,1024]{1,0:T(8,128)(2,1)S(1)}, u32[]{:S(2)}, u32[]{:S(2)}) collective-permute-start(bf16[256,1024]{1,0:T(8,128)(2,1)} %get-tuple-element.9.refs_2_), channel_id=1, source_target_pairs={{0,2},{1,3},{2,0},{3,1},{4,6},{5,7},{6,4},{7,5},{8,10},{9,11},{10,... | collective-permute-start | bytes 1572872 | tf_op jit(solution)/shard_map/ppermute | solution.py:257
  137.5 21.5 %collective-permute-start = (bf16[256,1024]{1,0:T(8,128)(2,1)}, bf16[256,1024]{1,0:T(8,128)(2,1)}, u32[]{:S(2)}, u32[]{:S(2)}) collective-permute-start(bf16[256,1024]{1,0:T(8,128)(2,1)} %get-tuple-element.13.refs_0_.refs_6_), channel_id=1, source_target_pairs={{0,1},{1,0},{2,3},{3,2},{4,5},{5,4},{6,7},{7,6},{8,9},{9,8},{10,11... | collective-permute-start | bytes 1572872 | tf_op jit(solution)/shard_map/ppermute | solution.py:257
  138.1 21.4 %collective-permute-start.2 = (bf16[256,1024]{1,0:T(8,128)(2,1)S(1)}, bf16[256,1024]{1,0:T(8,128)(2,1)}, u32[]{:S(2)}, u32[]{:S(2)}) collective-permute-start(bf16[256,1024]{1,0:T(8,128)(2,1)S(1)} %copy-done.4), channel_id=1, source_target_pairs={{0,2},{1,3},{2,0},{3,1},{4,6},{5,7},{6,4},{7,5},{8,10},{9,11},{10,... | collective-permute-start | bytes 1572872 | tf_op jit(solution)/shard_map/ppermute | solution.py:257
  159.0 65.3 %collective-permute-start.1 = (bf16[256,1024]{1,0:T(8,128)(2,1)}, bf16[256,1024]{1,0:T(8,128)(2,1)}, u32[]{:S(2)}, u32[]{:S(2)}) collective-permute-start(bf16[256,1024]{1,0:T(8,128)(2,1)} %collective-permute-done.refs_5_), channel_id=1, source_target_pairs={{0,2},{1,3},{2,0},{3,1},{4,6},{5,7},{6,4},{7,5},{8,10},{9,11},{10,... | collective-permute-start | bytes 1572872 | tf_op jit(solution)/shard_map/ppermute | solution.py:257
  159.5 64.8 %collective-permute-start.3 = (bf16[256,1024]{1,0:T(8,128)(2,1)}, bf16[256,1024]{1,0:T(8,128)(2,1)S(1)}, u32[]{:S(2)}, u32[]{:S(2)}) collective-permute-start(bf16[256,1024]{1,0:T(8,128)(2,1)} %collective-permute-done.2.refs_7_), channel_id=1, source_target_pairs={{0,1},{1,0},{2,3},{3,2},{4,5},{5,4},{6,7},{7,6},{8,9},{9,8},{10,11... | collective-permute-start | bytes 1572872 | tf_op jit(solution)/shard_map/ppermute | solution.py:257
  161.0 0.8 copy-start.7
  168.2 34.2 %collective-permute-start.18 = (f32[128,128]{1,0:T(8,128)S(1)}, f32[128,128]{1,0:T(8,128)S(1)}, u32[]{:S(2)}, u32[]{:S(2)}) collective-permute-start(f32[128,128]{1,0:T(8,128)S(1)} %get-tuple-element.15), channel_id=1, source_target_pairs={{0,1},{1,0},{2,3},{3,2},{4,5},{5,4},{6,7},{7,6},{8,9},{9,8},{10,11... | collective-permute-start | bytes 196616 | tf_op jit(solution)/shard_map/ppermute | solution.py:257
  168.8 33.6 %collective-permute-start.19 = (f32[128,128]{1,0:T(8,128)S(1)}, f32[128,128]{1,0:T(8,128)S(1)}, u32[]{:S(2)}, u32[]{:S(2)}) collective-permute-start(f32[128,128]{1,0:T(8,128)S(1)} %get-tuple-element.17), channel_id=1, source_target_pairs={{0,2},{1,3},{2,0},{3,1},{4,6},{5,7},{6,4},{7,5},{8,10},{9,11},{10,... | collective-permute-start | bytes 196616 | tf_op jit(solution)/shard_map/ppermute | solution.py:257
  170.4 35.1 %copy-start.3 = (f32[1,256,2560]{2,1,0:T(8,128)S(1)}, f32[1,256,2560]{2,1,0:T(8,128)}, u32[]{:S(2)}) copy-start(f32[1,256,2560]{2,1,0:T(8,128)} %own_rows.1) | copy-start | bytes 7864324
  170.4 32.0 %collective-permute-start.20 = (f32[128,128]{1,0:T(8,128)S(1)}, f32[128,128]{1,0:T(8,128)S(1)}, u32[]{:S(2)}, u32[]{:S(2)}) collective-permute-start(f32[128,128]{1,0:T(8,128)S(1)} %get-tuple-element.16), channel_id=1, source_target_pairs={{0,3},{1,2},{2,1},{3,0},{4,7},{5,6},{6,5},{7,4},{8,11},{9,10},{10,... | collective-permute-start | bytes 196616 | tf_op jit(solution)/shard_map/ppermute | solution.py:257
  203.3 10.2 %collective-permute-start.24 = (bf16[128,128]{1,0:T(8,128)(2,1)S(1)}, bf16[128,128]{1,0:T(8,128)(2,1)S(1)}, u32[]{:S(2)}, u32[]{:S(2)}) collective-permute-start(bf16[128,128]{1,0:T(8,128)(2,1)S(1)} %fusion.3), channel_id=1, source_target_pairs={{0,1},{1,0},{2,3},{3,2},{4,5},{5,4},{6,7},{7,6},{8,9},{9,8},{10,11... | collective-permute-start | bytes 98312 | tf_op jit(solution)/shard_map/ppermute | solution.py:257
  203.8 9.7 %collective-permute-start.25 = (bf16[128,128]{1,0:T(8,128)(2,1)S(1)}, bf16[128,128]{1,0:T(8,128)(2,1)S(1)}, u32[]{:S(2)}, u32[]{:S(2)}) collective-permute-start(bf16[128,128]{1,0:T(8,128)(2,1)S(1)} %fusion.3), channel_id=1, source_target_pairs={{0,2},{1,3},{2,0},{3,1},{4,6},{5,7},{6,4},{7,5},{8,10},{9,11},{10,... | collective-permute-start | bytes 98312 | tf_op jit(solution)/shard_map/ppermute | solution.py:257
  212.2 12.1 %collective-permute-start.21 = (bf16[128,128]{1,0:T(8,128)(2,1)S(1)}, bf16[128,128]{1,0:T(8,128)(2,1)S(1)}, u32[]{:S(2)}, u32[]{:S(2)}) collective-permute-start(bf16[128,128]{1,0:T(8,128)(2,1)S(1)} %fusion.3), channel_id=1, source_target_pairs={{0,3},{1,2},{2,1},{3,0},{4,7},{5,6},{6,5},{7,4},{8,11},{9,10},{10,... | collective-permute-start | bytes 98312 | tf_op jit(solution)/shard_map/ppermute | solution.py:257
  214.2 1.6 copy-start.2
  224.3 0.8 copy-start.8
  225.1 0.6 copy-start.9
  225.7 10.0 %copy-start.1 = (s32[32]{0:T(128)S(1)}, s32[32]{0:T(128)}, u32[]{:S(2)}) copy-start(s32[32]{0:T(128)} %param.10) | copy-start | bytes 388

commit v2 on v0

v2 whole, which is shorter than its diff:
```python
import functools

import jax
import jax.numpy as jnp
from jax import lax
from jax.experimental import pallas as pl
from jax.experimental.pallas import tpu as pltpu
from jax.sharding import PartitionSpec as P

BLOCK = 128
MIB = 1 << 20
PANELS_AT = 4

adapter_scale = 0.5


def tile_of(columns, most):
    return max(t for t in range(128, most + 1, 128) if columns % t == 0)


def whole_spec(array):
    zeros = (0,) * array.ndim
    return pl.BlockSpec(array.shape, lambda *_: zeros)


def cost(flops, moved):
    return pl.CostEstimate(flops=flops, bytes_accessed=moved, transcendentals=0)


class Arrays:
    def __init__(self):
        self.arrays = []

    def place(self, array):
        for number, known in enumerate(self.arrays):
            if known is array:
                return number
        self.arrays.append(array)
        return len(self.arrays) - 1


def view(ref, at):
    if at is None:
        return ref[...]
    return ref[:, at[0] : at[1]] if isinstance(at, tuple) else ref[at]


def cut_kernel(slices_ref, tokens_ref, out_ref):
    out_ref[0] = tokens_ref[...]


def cut_stack(tokens, slices, parts):
    rows, width = tokens.shape
    count, part, band = slices.shape[0], width // parts, rows * parts // 8
    return pl.pallas_call(
        cut_kernel,
        grid_spec=pltpu.PrefetchScalarGridSpec(
            num_scalar_prefetch=1,
            grid=(count, rows // band),
            in_specs=[pl.BlockSpec((band, part), lambda i, r, slices: (r, slices[i]))],
            out_specs=pl.BlockSpec((1, band, part), lambda i, r, slices: (i, r, 0)),
        ),
        out_shape=jax.ShapeDtypeStruct((count, rows, part), tokens.dtype),
        cost_estimate=cost(0, 4 * count * rows * part),
        name="cut_stack",
    )(slices, tokens)


def project_kernel(sets, weights_at, totals_at, update, plan_ref, *refs):
    out_ref = refs[-1]
    for number, terms in enumerate(sets):
        total = None
        for array, at, weight in terms:
            part = jnp.dot(
                view(refs[array], at), refs[weights_at + weight][...], preferred_element_type=jnp.float32
            )
            total = part if total is None else total + part
        if totals_at:
            before = refs[totals_at[number]][...]
            total = before if total is None else total + before
        if update is None:
            out_ref[number] = total
        else:
            first_set, shrinks_at, panels_at = update
            shrink = 0
            for at in shrinks_at:
                shrink += refs[at][plan_ref[first_set + number]].astype(jnp.float32)
            shrink = shrink.astype(jnp.bfloat16)
            for block, panel in enumerate(panels_at):
                rank = refs[panel].shape[0]
                term = jnp.dot(
                    shrink[:, block * rank : (block + 1) * rank],
                    refs[panel][...],
                    preferred_element_type=jnp.float32,
                )
                span = slice(block * BLOCK, (block + 1) * BLOCK)
                out_ref[span, :] = (total[span] + adapter_scale * term).astype(out_ref.dtype)


def project(sets, weight, tile, plan, rows, total=None, update=None, into=None, weigh=2, name=None):
    columns = weight.shape[1]
    known, halves, flat = Arrays(), [], []
    for terms in sets:
        flat.append([])
        for array, at, k, half in terms:
            if (k, half) not in halves:
                halves.append((k, half))
            flat[-1].append((known.place(array), at, halves.index((k, half))))
    depth = weight.shape[0] // 4
    operands = list(known.arrays)
    in_specs = [whole_spec(a) for a in operands]
    weights_at = len(operands)
    for k, half in halves:
        if k is None:
            in_specs.append(pl.BlockSpec((depth, tile), lambda n, plan, half=half: (half, n)))
        elif half is None:
            in_specs.append(pl.BlockSpec((depth, tile), lambda n, plan, k=k: (plan[k], n)))
        else:
            in_specs.append(
                pl.BlockSpec((depth // 2, tile), lambda n, plan, k=k, half=half: (plan[k] * 2 + half, n))
            )
        operands.append(weight)
    totals_at = []
    if total is not None:
        for number in range(len(sets)):
            in_specs.append(pl.BlockSpec((None, rows, tile), lambda n, plan, number=number: (number, 0, n)))
            operands.append(total)
            totals_at.append(len(operands) - 1)
    updating, aliases = None, {}
    if update is None:
        out_shape = jax.ShapeDtypeStruct((len(sets), rows, columns), jnp.float32)
        out_spec = pl.BlockSpec((len(sets), rows, tile), lambda n, plan: (0, 0, n))
    else:
        first_set, shrinks, panels = update
        shrinks_at, panels_at = [], []
        for shrink in shrinks:
            in_specs.append(whole_spec(shrink))
            operands.append(shrink)
            shrinks_at.append(len(operands) - 1)
        for block in range(rows // BLOCK):
            index = PANELS_AT + first_set * (rows // BLOCK) + block
            in_specs.append(
                pl.BlockSpec((None, panels.shape[1], tile), lambda n, plan, index=index: (plan[index], 0, n))
            )
            operands.append(panels)
            panels_at.append(len(operands) - 1)
        updating = (first_set, shrinks_at, panels_at)
        out_shape = jax.ShapeDtypeStruct(into.shape, into.dtype)
        out_spec = pl.BlockSpec((rows, tile), lambda n, plan: (plan[first_set], n))
        in_specs.append(pl.BlockSpec(memory_space=pl.ANY))
        operands.append(into)
        aliases = {len(operands): 0}
    products = sum(2 if half is None or k is None else 1 for terms in sets for _, _, k, half in terms)
    products *= rows * depth // 2
    moved = 2 * products // rows * columns + 4 * len(sets) * rows * columns * (1 if total is None else 2)
    return pl.pallas_call(
        functools.partial(project_kernel, flat, weights_at, totals_at, updating),
        grid_spec=pltpu.PrefetchScalarGridSpec(
            num_scalar_prefetch=1,
            grid=(columns // tile,),
            in_specs=in_specs,
            out_specs=out_spec,
        ),
        out_shape=out_shape,
        input_output_aliases=aliases,
        cost_estimate=cost(weigh * 2 * products * columns, weigh * moved),
        compiler_params=pltpu.CompilerParams(vmem_limit_bytes=56 * MIB),
        name=name,
    )(plan, *operands)


def finish_kernel(count, plan_ref, *refs):
    own_ref, near_ref, panel_one, panel_two, out_ref = refs[0], refs[1], refs[-3], refs[-2], refs[-1]
    number = pl.program_id(0)
    shrink = 0
    for ref in refs[2:-3]:
        shrink += ref[plan_ref[number]].astype(jnp.float32)
    shrink = shrink.astype(jnp.bfloat16)
    rank = panel_one.shape[0]
    for block, panel in enumerate((panel_one, panel_two)):
        term = adapter_scale * jnp.dot(
            shrink[:, block * rank : (block + 1) * rank], panel[...], preferred_element_type=jnp.float32
        )
        span = slice(block * BLOCK, (block + 1) * BLOCK)

        @pl.when(number == 0)
        def _():
            out_ref[span, :] = (own_ref[span] + term).astype(out_ref.dtype)

        @pl.when(number != 0)
        def _():
            out_ref[span, :] = (near_ref[span] + term).astype(out_ref.dtype)


def finish(own, near, shrinks, panels, plan, row_total):
    _, rows, columns = near.shape
    rank = panels.shape[1]
    tile = tile_of(columns, 2560)
    return pl.pallas_call(
        functools.partial(finish_kernel, 3),
        grid_spec=pltpu.PrefetchScalarGridSpec(
            num_scalar_prefetch=1,
            grid=(3, columns // tile),
            in_specs=[
                pl.BlockSpec((None, rows, tile), lambda s, n, plan: (0, 0, jnp.where(s == 0, n, columns // tile - 1))),
                pl.BlockSpec((None, rows, tile), lambda s, n, plan: (jnp.maximum(s - 1, 0), 0, n)),
            ]
            + [whole_spec(shrink) for shrink in shrinks]
            + [
                pl.BlockSpec(
                    (None, rank, tile), lambda s, n, plan, block=block: (plan[PANELS_AT + 2 * s + block], 0, n)
                )
                for block in range(2)
            ],
            out_specs=pl.BlockSpec((rows, tile), lambda s, n, plan: (plan[s], n)),
        ),
        out_shape=jax.ShapeDtypeStruct((row_total, columns), jnp.bfloat16),
        cost_estimate=cost(12 * rows * rank * columns, 18 * rows * columns),
        compiler_params=pltpu.CompilerParams(vmem_limit_bytes=56 * MIB),
        name="finish_rows",
    )(plan, own, near, *shrinks, panels, panels)


def shrink_kernel(sets, panels_at, plan_ref, *refs):
    panels_ref, out_ref = refs[panels_at], refs[-1]
    rank = panels_ref.shape[1]
    nt = (((1,), (1,)), ((), ()))
    for number, terms in enumerate(sets):
        blocks = refs[terms[0][0]].shape[-2] // BLOCK
        for block in range(blocks):
            panel = plan_ref[PANELS_AT + number * blocks + block]
            total = 0
            for array, at, start in terms:
                tokens = view(refs[array], at)[block * BLOCK : (block + 1) * BLOCK]
                total += lax.dot_general(
                    tokens,
                    panels_ref[panel, :, start : start + tokens.shape[1]],
                    nt,
                    preferred_element_type=jnp.float32,
                )
            out_ref[plan_ref[number], :, block * rank : (block + 1) * rank] = total.astype(
                out_ref.dtype
            )


def shrink_parts(tokens, sets, panels, plan):
    rows, width = tokens.shape
    known = Arrays()
    flat = [[(known.place(tokens), None, 0)]]
    flat += [[(known.place(array), at, start) for array, at, start in terms] for terms in sets]
    operands = known.arrays + [panels]
    _, rank, depth = panels.shape
    shape = (len(flat), BLOCK, rank * (rows // BLOCK))
    in_specs = [whole_spec(a) for a in operands]
    in_specs[0] = pl.BlockSpec((rows, depth), lambda i, plan: (0, plan[0]))
    return pl.pallas_call(
        functools.partial(shrink_kernel, flat, len(known.arrays)),
        grid_spec=pltpu.PrefetchScalarGridSpec(
            num_scalar_prefetch=1,
            grid=(1,),
            in_specs=in_specs,
            out_specs=pl.BlockSpec(shape, lambda *_: (0, 0, 0)),
        ),
        out_shape=jax.ShapeDtypeStruct(shape, tokens.dtype),
        cost_estimate=cost(8 * len(flat) * rows * depth * rank, 2 * (panels.size + len(flat) * rows * depth)),
        compiler_params=pltpu.CompilerParams(vmem_limit_bytes=56 * MIB),
        name="shrink_parts",
    )(plan, *operands)


def after(value, *others):
    return lax.optimization_barrier((value,) + others)[0]


def square(tokens, frozen_weight, down_weight, up_weight, owners, select_slot):
    group = lax.axis_index("grp")
    member = lax.axis_index("tp")
    rows, width = tokens.shape
    blocks = rows // BLOCK
    depth, half = width // 4, width // 8
    to_x = lambda v: lax.ppermute(v, "tp", [(i, i ^ 1) for i in range(4)])
    to_y = lambda v: lax.ppermute(v, "tp", [(i, i ^ 2) for i in range(4)])
    across = lambda v: lax.ppermute(v, "tp", [(i, i ^ 3) for i in range(4)])
    first, second = (0, half), (half, depth)

    members = member ^ jnp.arange(4, dtype=jnp.int32)
    mine = lax.dynamic_slice_in_dim(owners, group * 4 * blocks, 4 * blocks).reshape(4, blocks)
    mine = jnp.sum(jnp.where((members[:, None] == jnp.arange(4))[:, :, None], mine[None], 0), axis=1)
    plan = jnp.concatenate([members, mine.reshape(-1)]).astype(jnp.int32)

    def cut(j, second):
        return lax.dynamic_slice(tokens, (0, (member ^ 3 ^ j) * depth + second * half), (rows, half))

    def eighths(*places):
        numbers = jnp.stack([(member ^ 3 ^ j) * 2 + second for j, second in places])
        return cut_stack(tokens, numbers.astype(jnp.int32), 8)

    a0, b0 = cut(0, 0), cut(0, 1)
    xa0, yb0 = to_x(a0), to_y(b0)
    early_x, early_y = eighths((0, 1), (3, 0), (3, 1)), eighths((0, 0), (3, 0), (3, 1))
    x_early, y_early = to_x(early_x), to_y(early_y)
    late = cut_stack(tokens, jnp.stack([member ^ 2, member ^ 1]).astype(jnp.int32), 4)
    x12, y12 = to_x(late), to_y(late)

    def chosen(panels, select):
        return jnp.take(panels, select, axis=0, mode="clip")

    def exchange(panels):
        return lax.all_to_all(panels, "grp", split_axis=0, concat_axis=0, tiled=True)

    down_out = chosen(down_weight, after(select_slot, xa0, yb0, early_x, early_y))
    down = exchange(down_out)

    own = project(
        [[(tokens, (i * depth, (i + 1) * depth), None, i) for i in range(4)]],
        frozen_weight, tile_of(frozen_weight.shape[1], 512), after(plan, down_out, late), rows, weigh=0, name="own_rows",
    )

    tile = tile_of(frozen_weight.shape[1], 512)
    near = project(
        [
            [(xa0, None, 2, 0), (x_early, 0, 2, 1), (x_early, 1, 1, 0), (x_early, 2, 1, 1)],
            [(y_early, 1, 2, 0), (y_early, 2, 2, 1), (y_early, 0, 1, 0), (yb0, None, 1, 1)],
        ],
        frozen_weight, tile, after(plan, own), rows, weigh=0, name="near_rows",
    )
    up = exchange(chosen(up_weight, after(select_slot, down, near)))

    da0, db0 = to_y(after(xa0, x_early, y_early)), to_x(after(yb0, x_early, y_early))
    da3, db3 = to_y(after(x_early[1], near)), to_x(after(y_early[2], near))
    near = project(
        [[(x12, 0, 3, None), (x12, 1, 0, None)], [(y12, 1, 3, None), (y12, 0, 0, None)]],
        frozen_weight, tile, plan, rows, total=near, name="near_rows_rest",
    )

    share = shrink_parts(
        tokens,
        [[(x12, 1, 0)], [(y12, 0, 0)], [(da0, None, 0), (db0, None, half)]],
        down,
        after(plan, near),
    )
    shrinks = [share, to_x(share), to_y(share), across(share)]
    da12 = to_y(after(x12[:, :, :half], share))
    db12 = to_x(after(y12[:, :, half:], share))

    far = project(
        [[(da0, None, 0, 0), (db0, None, 0, 1), (da3, None, 3, 0), (db3, None, 3, 1)]],
        frozen_weight, tile_of(frozen_weight.shape[1], 640), after(plan, share), rows, name="far_rows",
    )
    out = finish(own, near, shrinks, up, after(plan, far), 4 * rows)
    return project(
        [[(da12, 0, 1, 0), (db12, 0, 1, 1), (da12, 1, 2, 0), (db12, 1, 2, 1)]],
        frozen_weight, tile_of(frozen_weight.shape[1], 640), plan, rows,
        total=far, update=(3, shrinks, up), into=out, name="last_rows",
    )


def general(tokens, frozen_weight, down_weight, up_weight, owners, select_slot):
    tp_count = lax.axis_size("tp")
    group = lax.axis_index("grp")
    member = lax.axis_index("tp")
    local_rows, width = tokens.shape
    group_rows = local_rows * tp_count
    blocks_here = group_rows // BLOCK
    rank_columns = down_weight.shape[1]
    column_slice = up_weight.shape[2]
    my_owners = lax.dynamic_slice_in_dim(owners, group * blocks_here, blocks_here)
    arrived_a, arrived_b = (
        lax.all_to_all(
            jnp.take(panels, select_slot, axis=0), "grp", split_axis=0, concat_axis=0, tiled=True
        )
        for panels in (down_weight, up_weight)
    )
    down_tile = jnp.take(arrived_a, my_owners, axis=0)
    up_tile = jnp.take(arrived_b, my_owners, axis=0)
    whole_a = lax.all_gather(down_tile, "tp", axis=2, tiled=True)
    span_rows = min(local_rows, BLOCK)
    pieces_here = local_rows // span_rows
    first_block = member * local_rows // BLOCK
    local_a = lax.dynamic_slice_in_dim(whole_a, first_block, pieces_here, 0)
    shrink_local = jnp.einsum(
        "pnd,prd->pnr",
        tokens.reshape(pieces_here, span_rows, width),
        local_a,
        preferred_element_type=jnp.float32,
    )
    shrink_local = shrink_local.astype(jnp.bfloat16).reshape(local_rows, rank_columns)
    shrink = lax.all_gather(shrink_local, "tp", axis=0, tiled=True)
    frozen_rows = jnp.dot(
        lax.all_gather(tokens, "tp", axis=0, tiled=True),
        frozen_weight,
        preferred_element_type=jnp.float32,
    )
    update_rows = jnp.einsum(
        "bnr,brc->bnc",
        shrink.reshape(blocks_here, BLOCK, rank_columns),
        up_tile,
        preferred_element_type=jnp.float32,
    )
    update_rows = update_rows.reshape(group_rows, column_slice)
    return (frozen_rows + adapter_scale * update_rows).astype(jnp.bfloat16)


def local(tokens, frozen_weight, down_weight, up_weight, adapter_storage_slot, adapter_of_block):
    group_count = lax.axis_size("grp")
    group = lax.axis_index("grp")
    loaded_here = down_weight.shape[0]
    adapters = jnp.arange(adapter_storage_slot.shape[0])
    named = adapter_of_block[:, None] == adapters[None, :]
    slot_numbers = jnp.sum(jnp.where(named, adapter_storage_slot[None, :], 0), axis=1)
    owners = slot_numbers // loaded_here
    offsets = slot_numbers % loaded_here
    owned_here = owners.reshape(group_count, -1) == group
    select_slot = jnp.sum(jnp.where(owned_here, offsets.reshape(group_count, -1), 0), axis=1)
    fits = lax.axis_size("tp") == 4 and tokens.shape[0] % BLOCK == 0
    way = square if fits else general
    return way(tokens, frozen_weight, down_weight, up_weight, owners, select_slot)


def solution(mesh):
    placed = (
        P(("grp", "tp"), None),
        P(None, "tp"),
        P("grp", None, "tp"),
        P("grp", None, "tp"),
        P(),
        P(),
    )
    return jax.shard_map(
        local, mesh=mesh, in_specs=placed, out_specs=P("grp", "tp"), check_vma=False
    )
```

time: 381 us -> 187 us (0.49)
  waiting for transfers between devices: 261 us -> 23 us
  Pallas kernels: 0 us -> 115 us
  matrix products: 64.7 us -> 0 us
  starting transfers between devices: 10.9 us -> 28.6 us
  between operations: 13.5 us -> 0.29 us
  blocking collectives: 8.94 us -> 0 us
  other arithmetic: 10.2 us -> 3.05 us
  local copies, waits for them, and re-layouts: 11.6 us -> 16.7 us
    all_gather x2 -> x0, waiting for transfers between devices: 151 us -> none  [the longest x1 140 us: local(): lax.all_gather(tokens, 'tp', axis=0, tiled=True)]
    pallas_call x0 -> x10, Pallas kernels: none -> 115 us  [the longest x5 86.8 us: project(): pl.pallas_call(functools.partial(project_kernel, flat, weights_at, totals...]
    all_to_all x2, waiting for transfers between devices: 109 us -> 0.01 us  [exchange(): lax.all_to_all(panels, 'grp', split_axis=0, concat_axis=0, tiled=True)]
    dot_general x3 -> x0, matrix products: 64.7 us -> none  [the longest x1 53.9 us: local(): jnp.dot(lax.all_gather(tokens, 'tp', axis=0, tiled=True), frozen_weight,...]
    ppermute x0 -> x15, waiting for transfers between devices: none -> 23 us  [the longest x7 20.2 us: square(): to_x = lambda v: lax.ppermute(v, 'tp', [(i, i ^ 1) for i in range(4)])]
    ppermute x0 -> x15, starting transfers between devices: none -> 18.5 us  [the longest x7 8.75 us: square(): to_y = lambda v: lax.ppermute(v, 'tp', [(i, i ^ 2) for i in range(4)])]
    select_n x5 -> x0, other arithmetic: 9.21 us -> none  [the longest x1 3.58 us: local(): jnp.where(available[:, None, None], jnp.take(up_weight, select_slot, axis...]
    all_gather x1 -> x0, blocking collectives: 8.94 us -> none  [local(): shrink = lax.all_gather(shrink_local, 'tp', axis=0, tiled=True)]
  transfers between devices with their start and end apart: 4 -> 17, of which waited for: 4 -> 8; matrix products, arithmetic and copies ran while one was open for 5% -> 6% of each run, Pallas kernels for 0% -> 54%
where the time goes in v2:
time: 187 us; the launch traced here: 186 us
  Pallas kernels  115 us (61%)
  starting transfers between devices  28.6 us (15%)
  waiting for transfers between devices  23 us (12%)
  local copies, waits for them, and re-layouts  16.7 us (9%)
  other arithmetic  3.05 us (2%)
    pallas_call x5, Pallas kernels, project(): pl.pallas_call(functools.partial(project_kernel, flat, weights_at, totals...  86.8 us
    ppermute x7, waiting for transfers between devices, square(): to_x = lambda v: lax.ppermute(v, 'tp', [(i, i ^ 1) for i in range(4)])  20.2 us
    pallas_call x3, Pallas kernels, cut_stack(): pl.pallas_call(cut_kernel, grid_spec=pltpu.PrefetchScalarGridSpec(num_sca...  12.7 us
    all_to_all x2, starting transfers between devices, exchange(): lax.all_to_all(panels, 'grp', split_axis=0, concat_axis=0, tiled=True)  10 us
    pallas_call x1, Pallas kernels, finish(): pl.pallas_call(functools.partial(finish_kernel, 3), grid_spec=pltpu.Prefe...  9.22 us
    ppermute x7, starting transfers between devices, square(): to_y = lambda v: lax.ppermute(v, 'tp', [(i, i ^ 2) for i in range(4)])  8.75 us
    ppermute x7, starting transfers between devices, square(): to_x = lambda v: lax.ppermute(v, 'tp', [(i, i ^ 1) for i in range(4)])  8.65 us
    pallas_call x1, Pallas kernels, shrink_parts(): pl.pallas_call(functools.partial(shrink_kernel, flat, len(known.arrays)),...  6.1 us
  transfers between devices with their start and end apart: 17, of which 8 were waited for; matrix products, arithmetic and copies ran while one was open for 6% of the time, Pallas kernels for 54%

profile of v2, /device:TPU:0, one launch (start us, length us, event | category | flops | bytes accessed | tf_op | source)
XLA Modules:
  0.0 186.5 jit_solution(5426379633496499489)
XLA Ops:
  0.0 2.2 %constant_dynamic-slice_fusion = (bf16[256,1024]{1,0:T(8,128)(2,1)S(1)}, bf16[256,1024]{1,0:T(8,128)(2,1)}) fusion(bf16[256,8192]{1,0:T(8,128)(2,1)} %refs_0_.3, s32[]{:T(128)S(6)} %select_n.45, s32[]{:T(128)S(6)} %select_n.44), kind=kLoop, calls=%fused_computation.29 | loop fusion | bytes 2097160 | tf_op jit(solution)/shard_map/dynamic_slice | solution.py:292
  2.2 2.9 %collective-permute-start.2 = (bf16[256,1024]{1,0:T(8,128)(2,1)}, bf16[256,1024]{1,0:T(8,128)(2,1)}, u32[]{:S(2)}, u32[]{:S(2)}) collective-permute-start(bf16[256,1024]{1,0:T(8,128)(2,1)} %get-tuple-element.32), channel_id=1, source_target_pairs={{0,1},{1,0},{2,3},{3,2},{4,5},{5,4},{6,7},{7,6},{8,9},{9,8},{10,11... | collective-permute-start | bytes 1572872 | tf_op jit(solution)/shard_map/ppermute | solution.py:281
  5.1 1.5 collective-permute-start.3
  6.6 0.7 add_add_fusion.slices_ref
  7.3 4.0 %cut_stack.4 = bf16[3,256,1024]{2,1,0:T(8,128)(2,1)} custom-call(s32[3]{0:T(128)} %add_add_fusion.slices_ref, bf16[256,8192]{1,0:T(8,128)(2,1)} %refs_0_.3), custom_call_target="tpu_custom_call" | custom-call | bytes 3145728 | tf_op jit(solution)/shard_map/cut_stack/pallas_call | solution.py:55
  11.4 0.7 add_add_fusion.1.slices_ref
  12.0 4.2 %cut_stack.5 = bf16[3,256,1024]{2,1,0:T(8,128)(2,1)} custom-call(s32[3]{0:T(128)} %add_add_fusion.1.slices_ref, bf16[256,8192]{1,0:T(8,128)(2,1)} %refs_0_.3), custom_call_target="tpu_custom_call" | custom-call | bytes 3145728 | tf_op jit(solution)/shard_map/cut_stack/pallas_call | solution.py:55
  16.5 0.8 collective-permute-done.2.refs_0_
  17.4 1.1 collective-permute-done.3.refs_3_
  18.5 2.0 %gather_fusion = bf16[8,64,2048]{2,1,0:T(8,128)(2,1)} fusion(bf16[4,64,2048]{2,1,0:T(8,128)(2,1)S(1)} %copy-done.4, s32[1024]{0:T(1024)S(1)} %pad_clamp_fusion.1), kind=kCustom, calls=%fused_computation | custom fusion | bytes 4194336 | tf_op jit(solution)/shard_map/jit(_take)/gather | solution.py:306
  20.6 4.9 %all-to-all-start = ((bf16[8,64,2048]{2,1,0:T(8,128)(2,1)}), bf16[8,64,2048]{2,1,0:T(8,128)(2,1)}, u32[]{:S(2)}, u32[]{:S(2)}) async-start(bf16[8,64,2048]{2,1,0:T(8,128)(2,1)} %gather_fusion), calls=%async_computation | async-start | bytes 4194304 | tf_op jit(solution)/shard_map/all_to_all | solution.py:309
  25.4 0.6 collective-permute-start.4
  26.0 1.5 collective-permute-start.5
  27.6 0.7 pad_add_fusion.1.slices_ref
  28.2 4.5 %cut_stack.3 = bf16[2,256,2048]{2,1,0:T(8,128)(2,1)} custom-call(s32[2]{0:T(128)} %pad_add_fusion.1.slices_ref, bf16[256,8192]{1,0:T(8,128)(2,1)} %refs_0_.3), custom_call_target="tpu_custom_call" | custom-call | bytes 4194304 | tf_op jit(solution)/shard_map/cut_stack/pallas_call | solution.py:55
  32.7 1.4 collective-permute-start
  35.3 0.6 pad_add_fusion.plan_ref
  35.9 22.2 %own_rows.1.refs_0_ = f32[1,256,2560]{2,1,0:T(8,128)} custom-call(s32[12]{0:T(128)} %pad_add_fusion.plan_ref, bf16[256,8192]{1,0:T(8,128)(2,1)} %refs_0_.3, bf16[8192,2560]{1,0:T(8,128)(2,1)} %refs_5_.5, bf16[8192,2560]{1,0:T(8,128)(2,1)} %refs_5_.5, bf16[8192,2560]{1,0:T(8,128)(2,1)} %refs_5_.5, bf16[8192,2560]{1,0:T(8,128)(2,1)} %refs_5_.5), custom_call_target="tpu_custom_call" | custom-call | tf_op jit(solution)/shard_map/own_rows/pallas_call | solution.py:156
  58.1 4.8 %collective-permute-done.4.refs_1_ = bf16[3,256,1024]{2,1,0:T(8,128)(2,1)} collective-permute-done((bf16[3,256,1024]{2,1,0:T(8,128)(2,1)}, bf16[3,256,1024]{2,1,0:T(8,128)(2,1)}, u32[]{:S(2)}, u32[]{:S(2)}) %collective-permute-start.4) | collective-permute-done | bytes 1572896 | tf_op jit(solution)/shard_map/ppermute | solution.py:281
  62.9 0.6 collective-permute-done.5.refs_2_
  63.6 17.5 %near_rows.1.refs_4_.refs_5_ = f32[2,256,2560]{2,1,0:T(8,128)} custom-call(s32[12]{0:T(128)} %pad_add_fusion.plan_ref, bf16[256,1024]{1,0:T(8,128)(2,1)} %collective-permute-done.2.refs_0_, bf16[3,256,1024]{2,1,0:T(8,128)(2,1)} %collective-permute-done.4.refs_1_, bf16[3,256,1024]{2,1,0:T(8,128)(2,1)} %collective-permute-done.5.refs_2_, ...), custom_call_target="tpu_custom_call" | custom-call | tf_op jit(solution)/shard_map/near_rows/pallas_call | solution.py:156
  81.2 2.3 %gather_fusion.1 = bf16[8,64,2560]{2,1,0:T(8,128)(2,1)} fusion(bf16[4,64,2560]{2,1,0:T(8,128)(2,1)S(1)} %copy-done, s32[1024]{0:T(1024)S(1)} %pad_clamp_fusion), kind=kCustom, calls=%fused_computation.1 | custom fusion | bytes 5242912 | tf_op jit(solution)/shard_map/jit(_take)/gather | solution.py:306
  83.5 5.1 %all-to-all-start.1 = ((bf16[8,64,2560]{2,1,0:T(8,128)(2,1)}), bf16[8,64,2560]{2,1,0:T(8,128)(2,1)}, u32[]{:S(2)}, u32[]{:S(2)}) async-start(bf16[8,64,2560]{2,1,0:T(8,128)(2,1)} %gather_fusion.1), calls=%async_computation.1 | async-start | bytes 5242880 | tf_op jit(solution)/shard_map/all_to_all | solution.py:309
  88.6 1.5 collective-permute-start.6
  90.1 1.4 collective-permute-start.7
  91.6 1.1 slice_bitcast_fusion.1
  92.6 0.6 collective-permute-start.10
  93.3 1.1 slice_bitcast_fusion
  94.4 13.4 %collective-permute-done.refs_0_.refs_1_ = bf16[2,256,2048]{2,1,0:T(8,128)(2,1)S(1)} collective-permute-done((bf16[2,256,2048]{2,1,0:T(8,128)(2,1)}, bf16[2,256,2048]{2,1,0:T(8,128)(2,1)S(1)}, u32[]{:S(2)}, u32[]{:S(2)}) %collective-permute-start) | collective-permute-done | bytes 2097184 | tf_op jit(solution)/shard_map/ppermute | solution.py:281
  108.5 0.6 copy-done.2
  109.1 18.9 %near_rows_rest.1.refs_1_ = f32[2,256,2560]{2,1,0:T(8,128)} custom-call(s32[12]{0:T(128)} %pad_add_fusion.plan_ref, bf16[2,256,2048]{2,1,0:T(8,128)(2,1)} %copy-done.2, bf16[2,256,2048]{2,1,0:T(8,128)(2,1)} %collective-permute-done.1.refs_1_.refs_2_, bf16[8192,2560]{1,0:T(8,128)(2,1)} %refs_5_.5, bf16[8192,2560]{1,0:T(8,128)(2,1)} %refs_5_.5, ...), custom_call_target="tpu_custom_call" | custom-call | flops 21474836480 | bytes 104857600 | tf_op jit(solution)/shard_map/near_rows_rest/pallas_call | solution.py:156
  128.1 2.4 %slice.21 = bf16[2,256,1024]{2,1,0:T(8,128)(2,1)} slice(bf16[2,256,2048]{2,1,0:T(8,128)(2,1)} %collective-permute-done.1.refs_1_.refs_2_), slice={[0:2], [0:256], [1024:2048]} | slice | bytes 2097152 | tf_op jit(solution)/shard_map/slice | solution.py:344
  130.5 1.1 slice.20
  131.6 0.8 copy-done.5
  132.4 0.8 copy-done.6
  133.2 6.1 %shrink_parts.1.refs_2_.refs_7_ = bf16[4,128,128]{2,1,0:T(8,128)(2,1)} custom-call(s32[12]{0:T(128)} %pad_add_fusion.plan_ref, bf16[256,8192]{1,0:T(8,128)(2,1)} %refs_0_.3, bf16[2,256,2048]{2,1,0:T(8,128)(2,1)} %copy-done.2, bf16[2,256,2048]{2,1,0:T(8,128)(2,1)} %collective-permute-done.1.refs_1_.refs_2_, bf16[256,1024]{1,0:T(8,128)(2,1)} %copy-done.5, ...), custom_call_target="tpu_custom_call" | custom-call | flops 1073741824 | bytes 6291456 | tf_op jit(solution)/shard_map/shrink_parts/pallas_call | solution.py:256
  139.3 0.8 collective-permute-start.12
  140.1 1.5 collective-permute-start.13
  141.6 1.1 collective-permute-start.14
  142.7 0.8 collective-permute-start.9
  143.6 1.5 collective-permute-start.8
  145.1 13.5 %far_rows.1.refs_6_ = f32[1,256,2560]{2,1,0:T(8,128)} custom-call(s32[12]{0:T(128)} %pad_add_fusion.plan_ref, bf16[256,1024]{1,0:T(8,128)(2,1)} %copy-done.5, bf16[256,1024]{1,0:T(8,128)(2,1)} %copy-done.6, bf16[256,1024]{1,0:T(8,128)(2,1)} %copy-done.10, bf16[256,1024]{1,0:T(8,128)(2,1)} %copy-done.11, bf16[8192,2560]{1,0:T(8,128)(2,1)} %refs_5_.5, ...), custom_call_target="tpu_custom_call" | custom-call | flops 10737418240 | bytes 47185920 | tf_op jit(solution)/shard_map/far_rows/pallas_call | solution.py:156
  158.7 0.6 copy-done.12
  159.4 9.2 %finish_rows.1.refs_13_ = bf16[1024,2560]{1,0:T(8,128)(2,1)} custom-call(s32[12]{0:T(128)} %pad_add_fusion.plan_ref, f32[1,256,2560]{2,1,0:T(8,128)} %own_rows.1.refs_0_, f32[2,256,2560]{2,1,0:T(8,128)} %near_rows_rest.1.refs_1_, bf16[4,128,128]{2,1,0:T(8,128)(2,1)} %shrink_parts.1.refs_2_.refs_7_, bf16[4,128,128]{2,1,0:T(8,128)(2,1)} %copy-done.12, ...), custom_call_target="tpu_custom_call" | custom-call | flops 503316480 | bytes 11796480 | tf_op jit(solution)/shard_map/finish_rows/pallas_call | solution.py:199
  168.6 1.1 collective-permute-done.9.refs_1_
  169.7 0.8 collective-permute-done.8.refs_0_
  170.7 1.0 copy-done.8
  171.7 14.6 %last_rows.1 = bf16[1024,2560]{1,0:T(8,128)(2,1)} custom-call(s32[12]{0:T(128)} %pad_add_fusion.plan_ref, bf16[2,256,1024]{2,1,0:T(8,128)(2,1)} %copy-done.8, bf16[2,256,1024]{2,1,0:T(8,128)(2,1)} %copy-done.7, bf16[8192,2560]{1,0:T(8,128)(2,1)} %refs_5_.5, bf16[8192,2560]{1,0:T(8,128)(2,1)} %refs_5_.5, ...), custom_call_target="tpu_custom_call", output_to_operand_aliasing={{}: (14, {})} | custom-call | flops 10737418240 | bytes 52428800 | tf_op jit(solution)/shard_map/last_rows/pallas_call | solution.py:156
  (55 shorter events, 2.5 us)
Async XLA Ops:
  0.0 81.2 %copy-start = (bf16[4,64,2560]{2,1,0:T(8,128)(2,1)S(1)}, bf16[4,64,2560]{2,1,0:T(8,128)(2,1)}, u32[]{:S(2)}) copy-start(bf16[4,64,2560]{2,1,0:T(8,128)(2,1)} %param.9) | copy-start | bytes 3932164
  2.2 15.2 %collective-permute-start.2 = (bf16[256,1024]{1,0:T(8,128)(2,1)}, bf16[256,1024]{1,0:T(8,128)(2,1)}, u32[]{:S(2)}, u32[]{:S(2)}) collective-permute-start(bf16[256,1024]{1,0:T(8,128)(2,1)} %get-tuple-element.32), channel_id=1, source_target_pairs={{0,1},{1,0},{2,3},{3,2},{4,5},{5,4},{6,7},{7,6},{8,9},{9,8},{10,11... | collective-permute-start | bytes 1572872 | tf_op jit(solution)/shard_map/ppermute | solution.py:281
  5.1 13.4 %collective-permute-start.3 = (bf16[256,1024]{1,0:T(8,128)(2,1)S(1)}, bf16[256,1024]{1,0:T(8,128)(2,1)S(1)}, u32[]{:S(2)}, u32[]{:S(2)}) collective-permute-start(bf16[256,1024]{1,0:T(8,128)(2,1)S(1)} %get-tuple-element.31), channel_id=1, source_target_pairs={{0,2},{1,3},{2,0},{3,1},{4,6},{5,7},{6,4},{7,5},{8,10},{9,11},{10,... | collective-permute-start | bytes 1572872 | tf_op jit(solution)/shard_map/ppermute | solution.py:282
  12.0 4.2 %copy-start.15 = (s32[32]{0:T(128)S(1)}, s32[32]{0:T(128)}, u32[]{:S(2)}) copy-start(s32[32]{0:T(128)} %param.10) | copy-start | bytes 388
  12.0 4.2 %copy-start.16 = (s32[64]{0:T(128)S(1)}, s32[64]{0:T(128)}, u32[]{:S(2)}) copy-start(s32[64]{0:T(128)} %param.11) | copy-start | bytes 772
  12.0 6.5 %copy-start.4 = (bf16[4,64,2048]{2,1,0:T(8,128)(2,1)S(1)}, bf16[4,64,2048]{2,1,0:T(8,128)(2,1)}, u32[]{:S(2)}) copy-start(bf16[4,64,2048]{2,1,0:T(8,128)(2,1)} %param.8) | copy-start | bytes 3145732
  18.5 2.1 %copy-start.9 = (bf16[256,1024]{1,0:T(8,128)(2,1)}, bf16[256,1024]{1,0:T(8,128)(2,1)S(1)}, u32[]{:S(2)}) copy-start(bf16[256,1024]{1,0:T(8,128)(2,1)S(1)} %collective-permute-done.3.refs_3_) | copy-start | bytes 1572868
  20.6 60.6 %all-to-all-start = ((bf16[8,64,2048]{2,1,0:T(8,128)(2,1)}), bf16[8,64,2048]{2,1,0:T(8,128)(2,1)}, u32[]{:S(2)}, u32[]{:S(2)}) async-start(bf16[8,64,2048]{2,1,0:T(8,128)(2,1)} %gather_fusion), calls=%async_computation | async-start | bytes 4194304 | tf_op jit(solution)/shard_map/all_to_all | solution.py:309
  25.4 37.5 %collective-permute-start.4 = (bf16[3,256,1024]{2,1,0:T(8,128)(2,1)}, bf16[3,256,1024]{2,1,0:T(8,128)(2,1)}, u32[]{:S(2)}, u32[]{:S(2)}) collective-permute-start(bf16[3,256,1024]{2,1,0:T(8,128)(2,1)} %cut_stack.4), channel_id=1, source_target_pairs={{0,1},{1,0},{2,3},{3,2},{4,5},{5,4},{6,7},{7,6},{8,9},{9,8},{10,11... | collective-permute-start | bytes 4718600 | tf_op jit(solution)/shard_map/ppermute | solution.py:281
  26.0 37.5 %collective-permute-start.5 = (bf16[3,256,1024]{2,1,0:T(8,128)(2,1)}, bf16[3,256,1024]{2,1,0:T(8,128)(2,1)}, u32[]{:S(2)}, u32[]{:S(2)}) collective-permute-start(bf16[3,256,1024]{2,1,0:T(8,128)(2,1)} %cut_stack.5), channel_id=1, source_target_pairs={{0,2},{1,3},{2,0},{3,1},{4,6},{5,7},{6,4},{7,5},{8,10},{9,11},{10,... | collective-permute-start | bytes 4718600 | tf_op jit(solution)/shard_map/ppermute | solution.py:282
  32.7 75.1 %collective-permute-start = (bf16[2,256,2048]{2,1,0:T(8,128)(2,1)}, bf16[2,256,2048]{2,1,0:T(8,128)(2,1)S(1)}, u32[]{:S(2)}, u32[]{:S(2)}) collective-permute-start(bf16[2,256,2048]{2,1,0:T(8,128)(2,1)} %cut_stack.3), channel_id=1, source_target_pairs={{0,1},{1,0},{2,3},{3,2},{4,5},{5,4},{6,7},{7,6},{8,9},{9,8},{10,11... | collective-permute-start | bytes 6291464 | tf_op jit(solution)/shard_map/ppermute | solution.py:281
  34.1 74.4 %collective-permute-start.1 = (bf16[2,256,2048]{2,1,0:T(8,128)(2,1)}, bf16[2,256,2048]{2,1,0:T(8,128)(2,1)}, u32[]{:S(2)}, u32[]{:S(2)}) collective-permute-start(bf16[2,256,2048]{2,1,0:T(8,128)(2,1)} %cut_stack.3), channel_id=1, source_target_pairs={{0,2},{1,3},{2,0},{3,1},{4,6},{5,7},{6,4},{7,5},{8,10},{9,11},{10,... | collective-permute-start | bytes 6291464 | tf_op jit(solution)/shard_map/ppermute | solution.py:282
  83.5 75.2 %all-to-all-start.1 = ((bf16[8,64,2560]{2,1,0:T(8,128)(2,1)}), bf16[8,64,2560]{2,1,0:T(8,128)(2,1)}, u32[]{:S(2)}, u32[]{:S(2)}) async-start(bf16[8,64,2560]{2,1,0:T(8,128)(2,1)} %gather_fusion.1), calls=%async_computation.1 | async-start | bytes 5242880 | tf_op jit(solution)/shard_map/all_to_all | solution.py:309
  88.6 42.9 %collective-permute-start.6 = (bf16[256,1024]{1,0:T(8,128)(2,1)}, bf16[256,1024]{1,0:T(8,128)(2,1)S(1)}, u32[]{:S(2)}, u32[]{:S(2)}) collective-permute-start(bf16[256,1024]{1,0:T(8,128)(2,1)} %collective-permute-done.2.refs_0_), channel_id=1, source_target_pairs={{0,2},{1,3},{2,0},{3,1},{4,6},{5,7},{6,4},{7,5},{8,10},{9,11},{10,... | collective-permute-start | bytes 1572872 | tf_op jit(solution)/shard_map/ppermute | solution.py:282
  90.1 41.4 %collective-permute-start.7 = (bf16[256,1024]{1,0:T(8,128)(2,1)}, bf16[256,1024]{1,0:T(8,128)(2,1)S(1)}, u32[]{:S(2)}, u32[]{:S(2)}) collective-permute-start(bf16[256,1024]{1,0:T(8,128)(2,1)} %copy-done.9), channel_id=1, source_target_pairs={{0,1},{1,0},{2,3},{3,2},{4,5},{5,4},{6,7},{7,6},{8,9},{9,8},{10,11... | collective-permute-start | bytes 1572872 | tf_op jit(solution)/shard_map/ppermute | solution.py:281
  92.6 50.1 %collective-permute-start.10 = (bf16[256,1024]{1,0:T(8,128)(2,1)S(1)}, bf16[256,1024]{1,0:T(8,128)(2,1)S(1)}, u32[]{:S(2)}, u32[]{:S(2)}) collective-permute-start(bf16[256,1024]{1,0:T(8,128)(2,1)S(1)} %slice_bitcast_fusion.1), channel_id=1, source_target_pairs={{0,2},{1,3},{2,0},{3,1},{4,6},{5,7},{6,4},{7,5},{8,10},{9,11},{10,... | collective-permute-start | bytes 1572872 | tf_op jit(solution)/shard_map/ppermute | solution.py:282
  107.8 1.3 copy-start.2
  107.8 35.8 %collective-permute-start.11 = (bf16[256,1024]{1,0:T(8,128)(2,1)S(1)}, bf16[256,1024]{1,0:T(8,128)(2,1)S(1)}, u32[]{:S(2)}, u32[]{:S(2)}) collective-permute-start(bf16[256,1024]{1,0:T(8,128)(2,1)S(1)} %slice_bitcast_fusion), channel_id=1, source_target_pairs={{0,1},{1,0},{2,3},{3,2},{4,5},{5,4},{6,7},{7,6},{8,9},{9,8},{10,11... | collective-permute-start | bytes 1572872 | tf_op jit(solution)/shard_map/ppermute | solution.py:281
  128.1 2.4 %copy-start.3 = (bf16[2,256,2048]{2,1,0:T(8,128)(2,1)S(1)}, bf16[2,256,2048]{2,1,0:T(8,128)(2,1)}, u32[]{:S(2)}) copy-start(bf16[2,256,2048]{2,1,0:T(8,128)(2,1)} %copy-done.2) | copy-start | bytes 6291460
  131.6 0.8 copy-start.5
  132.4 0.8 copy-start.6
  139.3 19.4 %collective-permute-start.12 = (bf16[4,128,128]{2,1,0:T(8,128)(2,1)}, bf16[4,128,128]{2,1,0:T(8,128)(2,1)S(1)}, u32[]{:S(2)}, u32[]{:S(2)}) collective-permute-start(bf16[4,128,128]{2,1,0:T(8,128)(2,1)} %shrink_parts.1.refs_2_.refs_7_), channel_id=1, source_target_pairs={{0,1},{1,0},{2,3},{3,2},{4,5},{5,4},{6,7},{7,6},{8,9},{9,8},{10,11... | collective-permute-start | bytes 393224 | tf_op jit(solution)/shard_map/ppermute | solution.py:281
  140.1 18.6 %collective-permute-start.13 = (bf16[4,128,128]{2,1,0:T(8,128)(2,1)}, bf16[4,128,128]{2,1,0:T(8,128)(2,1)S(1)}, u32[]{:S(2)}, u32[]{:S(2)}) collective-permute-start(bf16[4,128,128]{2,1,0:T(8,128)(2,1)} %shrink_parts.1.refs_2_.refs_7_), channel_id=1, source_target_pairs={{0,2},{1,3},{2,0},{3,1},{4,6},{5,7},{6,4},{7,5},{8,10},{9,11},{10,... | collective-permute-start | bytes 393224 | tf_op jit(solution)/shard_map/ppermute | solution.py:282
  141.6 17.1 %collective-permute-start.14 = (bf16[4,128,128]{2,1,0:T(8,128)(2,1)}, bf16[4,128,128]{2,1,0:T(8,128)(2,1)S(1)}, u32[]{:S(2)}, u32[]{:S(2)}) collective-permute-start(bf16[4,128,128]{2,1,0:T(8,128)(2,1)} %shrink_parts.1.refs_2_.refs_7_), channel_id=1, source_target_pairs={{0,3},{1,2},{2,1},{3,0},{4,7},{5,6},{6,5},{7,4},{8,11},{9,10},{10,... | collective-permute-start | bytes 393224 | tf_op jit(solution)/shard_map/ppermute | solution.py:283
  142.7 2.4 %copy-start.10 = (bf16[256,1024]{1,0:T(8,128)(2,1)}, bf16[256,1024]{1,0:T(8,128)(2,1)S(1)}, u32[]{:S(2)}) copy-start(bf16[256,1024]{1,0:T(8,128)(2,1)S(1)} %collective-permute-done.10.refs_2_) | copy-start | bytes 1572868
  142.7 26.9 %collective-permute-start.9 = (bf16[2,256,1024]{2,1,0:T(8,128)(2,1)}, bf16[2,256,1024]{2,1,0:T(8,128)(2,1)S(1)}, u32[]{:S(2)}, u32[]{:S(2)}) collective-permute-start(bf16[2,256,1024]{2,1,0:T(8,128)(2,1)} %slice.21), channel_id=1, source_target_pairs={{0,1},{1,0},{2,3},{3,2},{4,5},{5,4},{6,7},{7,6},{8,9},{9,8},{10,11... | collective-permute-start | bytes 3145736 | tf_op jit(solution)/shard_map/ppermute | solution.py:281
  143.6 1.5 copy-start.11
  143.6 27.0 %collective-permute-start.8 = (bf16[2,256,1024]{2,1,0:T(8,128)(2,1)}, bf16[2,256,1024]{2,1,0:T(8,128)(2,1)S(1)}, u32[]{:S(2)}, u32[]{:S(2)}) collective-permute-start(bf16[2,256,1024]{2,1,0:T(8,128)(2,1)} %slice.20), channel_id=1, source_target_pairs={{0,2},{1,3},{2,0},{3,1},{4,6},{5,7},{6,4},{7,5},{8,10},{9,11},{10,... | collective-permute-start | bytes 3145736 | tf_op jit(solution)/shard_map/ppermute | solution.py:282
  158.6 0.7 copy-start.12
  158.6 0.7 copy-start.13
  158.7 0.7 copy-start.14
  169.7 1.0 copy-start.7
  170.7 1.0 copy-start.8
  171.7 14.6 %copy-start.1 = (bf16[4,64,2560]{2,1,0:T(8,128)(2,1)S(1)}, bf16[4,64,2560]{2,1,0:T(8,128)(2,1)}, u32[]{:S(2)}) copy-start(bf16[4,64,2560]{2,1,0:T(8,128)(2,1)} %param.9) | copy-start | bytes 3932164

commit v3 on v2

--- a/solution.py
+++ b/solution.py
@@ -45,25 +45,30 @@
     return ref[:, at[0] : at[1]] if isinstance(at, tuple) else ref[at]
 
 
-def cut_kernel(slices_ref, tokens_ref, out_ref):
-    out_ref[0] = tokens_ref[...]
-
-
-def cut_stack(tokens, slices, parts):
+def cut_kernel(columns_ref, *refs):
+    stacks = len(refs) // 2
+    for source, out in zip(refs[:stacks], refs[stacks:]):
+        out[0] = source[...]
+
+
+def cut_stacks(tokens, columns, stacks):
     rows, width = tokens.shape
-    count, part, band = slices.shape[0], width // parts, rows * parts // 8
+    count, part = columns.shape[0] // stacks, width // 8
     return pl.pallas_call(
         cut_kernel,
         grid_spec=pltpu.PrefetchScalarGridSpec(
             num_scalar_prefetch=1,
-            grid=(count, rows // band),
-            in_specs=[pl.BlockSpec((band, part), lambda i, r, slices: (r, slices[i]))],
-            out_specs=pl.BlockSpec((1, band, part), lambda i, r, slices: (i, r, 0)),
+            grid=(count,),
+            in_specs=[
+                pl.BlockSpec((rows, part), lambda i, columns, first=stack * count: (0, columns[first + i]))
+                for stack in range(stacks)
+            ],
+            out_specs=[pl.BlockSpec((1, rows, part), lambda i, columns: (i, 0, 0))] * stacks,
         ),
-        out_shape=jax.ShapeDtypeStruct((count, rows, part), tokens.dtype),
-        cost_estimate=cost(0, 4 * count * rows * part),
-        name="cut_stack",
-    )(slices, tokens)
+        out_shape=[jax.ShapeDtypeStruct((count, rows, part), tokens.dtype)] * stacks,
+        cost_estimate=cost(0, 4 * stacks * count * rows * part),
+        name="cut_stacks",
+    )(columns, *[tokens] * stacks)
 
 
 def project_kernel(sets, weights_at, totals_at, update, plan_ref, *refs):
@@ -81,11 +86,8 @@
         if update is None:
             out_ref[number] = total
         else:
-            first_set, shrinks_at, panels_at = update
-            shrink = 0
-            for at in shrinks_at:
-                shrink += refs[at][plan_ref[first_set + number]].astype(jnp.float32)
-            shrink = shrink.astype(jnp.bfloat16)
+            shrink_at, panels_at = update
+            shrink = refs[shrink_at][...]
             for block, panel in enumerate(panels_at):
                 rank = refs[panel].shape[0]
                 term = jnp.dot(
@@ -131,12 +133,10 @@
         out_shape = jax.ShapeDtypeStruct((len(sets), rows, columns), jnp.float32)
         out_spec = pl.BlockSpec((len(sets), rows, tile), lambda n, plan: (0, 0, n))
     else:
-        first_set, shrinks, panels = update
-        shrinks_at, panels_at = [], []
-        for shrink in shrinks:
-            in_specs.append(whole_spec(shrink))
-            operands.append(shrink)
-            shrinks_at.append(len(operands) - 1)
+        first_set, shrink, panels = update
+        in_specs.append(whole_spec(shrink))
+        operands.append(shrink)
+        shrink_at, panels_at = len(operands) - 1, []
         for block in range(rows // BLOCK):
             index = PANELS_AT + first_set * (rows // BLOCK) + block
             in_specs.append(
@@ -144,7 +144,7 @@
             )
             operands.append(panels)
             panels_at.append(len(operands) - 1)
-        updating = (first_set, shrinks_at, panels_at)
+        updating = (shrink_at, panels_at)
         out_shape = jax.ShapeDtypeStruct(into.shape, into.dtype)
         out_spec = pl.BlockSpec((rows, tile), lambda n, plan: (plan[first_set], n))
         in_specs.append(pl.BlockSpec(memory_space=pl.ANY))
@@ -164,7 +164,7 @@
         out_shape=out_shape,
         input_output_aliases=aliases,
         cost_estimate=cost(weigh * 2 * products * columns, weigh * moved),
-        compiler_params=pltpu.CompilerParams(vmem_limit_bytes=56 * MIB),
+        compiler_params=pltpu.CompilerParams(vmem_limit_bytes=32 * MIB),
         name=name,
     )(plan, *operands)
 
@@ -172,10 +172,9 @@
 def finish_kernel(count, plan_ref, *refs):
     own_ref, near_ref, panel_one, panel_two, out_ref = refs[0], refs[1], refs[-3], refs[-2], refs[-1]
     number = pl.program_id(0)
-    shrink = 0
-    for ref in refs[2:-3]:
-        shrink += ref[plan_ref[number]].astype(jnp.float32)
-    shrink = shrink.astype(jnp.bfloat16)
+    shrink = refs[2][...]
+    for other in range(1, count):
+        shrink = jnp.where(number == other, refs[2 + other][...], shrink)
     rank = panel_one.shape[0]
     for block, panel in enumerate((panel_one, panel_two)):
         term = adapter_scale * jnp.dot(
@@ -216,16 +215,16 @@
         ),
         out_shape=jax.ShapeDtypeStruct((row_total, columns), jnp.bfloat16),
         cost_estimate=cost(12 * rows * rank * columns, 18 * rows * columns),
-        compiler_params=pltpu.CompilerParams(vmem_limit_bytes=56 * MIB),
+        compiler_params=pltpu.CompilerParams(vmem_limit_bytes=32 * MIB),
         name="finish_rows",
     )(plan, own, near, *shrinks, panels, panels)
 
 
 def shrink_kernel(sets, panels_at, plan_ref, *refs):
-    panels_ref, out_ref = refs[panels_at], refs[-1]
+    panels_ref = refs[panels_at]
     rank = panels_ref.shape[1]
     nt = (((1,), (1,)), ((), ()))
-    for number, terms in enumerate(sets):
+    for number, (terms, out_ref) in enumerate(zip(sets, refs[panels_at + 1 :])):
         blocks = refs[terms[0][0]].shape[-2] // BLOCK
         for block in range(blocks):
             panel = plan_ref[PANELS_AT + number * blocks + block]
@@ -238,9 +237,7 @@
                     nt,
                     preferred_element_type=jnp.float32,
                 )
-            out_ref[plan_ref[number], :, block * rank : (block + 1) * rank] = total.astype(
-                out_ref.dtype
-            )
+            out_ref[:, block * rank : (block + 1) * rank] = total
 
 
 def shrink_parts(tokens, sets, panels, plan):
@@ -250,7 +247,7 @@
     flat += [[(known.place(array), at, start) for array, at, start in terms] for terms in sets]
     operands = known.arrays + [panels]
     _, rank, depth = panels.shape
-    shape = (len(flat), BLOCK, rank * (rows // BLOCK))
+    shape = (BLOCK, rank * (rows // BLOCK))
     in_specs = [whole_spec(a) for a in operands]
     in_specs[0] = pl.BlockSpec((rows, depth), lambda i, plan: (0, plan[0]))
     return pl.pallas_call(
@@ -259,11 +256,11 @@
             num_scalar_prefetch=1,
             grid=(1,),
             in_specs=in_specs,
-            out_specs=pl.BlockSpec(shape, lambda *_: (0, 0, 0)),
+            out_specs=[pl.BlockSpec(shape, lambda *_: (0, 0))] * len(flat),
         ),
-        out_shape=jax.ShapeDtypeStruct(shape, tokens.dtype),
+        out_shape=[jax.ShapeDtypeStruct(shape, jnp.float32)] * len(flat),
         cost_estimate=cost(8 * len(flat) * rows * depth * rank, 2 * (panels.size + len(flat) * rows * depth)),
-        compiler_params=pltpu.CompilerParams(vmem_limit_bytes=56 * MIB),
+        compiler_params=pltpu.CompilerParams(vmem_limit_bytes=32 * MIB),
         name="shrink_parts",
     )(plan, *operands)
 
@@ -288,19 +285,14 @@
     mine = jnp.sum(jnp.where((members[:, None] == jnp.arange(4))[:, :, None], mine[None], 0), axis=1)
     plan = jnp.concatenate([members, mine.reshape(-1)]).astype(jnp.int32)
 
-    def cut(j, second):
-        return lax.dynamic_slice(tokens, (0, (member ^ 3 ^ j) * depth + second * half), (rows, half))
-
     def eighths(*places):
-        numbers = jnp.stack([(member ^ 3 ^ j) * 2 + second for j, second in places])
-        return cut_stack(tokens, numbers.astype(jnp.int32), 8)
-
-    a0, b0 = cut(0, 0), cut(0, 1)
-    xa0, yb0 = to_x(a0), to_y(b0)
-    early_x, early_y = eighths((0, 1), (3, 0), (3, 1)), eighths((0, 0), (3, 0), (3, 1))
-    x_early, y_early = to_x(early_x), to_y(early_y)
-    late = cut_stack(tokens, jnp.stack([member ^ 2, member ^ 1]).astype(jnp.int32), 4)
-    x12, y12 = to_x(late), to_y(late)
+        return jnp.stack([(member ^ 3 ^ j) * 2 + second for j, second in places]).astype(jnp.int32)
+
+    (s03,) = cut_stacks(tokens, eighths((0, 0), (0, 1), (3, 0), (3, 1)), 1)
+    x03, y03 = to_x(s03), to_y(s03)
+    a12, b12 = cut_stacks(tokens, eighths((1, 0), (2, 0), (1, 1), (2, 1)), 2)
+    xa12, ya12 = to_x(a12), to_y(a12)
+    xb12, yb12 = to_x(b12), to_y(b12)
 
     def chosen(panels, select):
         return jnp.take(panels, select, axis=0, mode="clip")
@@ -308,50 +300,65 @@
     def exchange(panels):
         return lax.all_to_all(panels, "grp", split_axis=0, concat_axis=0, tiled=True)
 
-    down_out = chosen(down_weight, after(select_slot, xa0, yb0, early_x, early_y))
+    down_out = chosen(down_weight, after(select_slot, a12, b12))
     down = exchange(down_out)
 
     own = project(
         [[(tokens, (i * depth, (i + 1) * depth), None, i) for i in range(4)]],
-        frozen_weight, tile_of(frozen_weight.shape[1], 512), after(plan, down_out, late), rows, weigh=0, name="own_rows",
+        frozen_weight, tile_of(frozen_weight.shape[1], 512), after(plan, down_out), rows, weigh=0, name="own_rows",
     )
 
     tile = tile_of(frozen_weight.shape[1], 512)
     near = project(
         [
-            [(xa0, None, 2, 0), (x_early, 0, 2, 1), (x_early, 1, 1, 0), (x_early, 2, 1, 1)],
-            [(y_early, 1, 2, 0), (y_early, 2, 2, 1), (y_early, 0, 1, 0), (yb0, None, 1, 1)],
+            [(x03, 0, 2, 0), (x03, 1, 2, 1), (x03, 2, 1, 0), (x03, 3, 1, 1)],
+            [(y03, 2, 2, 0), (y03, 3, 2, 1), (y03, 0, 1, 0), (y03, 1, 1, 1)],
         ],
-        frozen_weight, tile, after(plan, own), rows, weigh=0, name="near_rows",
+        frozen_weight, tile, after(plan, own), rows, weigh=6, name="near_rows",
     )
     up = exchange(chosen(up_weight, after(select_slot, down, near)))
-
-    da0, db0 = to_y(after(xa0, x_early, y_early)), to_x(after(yb0, x_early, y_early))
-    da3, db3 = to_y(after(x_early[1], near)), to_x(after(y_early[2], near))
     near = project(
-        [[(x12, 0, 3, None), (x12, 1, 0, None)], [(y12, 1, 3, None), (y12, 0, 0, None)]],
+        [
+            [(xa12, 0, 3, 0), (xa12, 1, 0, 0)],
+            [(ya12, 1, 3, 0), (ya12, 0, 0, 0)],
+        ],
+        frozen_weight, tile, plan, rows, total=near, weigh=2, name="near_rows_more",
+    )
+
+    da0, db0 = to_y(after(x03[0], xa12, ya12)), to_x(after(y03[1], xa12, ya12))
+    da3, db3 = to_y(after(x03[2], near)), to_x(after(y03[3], near))
+    near = project(
+        [
+            [(xb12, 0, 3, 1), (xb12, 1, 0, 1)],
+            [(yb12, 1, 3, 1), (yb12, 0, 0, 1)],
+        ],
         frozen_weight, tile, plan, rows, total=near, name="near_rows_rest",
     )
 
     share = shrink_parts(
         tokens,
-        [[(x12, 1, 0)], [(y12, 0, 0)], [(da0, None, 0), (db0, None, half)]],
+        [
+            [(xa12, 1, 0), (xb12, 1, half)],
+            [(ya12, 0, 0), (yb12, 0, half)],
+            [(da0, None, 0), (db0, None, half)],
+        ],
         down,
         after(plan, near),
     )
-    shrinks = [share, to_x(share), to_y(share), across(share)]
-    da12 = to_y(after(x12[:, :, :half], share))
-    db12 = to_x(after(y12[:, :, half:], share))
+    home = share[0] + to_x(share[1]) + to_y(share[2]) + across(share[3])
+    home = home.astype(jnp.bfloat16)
+    shrinks = [home, to_x(home), to_y(home), across(home)]
+    da12, db12 = to_y(after(xa12, home)), to_x(after(yb12, home))
 
     far = project(
         [[(da0, None, 0, 0), (db0, None, 0, 1), (da3, None, 3, 0), (db3, None, 3, 1)]],
-        frozen_weight, tile_of(frozen_weight.shape[1], 640), after(plan, share), rows, name="far_rows",
-    )
-    out = finish(own, near, shrinks, up, after(plan, far), 4 * rows)
+        frozen_weight, tile_of(frozen_weight.shape[1], 640), after(plan, home), rows, name="far_rows",
+    )
+    out = finish(own, near, shrinks[:3], up, after(plan, far), 4 * rows)
     return project(
         [[(da12, 0, 1, 0), (db12, 0, 1, 1), (da12, 1, 2, 0), (db12, 1, 2, 1)]],
         frozen_weight, tile_of(frozen_weight.shape[1], 640), plan, rows,
-        total=far, update=(3, shrinks, up), into=out, name="last_rows",
+        total=far, update=(3, shrinks[3], up), into=out, name="last_rows",
     )
 
 

time: 187 us -> 179 us (0.957)
  Pallas kernels: 115 us -> 96.5 us
  local copies, waits for them, and re-layouts: 16.7 us -> 23.4 us
  waiting for transfers between devices: 23 us -> 25.5 us
  starting transfers between devices: 28.6 us -> 30.5 us
    ppermute x7 -> x8, waiting for transfers between devices: 2.77 us -> 17 us  [square(): to_y = lambda v: lax.ppermute(v, 'tp', [(i, i ^ 2) for i in range(4)])]
    ppermute x7 -> x8, waiting for transfers between devices: 20.2 us -> 6.87 us  [square(): to_x = lambda v: lax.ppermute(v, 'tp', [(i, i ^ 1) for i in range(4)])]
    unnamed x34 -> x38, local copies, waits for them, and re-layouts: 4.08 us -> 16 us
    pallas_call x5 -> x6, Pallas kernels: 86.8 us -> 79.2 us  [project(): pl.pallas_call(functools.partial(project_kernel, flat, weights_at, totals...]
    pallas_call x3 -> x2, Pallas kernels: 12.7 us -> 7.87 us  [cut_stacks(): pl.pallas_call(cut_kernel, grid_spec=pltpu.PrefetchScalarGridSpec(num_sca...]
    pallas_call x1, Pallas kernels: 9.22 us -> 4.71 us  [finish(): pl.pallas_call(functools.partial(finish_kernel, 3), grid_spec=pltpu.Prefe...]
    slice x2 -> x0, local copies, waits for them, and re-layouts: 3.49 us -> none  [the longest x1 2.42 us: square(): db12 = to_x(after(y12[:, :, half:], share))]
    dynamic_slice x1 -> x0, local copies, waits for them, and re-layouts: 2.18 us -> none  [cut(): lax.dynamic_slice(tokens, (0, (member ^ 3 ^ j) * depth + second * half),...]
  transfers between devices with their start and end apart: 17 -> 20, of which waited for: 8 -> 8; matrix products, arithmetic and copies ran while one was open for 6% -> 5% of each run, Pallas kernels for 54% -> 44%
where the time goes in v3:
time: 179 us; the launch traced here: 178 us
  Pallas kernels  96.5 us (54%)
  starting transfers between devices  30.5 us (17%)
  waiting for transfers between devices  25.5 us (14%)
  local copies, waits for them, and re-layouts  23.4 us (13%)
  other arithmetic  1.8 us (1%)
    pallas_call x6, Pallas kernels, project(): pl.pallas_call(functools.partial(project_kernel, flat, weights_at, totals...  79.2 us
    ppermute x8, waiting for transfers between devices, square(): to_y = lambda v: lax.ppermute(v, 'tp', [(i, i ^ 2) for i in range(4)])  17 us
    unnamed x38, local copies, waits for them, and re-layouts  16 us
    all_to_all x2, starting transfers between devices, exchange(): lax.all_to_all(panels, 'grp', split_axis=0, concat_axis=0, tiled=True)  10.2 us
    ppermute x8, starting transfers between devices, square(): to_y = lambda v: lax.ppermute(v, 'tp', [(i, i ^ 2) for i in range(4)])  8.62 us
    ppermute x8, starting transfers between devices, square(): to_x = lambda v: lax.ppermute(v, 'tp', [(i, i ^ 1) for i in range(4)])  8.61 us
    pallas_call x2, Pallas kernels, cut_stacks(): pl.pallas_call(cut_kernel, grid_spec=pltpu.PrefetchScalarGridSpec(num_sca...  7.87 us
    ppermute x8, waiting for transfers between devices, square(): to_x = lambda v: lax.ppermute(v, 'tp', [(i, i ^ 1) for i in range(4)])  6.87 us
  transfers between devices with their start and end apart: 20, of which 8 were waited for; matrix products, arithmetic and copies ran while one was open for 5% of the time, Pallas kernels for 44%

profile of v3, /device:TPU:0, one launch (start us, length us, event | category | flops | bytes accessed | tf_op | source)
XLA Modules:
  0.0 177.9 jit_solution(1440782553867953858)
XLA Ops:
  0.0 0.6 pad_add_fusion.2.columns_ref
  0.6 4.5 %cut_stacks.3 = bf16[4,256,1024]{2,1,0:T(8,128)(2,1)} custom-call(s32[4]{0:T(128)} %pad_add_fusion.2.columns_ref, bf16[256,8192]{1,0:T(8,128)(2,1)} %refs_0_.7), custom_call_target="tpu_custom_call" | custom-call | bytes 4194304 | tf_op jit(solution)/shard_map/cut_stacks/pallas_call | solution.py:57
  5.1 3.0 %collective-permute-start.5 = (bf16[4,256,1024]{2,1,0:T(8,128)(2,1)}, bf16[4,256,1024]{2,1,0:T(8,128)(2,1)}, u32[]{:S(2)}, u32[]{:S(2)}) collective-permute-start(bf16[4,256,1024]{2,1,0:T(8,128)(2,1)} %cut_stacks.3), channel_id=1, source_target_pairs={{0,2},{1,3},{2,0},{3,1},{4,6},{5,7},{6,4},{7,5},{8,10},{9,11},{10,... | collective-permute-start | bytes 6291464 | tf_op jit(solution)/shard_map/ppermute | solution.py:279
  8.1 1.4 collective-permute-start.4
  9.5 0.6 pad_add_fusion.1.columns_ref
  10.2 3.4 %cut_stacks.2 = (bf16[2,256,1024]{2,1,0:T(8,128)(2,1)}, bf16[2,256,1024]{2,1,0:T(8,128)(2,1)}) custom-call(s32[4]{0:T(128)} %pad_add_fusion.1.columns_ref, bf16[256,8192]{1,0:T(8,128)(2,1)} %refs_0_.7, bf16[256,8192]{1,0:T(8,128)(2,1)} %refs_0_.7), custom_call_target="tpu_custom_call" | custom-call | bytes 4194304 | tf_op jit(solution)/shard_map/cut_stacks/pallas_call | solution.py:57
  13.6 0.5 collective-permute-start.3
  14.5 2.0 %gather_fusion = bf16[8,64,2048]{2,1,0:T(8,128)(2,1)} fusion(bf16[4,64,2048]{2,1,0:T(8,128)(2,1)S(1)} %copy-done.16, s32[1024]{0:T(1024)S(1)} %pad_clamp_fusion.1), kind=kCustom, calls=%fused_computation | custom fusion | bytes 4194336 | tf_op jit(solution)/shard_map/jit(_take)/gather | solution.py:298
  16.5 5.3 %all-to-all-start = ((bf16[8,64,2048]{2,1,0:T(8,128)(2,1)}), bf16[8,64,2048]{2,1,0:T(8,128)(2,1)S(1)}, u32[]{:S(2)}, u32[]{:S(2)}) async-start(bf16[8,64,2048]{2,1,0:T(8,128)(2,1)} %gather_fusion), calls=%async_computation | async-start | bytes 4194304 | tf_op jit(solution)/shard_map/all_to_all | solution.py:301
  22.6 2.2 %copy-done.2 = bf16[256,8192]{1,0:T(8,128)(2,1)S(1)} copy-done((bf16[256,8192]{1,0:T(8,128)(2,1)S(1)}, bf16[256,8192]{1,0:T(8,128)(2,1)}, u32[]{:S(2)}) %copy-start.2) | copy-done | bytes 4194328
  24.8 18.3 %own_rows.1.refs_0_ = f32[1,256,2560]{2,1,0:T(8,128)S(1)} custom-call(s32[12]{0:T(128)S(1)} %pad_add_fusion.plan_ref, bf16[256,8192]{1,0:T(8,128)(2,1)S(1)} %copy-done.2, bf16[8192,2560]{1,0:T(8,128)(2,1)} %refs_5_.5, bf16[8192,2560]{1,0:T(8,128)(2,1)} %refs_5_.5, bf16[8192,2560]{1,0:T(8,128)(2,1)} %refs_5_.5, bf16[8192,2560]{1,0:T(8,128)(2,1)} %refs_5_.5), custom_call_target="tpu_custom_call" | custom-call | tf_op jit(solution)/shard_map/own_rows/pallas_call | solution.py:156
  43.1 1.5 copy-done.10
  44.6 10.3 %collective-permute-done.5.refs_1_ = bf16[4,256,1024]{2,1,0:T(8,128)(2,1)} collective-permute-done((bf16[4,256,1024]{2,1,0:T(8,128)(2,1)}, bf16[4,256,1024]{2,1,0:T(8,128)(2,1)}, u32[]{:S(2)}, u32[]{:S(2)}) %collective-permute-start.5) | collective-permute-done | bytes 2097184 | tf_op jit(solution)/shard_map/ppermute | solution.py:279
  54.8 2.1 %collective-permute-done.4.refs_0_ = bf16[4,256,1024]{2,1,0:T(8,128)(2,1)} collective-permute-done((bf16[4,256,1024]{2,1,0:T(8,128)(2,1)}, bf16[4,256,1024]{2,1,0:T(8,128)(2,1)}, u32[]{:S(2)}, u32[]{:S(2)}) %collective-permute-start.4) | collective-permute-done | bytes 2097184 | tf_op jit(solution)/shard_map/ppermute | solution.py:278
  56.9 16.6 %near_rows.1.refs_4_.refs_5_ = f32[2,256,2560]{2,1,0:T(8,128)S(1)} custom-call(s32[12]{0:T(128)S(1)} %pad_add_fusion.plan_ref, bf16[4,256,1024]{2,1,0:T(8,128)(2,1)} %collective-permute-done.4.refs_0_, bf16[4,256,1024]{2,1,0:T(8,128)(2,1)} %collective-permute-done.5.refs_1_, bf16[8192,2560]{1,0:T(8,128)(2,1)} %refs_5_.5, bf16[8192,2560]{1,0:T(8,128)(2,1)} %refs_5_.5, ...), custom_call_target="tpu_custom_call" | custom-call | flops 64424509440 | bytes 283115520 | tf_op jit(solution)/shard_map/near_rows/pallas_call | solution.py:156
  73.5 2.3 %copy-done.6 = f32[2,256,2560]{2,1,0:T(8,128)} copy-done((f32[2,256,2560]{2,1,0:T(8,128)}, f32[2,256,2560]{2,1,0:T(8,128)S(1)}, u32[]{:S(2)}) %copy-start.6) | copy-done | bytes 5242904
  75.9 2.3 %gather_fusion.1 = bf16[8,64,2560]{2,1,0:T(8,128)(2,1)} fusion(bf16[4,64,2560]{2,1,0:T(8,128)(2,1)S(1)} %copy-done, s32[1024]{0:T(1024)S(1)} %pad_clamp_fusion), kind=kCustom, calls=%fused_computation.1 | custom fusion | bytes 5242912 | tf_op jit(solution)/shard_map/jit(_take)/gather | solution.py:298
  78.2 4.9 %all-to-all-start.1 = ((bf16[8,64,2560]{2,1,0:T(8,128)(2,1)}), bf16[8,64,2560]{2,1,0:T(8,128)(2,1)S(1)}, u32[]{:S(2)}, u32[]{:S(2)}) async-start(bf16[8,64,2560]{2,1,0:T(8,128)(2,1)} %gather_fusion.1), calls=%async_computation.1 | async-start | bytes 5242880 | tf_op jit(solution)/shard_map/all_to_all | solution.py:301
  83.0 0.5 collective-permute-start.2
  83.5 1.5 collective-permute-start.1
  85.0 1.3 slice_bitcast_fusion
  86.3 0.6 collective-permute-start.7
  86.9 1.3 slice_bitcast_fusion.1
  88.2 1.6 collective-permute-start.6
  89.8 2.5 %copy-done.7 = f32[2,256,2560]{2,1,0:T(8,128)S(1)} copy-done((f32[2,256,2560]{2,1,0:T(8,128)S(1)}, f32[2,256,2560]{2,1,0:T(8,128)}, u32[]{:S(2)}) %copy-start.7) | copy-done | bytes 5242904
  92.3 9.9 %near_rows_more.1.refs_4_.refs_5_ = f32[2,256,2560]{2,1,0:T(8,128)S(1)} custom-call(s32[12]{0:T(128)S(1)} %pad_add_fusion.plan_ref, bf16[2,256,1024]{2,1,0:T(8,128)(2,1)} %collective-permute-done.refs_0_.refs_1_, bf16[2,256,1024]{2,1,0:T(8,128)(2,1)} %collective-permute-done.3.refs_1_.refs_3_, bf16[8192,2560]{1,0:T(8,128)(2,1)} %refs_5_.5, ...), custom_call_target="tpu_custom_call" | custom-call | flops 10737418240 | bytes 62914560 | tf_op jit(solution)/shard_map/near_rows_more/pallas_call | solution.py:156
  102.2 0.5 collective-permute-start.13
  102.7 6.6 %collective-permute-done.2.refs_1_.refs_4_ = bf16[2,256,1024]{2,1,0:T(8,128)(2,1)} collective-permute-done((bf16[2,256,1024]{2,1,0:T(8,128)(2,1)}, bf16[2,256,1024]{2,1,0:T(8,128)(2,1)}, u32[]{:S(2)}, u32[]{:S(2)}) %collective-permute-start.2) | collective-permute-done | bytes 1048608 | tf_op jit(solution)/shard_map/ppermute | solution.py:279
  109.3 1.4 collective-permute-start.14
  110.8 9.9 %near_rows_rest.1.refs_1_ = f32[2,256,2560]{2,1,0:T(8,128)S(1)} custom-call(s32[12]{0:T(128)S(1)} %pad_add_fusion.plan_ref, bf16[2,256,1024]{2,1,0:T(8,128)(2,1)S(1)} %collective-permute-done.1.refs_0_.refs_2_, bf16[2,256,1024]{2,1,0:T(8,128)(2,1)} %collective-permute-done.2.refs_1_.refs_4_, bf16[8192,2560]{1,0:T(8,128)(2,1)} %refs_5_.5, ...), custom_call_target="tpu_custom_call" | custom-call | flops 10737418240 | bytes 62914560 | tf_op jit(solution)/shard_map/near_rows_rest/pallas_call | solution.py:156
  121.0 4.7 %shrink_parts.1 = (f32[128,128]{1,0:T(8,128)S(1)}, f32[128,128]{1,0:T(8,128)S(1)}, f32[128,128]{1,0:T(8,128)S(1)}, f32[128,128]{1,0:T(8,128)S(1)}) custom-call(s32[12]{0:T(128)S(1)} %pad_add_fusion.plan_ref, bf16[256,8192]{1,0:T(8,128)(2,1)S(1)} %copy-done.3, bf16[2,256,1024]{2,1,0:T(8,128)(2,1)} %collective-permute-done.refs_0_.refs_1_, ...), custom_call_target="tpu_custom_call" | custom-call | flops 1073741824 | bytes 6291456 | tf_op jit(solution)/shard_map/shrink_parts/pallas_call | solution.py:253
  125.7 0.6 collective-permute-start.8
  126.3 1.5 collective-permute-start.9
  127.8 1.5 collective-permute-start.10
  129.2 4.3 %collective-permute-done.8 = f32[128,128]{1,0:T(8,128)S(1)} collective-permute-done((f32[128,128]{1,0:T(8,128)S(1)}, f32[128,128]{1,0:T(8,128)S(1)}, u32[]{:S(2)}, u32[]{:S(2)}) %collective-permute-start.8) | collective-permute-done | bytes 65568 | tf_op jit(solution)/shard_map/ppermute | solution.py:278
  133.6 1.7 collective-permute-done.10
  135.3 0.5 collective-permute-start.17
  135.8 1.5 collective-permute-start.16
  137.3 1.5 collective-permute-start.15
  138.9 0.5 collective-permute-start.11
  139.3 1.5 collective-permute-start.12
  140.8 11.5 %far_rows.1.refs_6_ = f32[1,256,2560]{2,1,0:T(8,128)S(1)} custom-call(s32[12]{0:T(128)S(1)} %pad_add_fusion.plan_ref, bf16[256,1024]{1,0:T(8,128)(2,1)S(1)} %collective-permute-done.6.refs_5_.refs_0_, bf16[256,1024]{1,0:T(8,128)(2,1)S(1)} %collective-permute-done.7.refs_6_.refs_1_, bf16[256,1024]{1,0:T(8,128)(2,1)S(1)} %collective-permute-done.13.refs_2_, ...), custom_call_target="tpu_custom_call" | custom-call | flops 10737418240 | bytes 47185920 | tf_op jit(solution)/shard_map/far_rows/pallas_call | solution.py:156
  152.3 1.5 copy-done.12
  153.8 2.5 %copy-done.9 = f32[2,256,2560]{2,1,0:T(8,128)S(1)} copy-done((f32[2,256,2560]{2,1,0:T(8,128)S(1)}, f32[2,256,2560]{2,1,0:T(8,128)}, u32[]{:S(2)}) %copy-start.9) | copy-done | bytes 5242904
  156.3 1.7 copy-done.11
  158.0 4.7 %finish_rows.1.refs_10_ = bf16[1024,2560]{1,0:T(8,128)(2,1)} custom-call(s32[12]{0:T(128)S(1)} %pad_add_fusion.plan_ref, f32[1,256,2560]{2,1,0:T(8,128)S(1)} %copy-done.11, f32[2,256,2560]{2,1,0:T(8,128)S(1)} %copy-done.9, bf16[128,128]{1,0:T(8,128)(2,1)S(1)} %add_convert_fusion.refs_2_, bf16[128,128]{1,0:T(8,128)(2,1)S(1)} %collective-permute-done.16.refs_3_, ...), custom_call_target="tpu_custom_call" | custom-call | flops 503316480 | bytes 11796480 | tf_op jit(solution)/shard_map/finish_rows/pallas_call | solution.py:198
  163.1 1.7 copy-done.5
  164.8 13.1 %last_rows.1 = bf16[1024,2560]{1,0:T(8,128)(2,1)} custom-call(s32[12]{0:T(128)S(1)} %pad_add_fusion.plan_ref, bf16[2,256,1024]{2,1,0:T(8,128)(2,1)} %collective-permute-done.11.refs_0_, bf16[2,256,1024]{2,1,0:T(8,128)(2,1)} %collective-permute-done.12.refs_1_, bf16[8192,2560]{1,0:T(8,128)(2,1)} %refs_5_.5, ...), custom_call_target="tpu_custom_call", output_to_operand_aliasing={{}: (11, {})} | custom-call | flops 10737418240 | bytes 52428800 | tf_op jit(solution)/shard_map/last_rows/pallas_call | solution.py:156
  (62 shorter events, 1.8 us)
Async XLA Ops:
  0.0 75.9 %copy-start = (bf16[4,64,2560]{2,1,0:T(8,128)(2,1)S(1)}, bf16[4,64,2560]{2,1,0:T(8,128)(2,1)}, u32[]{:S(2)}) copy-start(bf16[4,64,2560]{2,1,0:T(8,128)(2,1)} %param.9) | copy-start | bytes 3932164
  5.1 49.8 %collective-permute-start.5 = (bf16[4,256,1024]{2,1,0:T(8,128)(2,1)}, bf16[4,256,1024]{2,1,0:T(8,128)(2,1)}, u32[]{:S(2)}, u32[]{:S(2)}) collective-permute-start(bf16[4,256,1024]{2,1,0:T(8,128)(2,1)} %cut_stacks.3), channel_id=1, source_target_pairs={{0,2},{1,3},{2,0},{3,1},{4,6},{5,7},{6,4},{7,5},{8,10},{9,11},{10,... | collective-permute-start | bytes 6291464 | tf_op jit(solution)/shard_map/ppermute | solution.py:279
  8.1 48.9 %collective-permute-start.4 = (bf16[4,256,1024]{2,1,0:T(8,128)(2,1)}, bf16[4,256,1024]{2,1,0:T(8,128)(2,1)}, u32[]{:S(2)}, u32[]{:S(2)}) collective-permute-start(bf16[4,256,1024]{2,1,0:T(8,128)(2,1)} %cut_stacks.3), channel_id=1, source_target_pairs={{0,1},{1,0},{2,3},{3,2},{4,5},{5,4},{6,7},{7,6},{8,9},{9,8},{10,11... | collective-permute-start | bytes 6291464 | tf_op jit(solution)/shard_map/ppermute | solution.py:278
  10.2 4.0 %copy-start.17 = (s32[32]{0:T(128)S(1)}, s32[32]{0:T(128)}, u32[]{:S(2)}) copy-start(s32[32]{0:T(128)} %param.10) | copy-start | bytes 388
  10.2 4.0 %copy-start.18 = (s32[64]{0:T(128)S(1)}, s32[64]{0:T(128)}, u32[]{:S(2)}) copy-start(s32[64]{0:T(128)} %param.11) | copy-start | bytes 772
  10.2 4.3 %copy-start.16 = (bf16[4,64,2048]{2,1,0:T(8,128)(2,1)S(1)}, bf16[4,64,2048]{2,1,0:T(8,128)(2,1)}, u32[]{:S(2)}) copy-start(bf16[4,64,2048]{2,1,0:T(8,128)(2,1)} %param.8) | copy-start | bytes 3145732
  13.6 72.7 %collective-permute-start.3 = (bf16[2,256,1024]{2,1,0:T(8,128)(2,1)}, bf16[2,256,1024]{2,1,0:T(8,128)(2,1)}, u32[]{:S(2)}, u32[]{:S(2)}) collective-permute-start(bf16[2,256,1024]{2,1,0:T(8,128)(2,1)} %get-tuple-element.24), channel_id=1, source_target_pairs={{0,2},{1,3},{2,0},{3,1},{4,6},{5,7},{6,4},{7,5},{8,10},{9,11},{10,... | collective-permute-start | bytes 3145736 | tf_op jit(solution)/shard_map/ppermute | solution.py:279
  14.1 72.2 %collective-permute-start = (bf16[2,256,1024]{2,1,0:T(8,128)(2,1)}, bf16[2,256,1024]{2,1,0:T(8,128)(2,1)}, u32[]{:S(2)}, u32[]{:S(2)}) collective-permute-start(bf16[2,256,1024]{2,1,0:T(8,128)(2,1)} %get-tuple-element.24), channel_id=1, source_target_pairs={{0,1},{1,0},{2,3},{3,2},{4,5},{5,4},{6,7},{7,6},{8,9},{9,8},{10,11... | collective-permute-start | bytes 3145736 | tf_op jit(solution)/shard_map/ppermute | solution.py:278
  16.5 59.4 %all-to-all-start = ((bf16[8,64,2048]{2,1,0:T(8,128)(2,1)}), bf16[8,64,2048]{2,1,0:T(8,128)(2,1)S(1)}, u32[]{:S(2)}, u32[]{:S(2)}) async-start(bf16[8,64,2048]{2,1,0:T(8,128)(2,1)} %gather_fusion), calls=%async_computation | async-start | bytes 4194304 | tf_op jit(solution)/shard_map/all_to_all | solution.py:301
  22.6 2.2 %copy-start.2 = (bf16[256,8192]{1,0:T(8,128)(2,1)S(1)}, bf16[256,8192]{1,0:T(8,128)(2,1)}, u32[]{:S(2)}) copy-start(bf16[256,8192]{1,0:T(8,128)(2,1)} %refs_0_.7) | copy-start | bytes 12582916
  43.1 1.5 copy-start.10
  73.5 2.4 %copy-start.6 = (f32[2,256,2560]{2,1,0:T(8,128)}, f32[2,256,2560]{2,1,0:T(8,128)S(1)}, u32[]{:S(2)}) copy-start(f32[2,256,2560]{2,1,0:T(8,128)S(1)} %near_rows.1.refs_4_.refs_5_) | copy-start | bytes 15728644
  75.9 2.3 %copy-start.14 = (bf16[8,64,2048]{2,1,0:T(8,128)(2,1)}, bf16[8,64,2048]{2,1,0:T(8,128)(2,1)S(1)}, u32[]{:S(2)}) copy-start(bf16[8,64,2048]{2,1,0:T(8,128)(2,1)S(1)} %all-to-all-done.refs_7_) | copy-start | bytes 6291460
  78.2 75.6 %all-to-all-start.1 = ((bf16[8,64,2560]{2,1,0:T(8,128)(2,1)}), bf16[8,64,2560]{2,1,0:T(8,128)(2,1)S(1)}, u32[]{:S(2)}, u32[]{:S(2)}) async-start(bf16[8,64,2560]{2,1,0:T(8,128)(2,1)} %gather_fusion.1), calls=%async_computation.1 | async-start | bytes 5242880 | tf_op jit(solution)/shard_map/all_to_all | solution.py:301
  83.0 26.3 %collective-permute-start.2 = (bf16[2,256,1024]{2,1,0:T(8,128)(2,1)}, bf16[2,256,1024]{2,1,0:T(8,128)(2,1)}, u32[]{:S(2)}, u32[]{:S(2)}) collective-permute-start(bf16[2,256,1024]{2,1,0:T(8,128)(2,1)} %get-tuple-element.25), channel_id=1, source_target_pairs={{0,2},{1,3},{2,0},{3,1},{4,6},{5,7},{6,4},{7,5},{8,10},{9,11},{10,... | collective-permute-start | bytes 3145736 | tf_op jit(solution)/shard_map/ppermute | solution.py:279
  83.5 27.3 %collective-permute-start.1 = (bf16[2,256,1024]{2,1,0:T(8,128)(2,1)}, bf16[2,256,1024]{2,1,0:T(8,128)(2,1)S(1)}, u32[]{:S(2)}, u32[]{:S(2)}) collective-permute-start(bf16[2,256,1024]{2,1,0:T(8,128)(2,1)} %get-tuple-element.25), channel_id=1, source_target_pairs={{0,1},{1,0},{2,3},{3,2},{4,5},{5,4},{6,7},{7,6},{8,9},{9,8},{10,11... | collective-permute-start | bytes 3145736 | tf_op jit(solution)/shard_map/ppermute | solution.py:278
  86.3 34.7 %collective-permute-start.7 = (bf16[256,1024]{1,0:T(8,128)(2,1)S(1)}, bf16[256,1024]{1,0:T(8,128)(2,1)S(1)}, u32[]{:S(2)}, u32[]{:S(2)}) collective-permute-start(bf16[256,1024]{1,0:T(8,128)(2,1)S(1)} %get-tuple-element.31), channel_id=1, source_target_pairs={{0,1},{1,0},{2,3},{3,2},{4,5},{5,4},{6,7},{7,6},{8,9},{9,8},{10,11... | collective-permute-start | bytes 1572872 | tf_op jit(solution)/shard_map/ppermute | solution.py:278
  88.2 32.8 %collective-permute-start.6 = (bf16[256,1024]{1,0:T(8,128)(2,1)S(1)}, bf16[256,1024]{1,0:T(8,128)(2,1)S(1)}, u32[]{:S(2)}, u32[]{:S(2)}) collective-permute-start(bf16[256,1024]{1,0:T(8,128)(2,1)S(1)} %get-tuple-element.30), channel_id=1, source_target_pairs={{0,2},{1,3},{2,0},{3,1},{4,6},{5,7},{6,4},{7,5},{8,10},{9,11},{10,... | collective-permute-start | bytes 1572872 | tf_op jit(solution)/shard_map/ppermute | solution.py:279
  89.8 2.5 %copy-start.7 = (f32[2,256,2560]{2,1,0:T(8,128)S(1)}, f32[2,256,2560]{2,1,0:T(8,128)}, u32[]{:S(2)}) copy-start(f32[2,256,2560]{2,1,0:T(8,128)} %copy-done.6) | copy-start | bytes 15728644
  102.2 18.8 %copy-start.15 = (bf16[8,64,2048]{2,1,0:T(8,128)(2,1)S(1)}, bf16[8,64,2048]{2,1,0:T(8,128)(2,1)}, u32[]{:S(2)}) copy-start(bf16[8,64,2048]{2,1,0:T(8,128)(2,1)} %copy-done.14) | copy-start | bytes 6291460
  102.2 36.7 %collective-permute-start.13 = (bf16[256,1024]{1,0:T(8,128)(2,1)S(1)}, bf16[256,1024]{1,0:T(8,128)(2,1)S(1)}, u32[]{:S(2)}, u32[]{:S(2)}) collective-permute-start(bf16[256,1024]{1,0:T(8,128)(2,1)S(1)} %get-tuple-element.39), channel_id=1, source_target_pairs={{0,2},{1,3},{2,0},{3,1},{4,6},{5,7},{6,4},{7,5},{8,10},{9,11},{10,... | collective-permute-start | bytes 1572872 | tf_op jit(solution)/shard_map/ppermute | solution.py:279
  109.3 30.0 %collective-permute-start.14 = (bf16[256,1024]{1,0:T(8,128)(2,1)S(1)}, bf16[256,1024]{1,0:T(8,128)(2,1)S(1)}, u32[]{:S(2)}, u32[]{:S(2)}) collective-permute-start(bf16[256,1024]{1,0:T(8,128)(2,1)S(1)} %get-tuple-element.40), channel_id=1, source_target_pairs={{0,1},{1,0},{2,3},{3,2},{4,5},{5,4},{6,7},{7,6},{8,9},{9,8},{10,11... | collective-permute-start | bytes 1572872 | tf_op jit(solution)/shard_map/ppermute | solution.py:278
  110.8 10.2 %copy-start.3 = (bf16[256,8192]{1,0:T(8,128)(2,1)S(1)}, bf16[256,8192]{1,0:T(8,128)(2,1)}, u32[]{:S(2)}) copy-start(bf16[256,8192]{1,0:T(8,128)(2,1)} %refs_0_.7) | copy-start | bytes 12582916
  120.7 5.0 %copy-start.8 = (f32[2,256,2560]{2,1,0:T(8,128)}, f32[2,256,2560]{2,1,0:T(8,128)S(1)}, u32[]{:S(2)}) copy-start(f32[2,256,2560]{2,1,0:T(8,128)S(1)} %near_rows_rest.1.refs_1_) | copy-start | bytes 15728644
  125.7 7.9 %collective-permute-start.8 = (f32[128,128]{1,0:T(8,128)S(1)}, f32[128,128]{1,0:T(8,128)S(1)}, u32[]{:S(2)}, u32[]{:S(2)}) collective-permute-start(f32[128,128]{1,0:T(8,128)S(1)} %get-tuple-element.33), channel_id=1, source_target_pairs={{0,1},{1,0},{2,3},{3,2},{4,5},{5,4},{6,7},{7,6},{8,9},{9,8},{10,11... | collective-permute-start | bytes 196616 | tf_op jit(solution)/shard_map/ppermute | solution.py:278
  126.3 7.3 %collective-permute-start.9 = (f32[128,128]{1,0:T(8,128)S(1)}, f32[128,128]{1,0:T(8,128)S(1)}, u32[]{:S(2)}, u32[]{:S(2)}) collective-permute-start(f32[128,128]{1,0:T(8,128)S(1)} %get-tuple-element.34), channel_id=1, source_target_pairs={{0,2},{1,3},{2,0},{3,1},{4,6},{5,7},{6,4},{7,5},{8,10},{9,11},{10,... | collective-permute-start | bytes 196616 | tf_op jit(solution)/shard_map/ppermute | solution.py:279
  127.8 7.5 %collective-permute-start.10 = (f32[128,128]{1,0:T(8,128)S(1)}, f32[128,128]{1,0:T(8,128)S(1)}, u32[]{:S(2)}, u32[]{:S(2)}) collective-permute-start(f32[128,128]{1,0:T(8,128)S(1)} %get-tuple-element.35), channel_id=1, source_target_pairs={{0,3},{1,2},{2,1},{3,0},{4,7},{5,6},{6,5},{7,4},{8,11},{9,10},{10,... | collective-permute-start | bytes 196616 | tf_op jit(solution)/shard_map/ppermute | solution.py:280
  135.3 18.5 %collective-permute-start.17 = (bf16[128,128]{1,0:T(8,128)(2,1)S(1)}, bf16[128,128]{1,0:T(8,128)(2,1)S(1)}, u32[]{:S(2)}, u32[]{:S(2)}) collective-permute-start(bf16[128,128]{1,0:T(8,128)(2,1)S(1)} %add_convert_fusion.refs_2_), channel_id=1, source_target_pairs={{0,2},{1,3},{2,0},{3,1},{4,6},{5,7},{6,4},{7,5},{8,10},{9,11},{10,... | collective-permute-start | bytes 98312 | tf_op jit(solution)/shard_map/ppermute | solution.py:279
  135.8 18.0 %collective-permute-start.16 = (bf16[128,128]{1,0:T(8,128)(2,1)S(1)}, bf16[128,128]{1,0:T(8,128)(2,1)S(1)}, u32[]{:S(2)}, u32[]{:S(2)}) collective-permute-start(bf16[128,128]{1,0:T(8,128)(2,1)S(1)} %add_convert_fusion.refs_2_), channel_id=1, source_target_pairs={{0,1},{1,0},{2,3},{3,2},{4,5},{5,4},{6,7},{7,6},{8,9},{9,8},{10,11... | collective-permute-start | bytes 98312 | tf_op jit(solution)/shard_map/ppermute | solution.py:278
  137.3 25.4 %collective-permute-start.15 = (bf16[128,128]{1,0:T(8,128)(2,1)S(1)}, bf16[128,128]{1,0:T(8,128)(2,1)S(1)}, u32[]{:S(2)}, u32[]{:S(2)}) collective-permute-start(bf16[128,128]{1,0:T(8,128)(2,1)S(1)} %add_convert_fusion.refs_2_), channel_id=1, source_target_pairs={{0,3},{1,2},{2,1},{3,0},{4,7},{5,6},{6,5},{7,4},{8,11},{9,10},{10,... | collective-permute-start | bytes 98312 | tf_op jit(solution)/shard_map/ppermute | solution.py:280
  138.9 24.0 %collective-permute-start.11 = (bf16[2,256,1024]{2,1,0:T(8,128)(2,1)}, bf16[2,256,1024]{2,1,0:T(8,128)(2,1)}, u32[]{:S(2)}, u32[]{:S(2)}) collective-permute-start(bf16[2,256,1024]{2,1,0:T(8,128)(2,1)} %collective-permute-done.refs_0_.refs_1_), channel_id=1, source_target_pairs={{0,2},{1,3},{2,0},{3,1},{4,6},{5,7},{6,4},{7,5},{8,10},{9,11},{10,... | collective-permute-start | bytes 3145736 | tf_op jit(solution)/shard_map/ppermute | solution.py:279
  139.3 23.7 %collective-permute-start.12 = (bf16[2,256,1024]{2,1,0:T(8,128)(2,1)}, bf16[2,256,1024]{2,1,0:T(8,128)(2,1)}, u32[]{:S(2)}, u32[]{:S(2)}) collective-permute-start(bf16[2,256,1024]{2,1,0:T(8,128)(2,1)} %collective-permute-done.2.refs_1_.refs_4_), channel_id=1, source_target_pairs={{0,1},{1,0},{2,3},{3,2},{4,5},{5,4},{6,7},{7,6},{8,9},{9,8},{10,11... | collective-permute-start | bytes 3145736 | tf_op jit(solution)/shard_map/ppermute | solution.py:278
  152.3 1.5 copy-start.12
  153.8 2.5 %copy-start.9 = (f32[2,256,2560]{2,1,0:T(8,128)S(1)}, f32[2,256,2560]{2,1,0:T(8,128)}, u32[]{:S(2)}) copy-start(f32[2,256,2560]{2,1,0:T(8,128)} %copy-done.8) | copy-start | bytes 15728644
  156.3 1.7 copy-start.11
  158.0 4.7 %copy-start.4 = (bf16[8,64,2560]{2,1,0:T(8,128)(2,1)}, bf16[8,64,2560]{2,1,0:T(8,128)(2,1)S(1)}, u32[]{:S(2)}) copy-start(bf16[8,64,2560]{2,1,0:T(8,128)(2,1)S(1)} %all-to-all-done.1.refs_5_.refs_6_.refs_8_.refs_9_) | copy-start | bytes 7864324
  158.0 5.0 %copy-start.13 = (f32[1,256,2560]{2,1,0:T(8,128)S(1)}, f32[1,256,2560]{2,1,0:T(8,128)}, u32[]{:S(2)}) copy-start(f32[1,256,2560]{2,1,0:T(8,128)} %copy-done.12) | copy-start | bytes 7864324
  163.1 1.7 copy-start.5
  164.8 13.1 %copy-start.1 = (bf16[4,64,2560]{2,1,0:T(8,128)(2,1)S(1)}, bf16[4,64,2560]{2,1,0:T(8,128)(2,1)}, u32[]{:S(2)}) copy-start(bf16[4,64,2560]{2,1,0:T(8,128)(2,1)} %param.9) | copy-start | bytes 3932164

commit v4 on v3

--- a/solution.py
+++ b/solution.py
@@ -10,6 +10,7 @@
 BLOCK = 128
 MIB = 1 << 20
 PANELS_AT = 4
+VMEM_BYTES = 32 * MIB
 
 adapter_scale = 0.5
 
@@ -43,32 +44,6 @@
     if at is None:
         return ref[...]
     return ref[:, at[0] : at[1]] if isinstance(at, tuple) else ref[at]
-
-
-def cut_kernel(columns_ref, *refs):
-    stacks = len(refs) // 2
-    for source, out in zip(refs[:stacks], refs[stacks:]):
-        out[0] = source[...]
-
-
-def cut_stacks(tokens, columns, stacks):
-    rows, width = tokens.shape
-    count, part = columns.shape[0] // stacks, width // 8
-    return pl.pallas_call(
-        cut_kernel,
-        grid_spec=pltpu.PrefetchScalarGridSpec(
-            num_scalar_prefetch=1,
-            grid=(count,),
-            in_specs=[
-                pl.BlockSpec((rows, part), lambda i, columns, first=stack * count: (0, columns[first + i]))
-                for stack in range(stacks)
-            ],
-            out_specs=[pl.BlockSpec((1, rows, part), lambda i, columns: (i, 0, 0))] * stacks,
-        ),
-        out_shape=[jax.ShapeDtypeStruct((count, rows, part), tokens.dtype)] * stacks,
-        cost_estimate=cost(0, 4 * stacks * count * rows * part),
-        name="cut_stacks",
-    )(columns, *[tokens] * stacks)
 
 
 def project_kernel(sets, weights_at, totals_at, update, plan_ref, *refs):
@@ -101,25 +76,23 @@
 
 def project(sets, weight, tile, plan, rows, total=None, update=None, into=None, weigh=2, name=None):
     columns = weight.shape[1]
-    known, halves, flat = Arrays(), [], []
+    known, spans, flat = Arrays(), [], []
     for terms in sets:
         flat.append([])
-        for array, at, k, half in terms:
-            if (k, half) not in halves:
-                halves.append((k, half))
-            flat[-1].append((known.place(array), at, halves.index((k, half))))
+        for array, at, k, span in terms:
+            if (k, span) not in spans:
+                spans.append((k, span))
+            flat[-1].append((known.place(array), at, spans.index((k, span))))
     depth = weight.shape[0] // 4
     operands = list(known.arrays)
     in_specs = [whole_spec(a) for a in operands]
     weights_at = len(operands)
-    for k, half in halves:
+    for k, span in spans:
         if k is None:
-            in_specs.append(pl.BlockSpec((depth, tile), lambda n, plan, half=half: (half, n)))
-        elif half is None:
-            in_specs.append(pl.BlockSpec((depth, tile), lambda n, plan, k=k: (plan[k], n)))
+            in_specs.append(pl.BlockSpec((depth, tile), lambda n, plan, span=span: (span, n)))
         else:
             in_specs.append(
-                pl.BlockSpec((depth // 2, tile), lambda n, plan, k=k, half=half: (plan[k] * 2 + half, n))
+                pl.BlockSpec((depth * span, tile), lambda n, plan, k=k, span=span: (plan[k] // span, n))
             )
         operands.append(weight)
     totals_at = []
@@ -150,8 +123,8 @@
         in_specs.append(pl.BlockSpec(memory_space=pl.ANY))
         operands.append(into)
         aliases = {len(operands): 0}
-    products = sum(2 if half is None or k is None else 1 for terms in sets for _, _, k, half in terms)
-    products *= rows * depth // 2
+    products = sum(1 if k is None else span for terms in sets for _, _, k, span in terms)
+    products *= rows * depth
     moved = 2 * products // rows * columns + 4 * len(sets) * rows * columns * (1 if total is None else 2)
     return pl.pallas_call(
         functools.partial(project_kernel, flat, weights_at, totals_at, updating),
@@ -163,8 +136,8 @@
         ),
         out_shape=out_shape,
         input_output_aliases=aliases,
-        cost_estimate=cost(weigh * 2 * products * columns, weigh * moved),
-        compiler_params=pltpu.CompilerParams(vmem_limit_bytes=32 * MIB),
+        cost_estimate=cost(int(weigh * 2 * products * columns), int(weigh * moved)),
+        compiler_params=pltpu.CompilerParams(vmem_limit_bytes=VMEM_BYTES),
         name=name,
     )(plan, *operands)
 
@@ -215,7 +188,7 @@
         ),
         out_shape=jax.ShapeDtypeStruct((row_total, columns), jnp.bfloat16),
         cost_estimate=cost(12 * rows * rank * columns, 18 * rows * columns),
-        compiler_params=pltpu.CompilerParams(vmem_limit_bytes=32 * MIB),
+        compiler_params=pltpu.CompilerParams(vmem_limit_bytes=VMEM_BYTES),
         name="finish_rows",
     )(plan, own, near, *shrinks, panels, panels)
 
@@ -260,7 +233,7 @@
         ),
         out_shape=[jax.ShapeDtypeStruct(shape, jnp.float32)] * len(flat),
         cost_estimate=cost(8 * len(flat) * rows * depth * rank, 2 * (panels.size + len(flat) * rows * depth)),
-        compiler_params=pltpu.CompilerParams(vmem_limit_bytes=32 * MIB),
+        compiler_params=pltpu.CompilerParams(vmem_limit_bytes=VMEM_BYTES),
         name="shrink_parts",
     )(plan, *operands)
 
@@ -274,25 +247,27 @@
     member = lax.axis_index("tp")
     rows, width = tokens.shape
     blocks = rows // BLOCK
-    depth, half = width // 4, width // 8
+    depth = width // 4
     to_x = lambda v: lax.ppermute(v, "tp", [(i, i ^ 1) for i in range(4)])
     to_y = lambda v: lax.ppermute(v, "tp", [(i, i ^ 2) for i in range(4)])
     across = lambda v: lax.ppermute(v, "tp", [(i, i ^ 3) for i in range(4)])
-    first, second = (0, half), (half, depth)
 
     members = member ^ jnp.arange(4, dtype=jnp.int32)
     mine = lax.dynamic_slice_in_dim(owners, group * 4 * blocks, 4 * blocks).reshape(4, blocks)
     mine = jnp.sum(jnp.where((members[:, None] == jnp.arange(4))[:, :, None], mine[None], 0), axis=1)
     plan = jnp.concatenate([members, mine.reshape(-1)]).astype(jnp.int32)
 
-    def eighths(*places):
-        return jnp.stack([(member ^ 3 ^ j) * 2 + second for j, second in places]).astype(jnp.int32)
-
-    (s03,) = cut_stacks(tokens, eighths((0, 0), (0, 1), (3, 0), (3, 1)), 1)
-    x03, y03 = to_x(s03), to_y(s03)
-    a12, b12 = cut_stacks(tokens, eighths((1, 0), (2, 0), (1, 1), (2, 1)), 2)
-    xa12, ya12 = to_x(a12), to_y(a12)
-    xb12, yb12 = to_x(b12), to_y(b12)
+    def part(array, start, size):
+        return lax.dynamic_slice(array, (0, start), (rows, size))
+
+    def cut(j, *others):
+        return part(tokens, after((member ^ 3 ^ j) * depth, *others), depth)
+
+    s0, s3 = cut(0), cut(3)
+    x0, y3 = to_x(s0), to_y(s3)
+    s1, s2 = cut(1, s0, s3), cut(2, s0, s3)
+    x1, y2 = to_x(s1), to_y(s2)
+    x2, y1 = to_x(after(s2, x0, y3)), to_y(after(s1, x0, y3))
 
     def chosen(panels, select):
         return jnp.take(panels, select, axis=0, mode="clip")
@@ -300,7 +275,7 @@
     def exchange(panels):
         return lax.all_to_all(panels, "grp", split_axis=0, concat_axis=0, tiled=True)
 
-    down_out = chosen(down_weight, after(select_slot, a12, b12))
+    down_out = chosen(down_weight, after(select_slot, s1, s2))
     down = exchange(down_out)
 
     own = project(
@@ -309,54 +284,36 @@
     )
 
     tile = tile_of(frozen_weight.shape[1], 512)
+
+    d0, d3 = to_y(after(x0, x1, y2)), to_x(after(y3, x1, y2))
     near = project(
-        [
-            [(x03, 0, 2, 0), (x03, 1, 2, 1), (x03, 2, 1, 0), (x03, 3, 1, 1)],
-            [(y03, 2, 2, 0), (y03, 3, 2, 1), (y03, 0, 1, 0), (y03, 1, 1, 1)],
-        ],
+        [[(x0, None, 2, 1), (x1, None, 3, 1)], [(y3, None, 2, 1), (y2, None, 3, 1)]],
         frozen_weight, tile, after(plan, own), rows, weigh=6, name="near_rows",
     )
     up = exchange(chosen(up_weight, after(select_slot, down, near)))
+    x3, y0 = to_x(after(s3, x2, y1)), to_y(after(s0, x2, y1))
     near = project(
-        [
-            [(xa12, 0, 3, 0), (xa12, 1, 0, 0)],
-            [(ya12, 1, 3, 0), (ya12, 0, 0, 0)],
-        ],
-        frozen_weight, tile, plan, rows, total=near, weigh=2, name="near_rows_more",
-    )
-
-    da0, db0 = to_y(after(x03[0], xa12, ya12)), to_x(after(y03[1], xa12, ya12))
-    da3, db3 = to_y(after(x03[2], near)), to_x(after(y03[3], near))
-    near = project(
-        [
-            [(xb12, 0, 3, 1), (xb12, 1, 0, 1)],
-            [(yb12, 1, 3, 1), (yb12, 0, 0, 1)],
-        ],
-        frozen_weight, tile, plan, rows, total=near, name="near_rows_rest",
-    )
-
-    share = shrink_parts(
-        tokens,
-        [
-            [(xa12, 1, 0), (xb12, 1, half)],
-            [(ya12, 0, 0), (yb12, 0, half)],
-            [(da0, None, 0), (db0, None, half)],
-        ],
-        down,
-        after(plan, near),
-    )
+        [[(x2, None, 0, 1)], [(y1, None, 0, 1)]],
+        frozen_weight, tile, plan, rows, total=near, weigh=0, name="near_rows_more",
+    )
+
+    share = shrink_parts(tokens, [[(x2, None, 0)], [(y1, None, 0)], [(d0, None, 0)]], down, after(plan, near, d3))
     home = share[0] + to_x(share[1]) + to_y(share[2]) + across(share[3])
     home = home.astype(jnp.bfloat16)
     shrinks = [home, to_x(home), to_y(home), across(home)]
-    da12, db12 = to_y(after(xa12, home)), to_x(after(yb12, home))
+    d1, d2 = to_y(after(x1, home)), to_x(after(y2, home))
 
     far = project(
-        [[(da0, None, 0, 0), (db0, None, 0, 1), (da3, None, 3, 0), (db3, None, 3, 1)]],
-        frozen_weight, tile_of(frozen_weight.shape[1], 640), after(plan, home), rows, name="far_rows",
-    )
-    out = finish(own, near, shrinks[:3], up, after(plan, far), 4 * rows)
+        [[(d0, None, 0, 1), (d3, None, 3, 1)]],
+        frozen_weight, tile_of(frozen_weight.shape[1], 640), after(plan, share[0]), rows, weigh=4, name="far_rows",
+    )
+    near = project(
+        [[(x3, None, 1, 1)], [(y0, None, 1, 1)]],
+        frozen_weight, tile, after(plan, home, far), rows, total=near, weigh=4, name="near_rows_rest",
+    )
+    out = finish(own, near, shrinks[:3], up, plan, 4 * rows)
     return project(
-        [[(da12, 0, 1, 0), (db12, 0, 1, 1), (da12, 1, 2, 0), (db12, 1, 2, 1)]],
+        [[(d1, None, 1, 1), (d2, None, 2, 1)]],
         frozen_weight, tile_of(frozen_weight.shape[1], 640), plan, rows,
         total=far, update=(3, shrinks[3], up), into=out, name="last_rows",
     )

time: 179 us -> 169 us (0.944)
  waiting for transfers between devices: 25.5 us -> 15 us
  Pallas kernels: 96.5 us -> 87.7 us
  local copies, waits for them, and re-layouts: 23.4 us -> 31.7 us
  starting transfers between devices: 30.5 us -> 32.9 us
    ppermute x8, waiting for transfers between devices: 17 us -> 6.82 us  [square(): to_y = lambda v: lax.ppermute(v, 'tp', [(i, i ^ 2) for i in range(4)])]
    dynamic_slice x0 -> x2, local copies, waits for them, and re-layouts: none -> 8.54 us  [part(): return lax.dynamic_slice(array, (0, start), (rows, size))]
    pallas_call x2 -> x0, Pallas kernels: 7.87 us -> none  [cut_stacks(): pl.pallas_call(cut_kernel, grid_spec=pltpu.PrefetchScalarGridSpec(num_sca...]
    ppermute x8, starting transfers between devices: 8.62 us -> 11.3 us  [square(): to_y = lambda v: lax.ppermute(v, 'tp', [(i, i ^ 2) for i in range(4)])]
    squeeze x2 -> x0, local copies, waits for them, and re-layouts: 2.54 us -> none  [square(): da3, db3 = (to_y(after(x03[2], near)), to_x(after(y03[3], near)))]
    unnamed x38, local copies, waits for them, and re-layouts: 16 us -> 18.4 us
  transfers between devices with their start and end apart: 20 -> 20, of which waited for: 8 -> 7; matrix products, arithmetic and copies ran while one was open for 5% -> 6% of each run, Pallas kernels for 44% -> 44%
where the time goes in v4:
time: 169 us; the launch traced here: 168 us
  Pallas kernels  87.7 us (52%)
  starting transfers between devices  32.9 us (19%)
  local copies, waits for them, and re-layouts  31.7 us (19%)
  waiting for transfers between devices  15 us (9%)
    pallas_call x6, Pallas kernels, project(): pl.pallas_call(functools.partial(project_kernel, flat, weights_at, totals...  79.3 us
    unnamed x38, local copies, waits for them, and re-layouts  18.4 us
    ppermute x8, starting transfers between devices, square(): to_y = lambda v: lax.ppermute(v, 'tp', [(i, i ^ 2) for i in range(4)])  11.3 us
    all_to_all x2, starting transfers between devices, exchange(): lax.all_to_all(panels, 'grp', split_axis=0, concat_axis=0, tiled=True)  10.2 us
    ppermute x8, starting transfers between devices, square(): to_x = lambda v: lax.ppermute(v, 'tp', [(i, i ^ 1) for i in range(4)])  9.64 us
    dynamic_slice x2, local copies, waits for them, and re-layouts, part(): return lax.dynamic_slice(array, (0, start), (rows, size))  8.54 us
    ppermute x8, waiting for transfers between devices, square(): to_x = lambda v: lax.ppermute(v, 'tp', [(i, i ^ 1) for i in range(4)])  6.84 us
    ppermute x8, waiting for transfers between devices, square(): to_y = lambda v: lax.ppermute(v, 'tp', [(i, i ^ 2) for i in range(4)])  6.82 us
  transfers between devices with their start and end apart: 20, of which 7 were waited for; matrix products, arithmetic and copies ran while one was open for 6% of the time, Pallas kernels for 44%

profile of v4, /device:TPU:0, one launch (start us, length us, event | category | flops | bytes accessed | tf_op | source)
XLA Modules:
  0.0 168.1 jit_solution(4242252288217502537)
XLA Ops:
  0.0 4.3 %constant_dynamic-slice_fusion.2 = (bf16[256,2048]{1,0:T(8,128)(2,1)}, bf16[256,2048]{1,0:T(8,128)(2,1)}) fusion(bf16[256,8192]{1,0:T(8,128)(2,1)} %refs_0_.3, s32[]{:T(128)S(6)} %select_n.48, s32[]{:T(128)S(6)} %select_n.47), kind=kLoop, calls=%fused_computation.26 | loop fusion | bytes 4194312 | tf_op jit(solution)/shard_map/dynamic_slice | solution.py:261
  4.3 3.1 %collective-permute-start.2 = (bf16[256,2048]{1,0:T(8,128)(2,1)}, bf16[256,2048]{1,0:T(8,128)(2,1)}, u32[]{:S(2)}, u32[]{:S(2)}) collective-permute-start(bf16[256,2048]{1,0:T(8,128)(2,1)} %get-tuple-element.45), channel_id=1, source_target_pairs={{0,2},{1,3},{2,0},{3,1},{4,6},{5,7},{6,4},{7,5},{8,10},{9,11},{10,... | collective-permute-start | bytes 3145736 | tf_op jit(solution)/shard_map/ppermute | solution.py:252
  7.3 1.5 collective-permute-start.1
  8.8 4.3 %constant_dynamic-slice_fusion = (bf16[256,2048]{1,0:T(8,128)(2,1)}, bf16[256,2048]{1,0:T(8,128)(2,1)}) fusion(bf16[256,8192]{1,0:T(8,128)(2,1)} %refs_0_.3, s32[]{:T(128)S(6)} %select_n.50, s32[]{:T(128)S(6)} %select_n.49), kind=kLoop, calls=%fused_computation.24 | loop fusion | bytes 4194312 | tf_op jit(solution)/shard_map/dynamic_slice | solution.py:261
  13.1 0.5 collective-permute-start.5
  14.0 2.0 %gather_fusion = bf16[8,64,2048]{2,1,0:T(8,128)(2,1)} fusion(bf16[4,64,2048]{2,1,0:T(8,128)(2,1)S(1)} %copy-done.16, s32[1024]{0:T(1024)S(1)} %pad_clamp_fusion.1), kind=kCustom, calls=%fused_computation | custom fusion | bytes 4194336 | tf_op jit(solution)/shard_map/jit(_take)/gather | solution.py:273
  16.0 5.3 %all-to-all-start = ((bf16[8,64,2048]{2,1,0:T(8,128)(2,1)}), bf16[8,64,2048]{2,1,0:T(8,128)(2,1)S(1)}, u32[]{:S(2)}, u32[]{:S(2)}) async-start(bf16[8,64,2048]{2,1,0:T(8,128)(2,1)} %gather_fusion), calls=%async_computation | async-start | bytes 4194304 | tf_op jit(solution)/shard_map/all_to_all | solution.py:276
  21.7 0.1 select_reduce_fusion.1
  22.1 2.2 %copy-done.4 = bf16[256,8192]{1,0:T(8,128)(2,1)S(1)} copy-done((bf16[256,8192]{1,0:T(8,128)(2,1)S(1)}, bf16[256,8192]{1,0:T(8,128)(2,1)}, u32[]{:S(2)}) %copy-start.4) | copy-done | bytes 4194328
  24.3 18.5 %own_rows.1.refs_0_ = f32[1,256,2560]{2,1,0:T(8,128)S(1)} custom-call(s32[12]{0:T(128)S(1)} %pad_add_fusion.plan_ref, bf16[256,8192]{1,0:T(8,128)(2,1)S(1)} %copy-done.4, bf16[8192,2560]{1,0:T(8,128)(2,1)} %refs_3_.5, bf16[8192,2560]{1,0:T(8,128)(2,1)} %refs_3_.5, bf16[8192,2560]{1,0:T(8,128)(2,1)} %refs_3_.5, bf16[8192,2560]{1,0:T(8,128)(2,1)} %refs_3_.5), custom_call_target="tpu_custom_call" | custom-call | tf_op jit(solution)/shard_map/own_rows/pallas_call | solution.py:129
  42.8 1.5 copy-done.10
  44.3 1.5 collective-permute-start.4
  45.8 1.5 collective-permute-start.3
  47.3 6.8 %collective-permute-done.5.refs_3_ = bf16[256,2048]{1,0:T(8,128)(2,1)} collective-permute-done((bf16[256,2048]{1,0:T(8,128)(2,1)}, bf16[256,2048]{1,0:T(8,128)(2,1)}, u32[]{:S(2)}, u32[]{:S(2)}) %collective-permute-start.5) | collective-permute-done | bytes 1048608 | tf_op jit(solution)/shard_map/ppermute | solution.py:252
  54.1 2.1 %collective-permute-done.refs_1_ = bf16[256,2048]{1,0:T(8,128)(2,1)} collective-permute-done((bf16[256,2048]{1,0:T(8,128)(2,1)}, bf16[256,2048]{1,0:T(8,128)(2,1)}, u32[]{:S(2)}, u32[]{:S(2)}) %collective-permute-start) | collective-permute-done | bytes 1048608 | tf_op jit(solution)/shard_map/ppermute | solution.py:251
  56.2 1.5 collective-permute-start.6
  57.7 0.5 collective-permute-start.7
  58.2 16.1 %near_rows.1.refs_3_.refs_4_ = f32[2,256,2560]{2,1,0:T(8,128)S(1)} custom-call(s32[12]{0:T(128)S(1)} %pad_add_fusion.plan_ref, bf16[256,2048]{1,0:T(8,128)(2,1)} %collective-permute-done.1.refs_0_, bf16[256,2048]{1,0:T(8,128)(2,1)} %collective-permute-done.refs_1_, bf16[256,2048]{1,0:T(8,128)(2,1)} %collective-permute-done.2.refs_2_, ...), custom_call_target="tpu_custom_call" | custom-call | flops 64424509440 | bytes 283115520 | tf_op jit(solution)/shard_map/near_rows/pallas_call | solution.py:129
  74.3 2.3 %copy-done.6 = f32[2,256,2560]{2,1,0:T(8,128)} copy-done((f32[2,256,2560]{2,1,0:T(8,128)}, f32[2,256,2560]{2,1,0:T(8,128)S(1)}, u32[]{:S(2)}) %copy-start.6) | copy-done | bytes 5242904
  76.7 2.2 %gather_fusion.1 = bf16[8,64,2560]{2,1,0:T(8,128)(2,1)} fusion(bf16[4,64,2560]{2,1,0:T(8,128)(2,1)S(1)} %copy-done, s32[1024]{0:T(1024)S(1)} %pad_clamp_fusion), kind=kCustom, calls=%fused_computation.1 | custom fusion | bytes 5242912 | tf_op jit(solution)/shard_map/jit(_take)/gather | solution.py:273
  78.9 4.9 %all-to-all-start.1 = ((bf16[8,64,2560]{2,1,0:T(8,128)(2,1)}), bf16[8,64,2560]{2,1,0:T(8,128)(2,1)S(1)}, u32[]{:S(2)}, u32[]{:S(2)}) async-start(bf16[8,64,2560]{2,1,0:T(8,128)(2,1)} %gather_fusion.1), calls=%async_computation.1 | async-start | bytes 5242880 | tf_op jit(solution)/shard_map/all_to_all | solution.py:276
  83.8 0.6 collective-permute-start.14
  84.4 1.8 %collective-permute-start.15 = (bf16[256,2048]{1,0:T(8,128)(2,1)}, bf16[256,2048]{1,0:T(8,128)(2,1)S(1)}, u32[]{:S(2)}, u32[]{:S(2)}) collective-permute-start(bf16[256,2048]{1,0:T(8,128)(2,1)} %get-tuple-element.46), channel_id=1, source_target_pairs={{0,2},{1,3},{2,0},{3,1},{4,6},{5,7},{6,4},{7,5},{8,10},{9,11},{10,... | collective-permute-start | bytes 3145736 | tf_op jit(solution)/shard_map/ppermute | solution.py:252
  86.1 2.5 %copy-done.7 = f32[2,256,2560]{2,1,0:T(8,128)S(1)} copy-done((f32[2,256,2560]{2,1,0:T(8,128)S(1)}, f32[2,256,2560]{2,1,0:T(8,128)}, u32[]{:S(2)}) %copy-start.7) | copy-done | bytes 5242904
  88.6 10.2 %near_rows_more.1.refs_3_.refs_4_ = f32[2,256,2560]{2,1,0:T(8,128)S(1)} custom-call(s32[12]{0:T(128)S(1)} %pad_add_fusion.plan_ref, bf16[256,2048]{1,0:T(8,128)(2,1)} %collective-permute-done.3.refs_0_.refs_1_, bf16[256,2048]{1,0:T(8,128)(2,1)} %collective-permute-done.4.refs_1_.refs_2_, bf16[8192,2560]{1,0:T(8,128)(2,1)} %refs_3_.5, ...), custom_call_target="tpu_custom_call" | custom-call | tf_op jit(solution)/shard_map/near_rows_more/pallas_call | solution.py:129
  98.8 2.3 %collective-permute-done.6.refs_1_ = bf16[256,2048]{1,0:T(8,128)(2,1)} collective-permute-done((bf16[256,2048]{1,0:T(8,128)(2,1)}, bf16[256,2048]{1,0:T(8,128)(2,1)}, u32[]{:S(2)}, u32[]{:S(2)}) %collective-permute-start.6) | collective-permute-done | bytes 1048608 | tf_op jit(solution)/shard_map/ppermute | solution.py:251
  101.2 3.7 %shrink_parts.1 = (f32[128,128]{1,0:T(8,128)S(1)}, f32[128,128]{1,0:T(8,128)S(1)}, f32[128,128]{1,0:T(8,128)S(1)}, f32[128,128]{1,0:T(8,128)S(1)}) custom-call(s32[12]{0:T(128)S(1)} %pad_add_fusion.plan_ref, bf16[256,8192]{1,0:T(8,128)(2,1)S(1)} %copy-done.5, bf16[256,2048]{1,0:T(8,128)(2,1)} %collective-permute-done.3.refs_0_.refs_1_, ...), custom_call_target="tpu_custom_call" | custom-call | flops 1073741824 | bytes 6291456 | tf_op jit(solution)/shard_map/shrink_parts/pallas_call | solution.py:226
  104.9 1.5 collective-permute-start.8
  106.4 0.5 collective-permute-start.9
  106.9 1.5 collective-permute-start.10
  108.4 12.0 %far_rows.1.refs_4_ = f32[1,256,2560]{2,1,0:T(8,128)S(1)} custom-call(s32[12]{0:T(128)S(1)} %pad_add_fusion.plan_ref, bf16[256,2048]{1,0:T(8,128)(2,1)} %collective-permute-done.7.refs_3_.refs_0_, bf16[256,2048]{1,0:T(8,128)(2,1)} %collective-permute-done.6.refs_1_, bf16[8192,2560]{1,0:T(8,128)(2,1)} %refs_3_.5, bf16[8192,2560]{1,0:T(8,128)(2,1)} %refs_3_.5), custom_call_target="tpu_custom_call" | custom-call | flops 21474836480 | bytes 94371840 | tf_op jit(solution)/shard_map/far_rows/pallas_call | solution.py:129
  120.4 1.5 copy-done.8
  121.9 2.2 %collective-permute-done.8 = f32[128,128]{1,0:T(8,128)S(1)} collective-permute-done((f32[128,128]{1,0:T(8,128)S(1)}, f32[128,128]{1,0:T(8,128)S(1)}, u32[]{:S(2)}, u32[]{:S(2)}) %collective-permute-start.8) | collective-permute-done | bytes 65568 | tf_op jit(solution)/shard_map/ppermute | solution.py:251
  124.2 0.5 collective-permute-done.10
  124.7 1.7 %collective-permute-start.17 = (bf16[128,128]{1,0:T(8,128)(2,1)S(1)}, bf16[128,128]{1,0:T(8,128)(2,1)S(1)}, u32[]{:S(2)}, u32[]{:S(2)}) collective-permute-start(bf16[128,128]{1,0:T(8,128)(2,1)S(1)} %add_convert_fusion.refs_2_), channel_id=1, source_target_pairs={{0,2},{1,3},{2,0},{3,1},{4,6},{5,7},{6,4},{7,5},{8,10},{9,11},{10,... | collective-permute-start | bytes 98312 | tf_op jit(solution)/shard_map/ppermute | solution.py:252
  126.4 1.5 collective-permute-start.16
  127.9 0.3 collective-permute-start.13
  128.2 1.7 collective-permute-start.11
  129.9 1.5 collective-permute-start.12
  131.4 9.5 %near_rows_rest.1.refs_1_ = f32[2,256,2560]{2,1,0:T(8,128)S(1)} custom-call(s32[12]{0:T(128)S(1)} %pad_add_fusion.plan_ref, bf16[256,2048]{1,0:T(8,128)(2,1)S(1)} %collective-permute-done.14.refs_0_, bf16[256,2048]{1,0:T(8,128)(2,1)S(1)} %collective-permute-done.15.refs_1_, bf16[8192,2560]{1,0:T(8,128)(2,1)} %refs_3_.5, ...), custom_call_target="tpu_custom_call" | custom-call | flops 21474836480 | bytes 125829120 | tf_op jit(solution)/shard_map/near_rows_rest/pallas_call | solution.py:129
  140.9 2.3 %copy-done.14 = f32[2,256,2560]{2,1,0:T(8,128)} copy-done((f32[2,256,2560]{2,1,0:T(8,128)}, f32[2,256,2560]{2,1,0:T(8,128)S(1)}, u32[]{:S(2)}) %copy-start.14) | copy-done | bytes 5242904
  143.2 0.8 all-to-all-done.1.refs_5_.refs_6_.refs_7_
  144.1 1.7 %copy-done.11 = f32[1,256,2560]{2,1,0:T(8,128)S(1)} copy-done((f32[1,256,2560]{2,1,0:T(8,128)S(1)}, f32[1,256,2560]{2,1,0:T(8,128)}, u32[]{:S(2)}) %copy-start.11) | copy-done | bytes 2621464
  145.8 2.5 %copy-done.15 = f32[2,256,2560]{2,1,0:T(8,128)S(1)} copy-done((f32[2,256,2560]{2,1,0:T(8,128)S(1)}, f32[2,256,2560]{2,1,0:T(8,128)}, u32[]{:S(2)}) %copy-start.15) | copy-done | bytes 5242904
  148.3 4.7 %finish_rows.1.refs_8_ = bf16[1024,2560]{1,0:T(8,128)(2,1)} custom-call(s32[12]{0:T(128)S(1)} %pad_add_fusion.plan_ref, f32[1,256,2560]{2,1,0:T(8,128)S(1)} %copy-done.11, f32[2,256,2560]{2,1,0:T(8,128)S(1)} %copy-done.15, bf16[128,128]{1,0:T(8,128)(2,1)S(1)} %add_convert_fusion.refs_2_, bf16[128,128]{1,0:T(8,128)(2,1)S(1)} %collective-permute-done.16.refs_3_, ...), custom_call_target="tpu_custom_call" | custom-call | flops 503316480 | bytes 11796480 | tf_op jit(solution)/shard_map/finish_rows/pallas_call | solution.py:171
  153.0 0.2 collective-permute-done.12.refs_1_
  153.3 1.7 %copy-done.3 = bf16[8,64,2560]{2,1,0:T(8,128)(2,1)S(1)} copy-done((bf16[8,64,2560]{2,1,0:T(8,128)(2,1)S(1)}, bf16[8,64,2560]{2,1,0:T(8,128)(2,1)}, u32[]{:S(2)}) %copy-start.3) | copy-done | bytes 2621464
  155.0 13.1 %last_rows.1 = bf16[1024,2560]{1,0:T(8,128)(2,1)} custom-call(s32[12]{0:T(128)S(1)} %pad_add_fusion.plan_ref, bf16[256,2048]{1,0:T(8,128)(2,1)} %collective-permute-done.11.refs_0_, bf16[256,2048]{1,0:T(8,128)(2,1)} %collective-permute-done.12.refs_1_, bf16[8192,2560]{1,0:T(8,128)(2,1)} %refs_3_.5, ...), custom_call_target="tpu_custom_call", output_to_operand_aliasing={{}: (9, {})} | custom-call | flops 10737418240 | bytes 52428800 | tf_op jit(solution)/shard_map/last_rows/pallas_call | solution.py:129
  (58 shorter events, 1.1 us)
Async XLA Ops:
  0.0 76.7 %copy-start = (bf16[4,64,2560]{2,1,0:T(8,128)(2,1)S(1)}, bf16[4,64,2560]{2,1,0:T(8,128)(2,1)}, u32[]{:S(2)}) copy-start(bf16[4,64,2560]{2,1,0:T(8,128)(2,1)} %param.9) | copy-start | bytes 3932164
  4.3 9.5 %copy-start.17 = (s32[32]{0:T(128)S(1)}, s32[32]{0:T(128)}, u32[]{:S(2)}) copy-start(s32[32]{0:T(128)} %param.10) | copy-start | bytes 388
  4.3 9.5 %copy-start.18 = (s32[64]{0:T(128)S(1)}, s32[64]{0:T(128)}, u32[]{:S(2)}) copy-start(s32[64]{0:T(128)} %param.11) | copy-start | bytes 772
  4.3 9.8 %copy-start.16 = (bf16[4,64,2048]{2,1,0:T(8,128)(2,1)S(1)}, bf16[4,64,2048]{2,1,0:T(8,128)(2,1)}, u32[]{:S(2)}) copy-start(bf16[4,64,2048]{2,1,0:T(8,128)(2,1)} %param.8) | copy-start | bytes 3145732
  4.3 40.0 %collective-permute-start.2 = (bf16[256,2048]{1,0:T(8,128)(2,1)}, bf16[256,2048]{1,0:T(8,128)(2,1)}, u32[]{:S(2)}, u32[]{:S(2)}) collective-permute-start(bf16[256,2048]{1,0:T(8,128)(2,1)} %get-tuple-element.45), channel_id=1, source_target_pairs={{0,2},{1,3},{2,0},{3,1},{4,6},{5,7},{6,4},{7,5},{8,10},{9,11},{10,... | collective-permute-start | bytes 3145736 | tf_op jit(solution)/shard_map/ppermute | solution.py:252
  7.3 37.0 %collective-permute-start.1 = (bf16[256,2048]{1,0:T(8,128)(2,1)}, bf16[256,2048]{1,0:T(8,128)(2,1)}, u32[]{:S(2)}, u32[]{:S(2)}) collective-permute-start(bf16[256,2048]{1,0:T(8,128)(2,1)} %get-tuple-element.46), channel_id=1, source_target_pairs={{0,1},{1,0},{2,3},{3,2},{4,5},{5,4},{6,7},{7,6},{8,9},{9,8},{10,11... | collective-permute-start | bytes 3145736 | tf_op jit(solution)/shard_map/ppermute | solution.py:251
  13.1 41.0 %collective-permute-start.5 = (bf16[256,2048]{1,0:T(8,128)(2,1)}, bf16[256,2048]{1,0:T(8,128)(2,1)}, u32[]{:S(2)}, u32[]{:S(2)}) collective-permute-start(bf16[256,2048]{1,0:T(8,128)(2,1)} %get-tuple-element.28), channel_id=1, source_target_pairs={{0,2},{1,3},{2,0},{3,1},{4,6},{5,7},{6,4},{7,5},{8,10},{9,11},{10,... | collective-permute-start | bytes 3145736 | tf_op jit(solution)/shard_map/ppermute | solution.py:252
  13.6 42.6 %collective-permute-start = (bf16[256,2048]{1,0:T(8,128)(2,1)}, bf16[256,2048]{1,0:T(8,128)(2,1)}, u32[]{:S(2)}, u32[]{:S(2)}) collective-permute-start(bf16[256,2048]{1,0:T(8,128)(2,1)} %get-tuple-element.29), channel_id=1, source_target_pairs={{0,1},{1,0},{2,3},{3,2},{4,5},{5,4},{6,7},{7,6},{8,9},{9,8},{10,11... | collective-permute-start | bytes 3145736 | tf_op jit(solution)/shard_map/ppermute | solution.py:251
  16.0 60.6 %all-to-all-start = ((bf16[8,64,2048]{2,1,0:T(8,128)(2,1)}), bf16[8,64,2048]{2,1,0:T(8,128)(2,1)S(1)}, u32[]{:S(2)}, u32[]{:S(2)}) async-start(bf16[8,64,2048]{2,1,0:T(8,128)(2,1)} %gather_fusion), calls=%async_computation | async-start | bytes 4194304 | tf_op jit(solution)/shard_map/all_to_all | solution.py:276
  22.1 2.2 %copy-start.4 = (bf16[256,8192]{1,0:T(8,128)(2,1)S(1)}, bf16[256,8192]{1,0:T(8,128)(2,1)}, u32[]{:S(2)}) copy-start(bf16[256,8192]{1,0:T(8,128)(2,1)} %refs_0_.3) | copy-start | bytes 12582916
  42.8 1.5 copy-start.10
  44.3 39.5 %collective-permute-start.4 = (bf16[256,2048]{1,0:T(8,128)(2,1)}, bf16[256,2048]{1,0:T(8,128)(2,1)}, u32[]{:S(2)}, u32[]{:S(2)}) collective-permute-start(bf16[256,2048]{1,0:T(8,128)(2,1)} %get-tuple-element.29), channel_id=1, source_target_pairs={{0,2},{1,3},{2,0},{3,1},{4,6},{5,7},{6,4},{7,5},{8,10},{9,11},{10,... | collective-permute-start | bytes 3145736 | tf_op jit(solution)/shard_map/ppermute | solution.py:252
  45.8 38.0 %collective-permute-start.3 = (bf16[256,2048]{1,0:T(8,128)(2,1)}, bf16[256,2048]{1,0:T(8,128)(2,1)}, u32[]{:S(2)}, u32[]{:S(2)}) collective-permute-start(bf16[256,2048]{1,0:T(8,128)(2,1)} %get-tuple-element.28), channel_id=1, source_target_pairs={{0,1},{1,0},{2,3},{3,2},{4,5},{5,4},{6,7},{7,6},{8,9},{9,8},{10,11... | collective-permute-start | bytes 3145736 | tf_op jit(solution)/shard_map/ppermute | solution.py:251
  56.2 44.9 %collective-permute-start.6 = (bf16[256,2048]{1,0:T(8,128)(2,1)}, bf16[256,2048]{1,0:T(8,128)(2,1)}, u32[]{:S(2)}, u32[]{:S(2)}) collective-permute-start(bf16[256,2048]{1,0:T(8,128)(2,1)} %collective-permute-done.2.refs_2_), channel_id=1, source_target_pairs={{0,1},{1,0},{2,3},{3,2},{4,5},{5,4},{6,7},{7,6},{8,9},{9,8},{10,11... | collective-permute-start | bytes 3145736 | tf_op jit(solution)/shard_map/ppermute | solution.py:251
  57.7 43.5 %collective-permute-start.7 = (bf16[256,2048]{1,0:T(8,128)(2,1)}, bf16[256,2048]{1,0:T(8,128)(2,1)}, u32[]{:S(2)}, u32[]{:S(2)}) collective-permute-start(bf16[256,2048]{1,0:T(8,128)(2,1)} %collective-permute-done.1.refs_0_), channel_id=1, source_target_pairs={{0,2},{1,3},{2,0},{3,1},{4,6},{5,7},{6,4},{7,5},{8,10},{9,11},{10,... | collective-permute-start | bytes 3145736 | tf_op jit(solution)/shard_map/ppermute | solution.py:252
  74.3 2.4 %copy-start.6 = (f32[2,256,2560]{2,1,0:T(8,128)}, f32[2,256,2560]{2,1,0:T(8,128)S(1)}, u32[]{:S(2)}) copy-start(f32[2,256,2560]{2,1,0:T(8,128)S(1)} %near_rows.1.refs_3_.refs_4_) | copy-start | bytes 15728644
  76.7 2.2 %copy-start.12 = (bf16[8,64,2048]{2,1,0:T(8,128)(2,1)}, bf16[8,64,2048]{2,1,0:T(8,128)(2,1)S(1)}, u32[]{:S(2)}) copy-start(bf16[8,64,2048]{2,1,0:T(8,128)(2,1)S(1)} %all-to-all-done.refs_4_) | copy-start | bytes 6291460
  78.9 65.2 %all-to-all-start.1 = ((bf16[8,64,2560]{2,1,0:T(8,128)(2,1)}), bf16[8,64,2560]{2,1,0:T(8,128)(2,1)S(1)}, u32[]{:S(2)}, u32[]{:S(2)}) async-start(bf16[8,64,2560]{2,1,0:T(8,128)(2,1)} %gather_fusion.1), calls=%async_computation.1 | async-start | bytes 5242880 | tf_op jit(solution)/shard_map/all_to_all | solution.py:276
  83.8 44.5 %collective-permute-start.14 = (bf16[256,2048]{1,0:T(8,128)(2,1)}, bf16[256,2048]{1,0:T(8,128)(2,1)S(1)}, u32[]{:S(2)}, u32[]{:S(2)}) collective-permute-start(bf16[256,2048]{1,0:T(8,128)(2,1)} %get-tuple-element.45), channel_id=1, source_target_pairs={{0,1},{1,0},{2,3},{3,2},{4,5},{5,4},{6,7},{7,6},{8,9},{9,8},{10,11... | collective-permute-start | bytes 3145736 | tf_op jit(solution)/shard_map/ppermute | solution.py:251
  84.4 45.5 %collective-permute-start.15 = (bf16[256,2048]{1,0:T(8,128)(2,1)}, bf16[256,2048]{1,0:T(8,128)(2,1)S(1)}, u32[]{:S(2)}, u32[]{:S(2)}) collective-permute-start(bf16[256,2048]{1,0:T(8,128)(2,1)} %get-tuple-element.46), channel_id=1, source_target_pairs={{0,2},{1,3},{2,0},{3,1},{4,6},{5,7},{6,4},{7,5},{8,10},{9,11},{10,... | collective-permute-start | bytes 3145736 | tf_op jit(solution)/shard_map/ppermute | solution.py:252
  86.1 2.5 %copy-start.7 = (f32[2,256,2560]{2,1,0:T(8,128)S(1)}, f32[2,256,2560]{2,1,0:T(8,128)}, u32[]{:S(2)}) copy-start(f32[2,256,2560]{2,1,0:T(8,128)} %copy-done.6) | copy-start | bytes 15728644
  88.6 12.5 %copy-start.5 = (bf16[256,8192]{1,0:T(8,128)(2,1)S(1)}, bf16[256,8192]{1,0:T(8,128)(2,1)}, u32[]{:S(2)}) copy-start(bf16[256,8192]{1,0:T(8,128)(2,1)} %refs_0_.3) | copy-start | bytes 12582916
  88.6 12.5 %copy-start.13 = (bf16[8,64,2048]{2,1,0:T(8,128)(2,1)S(1)}, bf16[8,64,2048]{2,1,0:T(8,128)(2,1)}, u32[]{:S(2)}) copy-start(bf16[8,64,2048]{2,1,0:T(8,128)(2,1)} %copy-done.12) | copy-start | bytes 6291460
  104.9 19.3 %collective-permute-start.8 = (f32[128,128]{1,0:T(8,128)S(1)}, f32[128,128]{1,0:T(8,128)S(1)}, u32[]{:S(2)}, u32[]{:S(2)}) collective-permute-start(f32[128,128]{1,0:T(8,128)S(1)} %get-tuple-element.37), channel_id=1, source_target_pairs={{0,1},{1,0},{2,3},{3,2},{4,5},{5,4},{6,7},{7,6},{8,9},{9,8},{10,11... | collective-permute-start | bytes 196616 | tf_op jit(solution)/shard_map/ppermute | solution.py:251
  106.4 17.7 %collective-permute-start.9 = (f32[128,128]{1,0:T(8,128)S(1)}, f32[128,128]{1,0:T(8,128)S(1)}, u32[]{:S(2)}, u32[]{:S(2)}) collective-permute-start(f32[128,128]{1,0:T(8,128)S(1)} %get-tuple-element.38), channel_id=1, source_target_pairs={{0,2},{1,3},{2,0},{3,1},{4,6},{5,7},{6,4},{7,5},{8,10},{9,11},{10,... | collective-permute-start | bytes 196616 | tf_op jit(solution)/shard_map/ppermute | solution.py:252
  106.9 17.7 %collective-permute-start.10 = (f32[128,128]{1,0:T(8,128)S(1)}, f32[128,128]{1,0:T(8,128)S(1)}, u32[]{:S(2)}, u32[]{:S(2)}) collective-permute-start(f32[128,128]{1,0:T(8,128)S(1)} %get-tuple-element.39), channel_id=1, source_target_pairs={{0,3},{1,2},{2,1},{3,0},{4,7},{5,6},{6,5},{7,4},{8,11},{9,10},{10,... | collective-permute-start | bytes 196616 | tf_op jit(solution)/shard_map/ppermute | solution.py:253
  120.4 1.5 copy-start.8
  124.7 18.5 %collective-permute-start.17 = (bf16[128,128]{1,0:T(8,128)(2,1)S(1)}, bf16[128,128]{1,0:T(8,128)(2,1)S(1)}, u32[]{:S(2)}, u32[]{:S(2)}) collective-permute-start(bf16[128,128]{1,0:T(8,128)(2,1)S(1)} %add_convert_fusion.refs_2_), channel_id=1, source_target_pairs={{0,2},{1,3},{2,0},{3,1},{4,6},{5,7},{6,4},{7,5},{8,10},{9,11},{10,... | collective-permute-start | bytes 98312 | tf_op jit(solution)/shard_map/ppermute | solution.py:252
  126.4 16.8 %collective-permute-start.16 = (bf16[128,128]{1,0:T(8,128)(2,1)S(1)}, bf16[128,128]{1,0:T(8,128)(2,1)S(1)}, u32[]{:S(2)}, u32[]{:S(2)}) collective-permute-start(bf16[128,128]{1,0:T(8,128)(2,1)S(1)} %add_convert_fusion.refs_2_), channel_id=1, source_target_pairs={{0,1},{1,0},{2,3},{3,2},{4,5},{5,4},{6,7},{7,6},{8,9},{9,8},{10,11... | collective-permute-start | bytes 98312 | tf_op jit(solution)/shard_map/ppermute | solution.py:251
  127.9 25.1 %collective-permute-start.13 = (bf16[128,128]{1,0:T(8,128)(2,1)S(1)}, bf16[128,128]{1,0:T(8,128)(2,1)S(1)}, u32[]{:S(2)}, u32[]{:S(2)}) collective-permute-start(bf16[128,128]{1,0:T(8,128)(2,1)S(1)} %add_convert_fusion.refs_2_), channel_id=1, source_target_pairs={{0,3},{1,2},{2,1},{3,0},{4,7},{5,6},{6,5},{7,4},{8,11},{9,10},{10,... | collective-permute-start | bytes 98312 | tf_op jit(solution)/shard_map/ppermute | solution.py:253
  128.2 24.8 %collective-permute-start.11 = (bf16[256,2048]{1,0:T(8,128)(2,1)}, bf16[256,2048]{1,0:T(8,128)(2,1)}, u32[]{:S(2)}, u32[]{:S(2)}) collective-permute-start(bf16[256,2048]{1,0:T(8,128)(2,1)} %collective-permute-done.refs_1_), channel_id=1, source_target_pairs={{0,2},{1,3},{2,0},{3,1},{4,6},{5,7},{6,4},{7,5},{8,10},{9,11},{10,... | collective-permute-start | bytes 3145736 | tf_op jit(solution)/shard_map/ppermute | solution.py:252
  129.9 23.3 %collective-permute-start.12 = (bf16[256,2048]{1,0:T(8,128)(2,1)}, bf16[256,2048]{1,0:T(8,128)(2,1)}, u32[]{:S(2)}, u32[]{:S(2)}) collective-permute-start(bf16[256,2048]{1,0:T(8,128)(2,1)} %collective-permute-done.5.refs_3_), channel_id=1, source_target_pairs={{0,1},{1,0},{2,3},{3,2},{4,5},{5,4},{6,7},{7,6},{8,9},{9,8},{10,11... | collective-permute-start | bytes 3145736 | tf_op jit(solution)/shard_map/ppermute | solution.py:251
  140.9 2.4 %copy-start.14 = (f32[2,256,2560]{2,1,0:T(8,128)}, f32[2,256,2560]{2,1,0:T(8,128)S(1)}, u32[]{:S(2)}) copy-start(f32[2,256,2560]{2,1,0:T(8,128)S(1)} %near_rows_rest.1.refs_1_) | copy-start | bytes 15728644
  144.1 1.7 %copy-start.11 = (f32[1,256,2560]{2,1,0:T(8,128)S(1)}, f32[1,256,2560]{2,1,0:T(8,128)}, u32[]{:S(2)}) copy-start(f32[1,256,2560]{2,1,0:T(8,128)} %copy-done.10) | copy-start | bytes 7864324
  145.8 2.5 %copy-start.15 = (f32[2,256,2560]{2,1,0:T(8,128)S(1)}, f32[2,256,2560]{2,1,0:T(8,128)}, u32[]{:S(2)}) copy-start(f32[2,256,2560]{2,1,0:T(8,128)} %copy-done.14) | copy-start | bytes 15728644
  148.3 4.7 %copy-start.2 = (bf16[8,64,2560]{2,1,0:T(8,128)(2,1)}, bf16[8,64,2560]{2,1,0:T(8,128)(2,1)S(1)}, u32[]{:S(2)}) copy-start(bf16[8,64,2560]{2,1,0:T(8,128)(2,1)S(1)} %all-to-all-done.1.refs_5_.refs_6_.refs_7_) | copy-start | bytes 7864324
  148.3 5.0 %copy-start.9 = (f32[1,256,2560]{2,1,0:T(8,128)S(1)}, f32[1,256,2560]{2,1,0:T(8,128)}, u32[]{:S(2)}) copy-start(f32[1,256,2560]{2,1,0:T(8,128)} %copy-done.8) | copy-start | bytes 7864324
  153.2 1.7 %copy-start.3 = (bf16[8,64,2560]{2,1,0:T(8,128)(2,1)S(1)}, bf16[8,64,2560]{2,1,0:T(8,128)(2,1)}, u32[]{:S(2)}) copy-start(bf16[8,64,2560]{2,1,0:T(8,128)(2,1)} %copy-done.2) | copy-start | bytes 7864324
  155.0 13.1 %copy-start.1 = (bf16[4,64,2560]{2,1,0:T(8,128)(2,1)S(1)}, bf16[4,64,2560]{2,1,0:T(8,128)(2,1)}, u32[]{:S(2)}) copy-start(bf16[4,64,2560]{2,1,0:T(8,128)(2,1)} %param.9) | copy-start | bytes 3932164

commit v5 on v4

--- a/solution.py
+++ b/solution.py
@@ -10,7 +10,7 @@
 BLOCK = 128
 MIB = 1 << 20
 PANELS_AT = 4
-VMEM_BYTES = 32 * MIB
+VMEM_BYTES = 24 * MIB
 
 adapter_scale = 0.5
 
@@ -97,16 +97,18 @@
         operands.append(weight)
     totals_at = []
     if total is not None:
+        total = pltpu.with_memory_space_constraint(total, pltpu.HBM)
         for number in range(len(sets)):
             in_specs.append(pl.BlockSpec((None, rows, tile), lambda n, plan, number=number: (number, 0, n)))
             operands.append(total)
             totals_at.append(len(operands) - 1)
     updating, aliases = None, {}
     if update is None:
-        out_shape = jax.ShapeDtypeStruct((len(sets), rows, columns), jnp.float32)
+        out_shape = pltpu.HBM((len(sets), rows, columns), jnp.float32)
         out_spec = pl.BlockSpec((len(sets), rows, tile), lambda n, plan: (0, 0, n))
     else:
         first_set, shrink, panels = update
+        panels = pltpu.with_memory_space_constraint(panels, pltpu.HBM)
         in_specs.append(whole_spec(shrink))
         operands.append(shrink)
         shrink_at, panels_at = len(operands) - 1, []
@@ -167,6 +169,7 @@
 def finish(own, near, shrinks, panels, plan, row_total):
     _, rows, columns = near.shape
     rank = panels.shape[1]
+    own, near, panels = (pltpu.with_memory_space_constraint(array, pltpu.HBM) for array in (own, near, panels))
     tile = tile_of(columns, 2560)
     return pl.pallas_call(
         functools.partial(finish_kernel, 3),
@@ -275,12 +278,12 @@
     def exchange(panels):
         return lax.all_to_all(panels, "grp", split_axis=0, concat_axis=0, tiled=True)
 
-    down_out = chosen(down_weight, after(select_slot, s1, s2))
+    down_out = chosen(down_weight, after(select_slot, s0, s3))
     down = exchange(down_out)
 
     own = project(
         [[(tokens, (i * depth, (i + 1) * depth), None, i) for i in range(4)]],
-        frozen_weight, tile_of(frozen_weight.shape[1], 512), after(plan, down_out), rows, weigh=0, name="own_rows",
+        frozen_weight, tile_of(frozen_weight.shape[1], 256), after(plan, down_out), rows, weigh=0, name="own_rows",
     )
 
     tile = tile_of(frozen_weight.shape[1], 512)

time: 169 us -> 166 us (0.982)
  local copies, waits for them, and re-layouts: 31.7 us -> 15.4 us
  Pallas kernels: 87.7 us -> 102 us
    unnamed x38 -> x14, local copies, waits for them, and re-layouts: 18.4 us -> 2.22 us
    pallas_call x6, Pallas kernels: 79.3 us -> 89.1 us  [project(): pl.pallas_call(functools.partial(project_kernel, flat, weights_at, totals...]
    pallas_call x1, Pallas kernels: 4.71 us -> 8.92 us  [finish(): pl.pallas_call(functools.partial(finish_kernel, 3), grid_spec=pltpu.Prefe...]
    ppermute x8, waiting for transfers between devices: 6.84 us -> 9.2 us  [square(): to_x = lambda v: lax.ppermute(v, 'tp', [(i, i ^ 1) for i in range(4)])]
  transfers between devices with their start and end apart: 20 -> 20, of which waited for: 7 -> 6; matrix products, arithmetic and copies ran while one was open for 6% -> 6% of each run, Pallas kernels for 44% -> 54%
where the time goes in v5:
time: 166 us
  Pallas kernels  102 us (61%)
  starting transfers between devices  32.8 us (20%)
  local copies, waits for them, and re-layouts  15.4 us (9%)
  waiting for transfers between devices  15.4 us (9%)
    pallas_call x6, Pallas kernels, project(): pl.pallas_call(functools.partial(project_kernel, flat, weights_at, totals...  89.1 us
    ppermute x8, starting transfers between devices, square(): to_y = lambda v: lax.ppermute(v, 'tp', [(i, i ^ 2) for i in range(4)])  11.2 us
    all_to_all x2, starting transfers between devices, exchange(): lax.all_to_all(panels, 'grp', split_axis=0, concat_axis=0, tiled=True)  10.2 us
    ppermute x8, starting transfers between devices, square(): to_x = lambda v: lax.ppermute(v, 'tp', [(i, i ^ 1) for i in range(4)])  9.63 us
    ppermute x8, waiting for transfers between devices, square(): to_x = lambda v: lax.ppermute(v, 'tp', [(i, i ^ 1) for i in range(4)])  9.2 us
    pallas_call x1, Pallas kernels, finish(): pl.pallas_call(functools.partial(finish_kernel, 3), grid_spec=pltpu.Prefe...  8.92 us
    dynamic_slice x2, local copies, waits for them, and re-layouts, part(): return lax.dynamic_slice(array, (0, start), (rows, size))  8.49 us
    ppermute x8, waiting for transfers between devices, square(): to_y = lambda v: lax.ppermute(v, 'tp', [(i, i ^ 2) for i in range(4)])  5.67 us
  transfers between devices with their start and end apart: 20, of which 6 were waited for; matrix products, arithmetic and copies ran while one was open for 6% of the time, Pallas kernels for 54%

profile of v5, /device:TPU:0, one launch (start us, length us, event | category | flops | bytes accessed | tf_op | source)
XLA Modules:
  0.0 166.0 jit_solution(17241443808885929158)
XLA Ops:
  0.0 4.3 %constant_dynamic-slice_fusion.2 = (bf16[256,2048]{1,0:T(8,128)(2,1)}, bf16[256,2048]{1,0:T(8,128)(2,1)}) fusion(bf16[256,8192]{1,0:T(8,128)(2,1)} %refs_0_.3, s32[]{:T(128)S(6)} %select_n.48, s32[]{:T(128)S(6)} %select_n.47), kind=kLoop, calls=%fused_computation.26 | loop fusion | bytes 4194312 | tf_op jit(solution)/shard_map/dynamic_slice | solution.py:264
  4.3 3.1 %collective-permute-start.2 = (bf16[256,2048]{1,0:T(8,128)(2,1)}, bf16[256,2048]{1,0:T(8,128)(2,1)}, u32[]{:S(2)}, u32[]{:S(2)}) collective-permute-start(bf16[256,2048]{1,0:T(8,128)(2,1)} %get-tuple-element.45), channel_id=1, source_target_pairs={{0,2},{1,3},{2,0},{3,1},{4,6},{5,7},{6,4},{7,5},{8,10},{9,11},{10,... | collective-permute-start | bytes 3145736 | tf_op jit(solution)/shard_map/ppermute | solution.py:255
  7.4 1.5 collective-permute-start.1
  8.8 4.2 %constant_dynamic-slice_fusion = (bf16[256,2048]{1,0:T(8,128)(2,1)}, bf16[256,2048]{1,0:T(8,128)(2,1)}) fusion(bf16[256,8192]{1,0:T(8,128)(2,1)} %refs_0_.3, s32[]{:T(128)S(6)} %select_n.50, s32[]{:T(128)S(6)} %select_n.49), kind=kLoop, calls=%fused_computation.24 | loop fusion | bytes 4194312 | tf_op jit(solution)/shard_map/dynamic_slice | solution.py:264
  13.0 0.5 collective-permute-start.5
  13.5 0.1 collective-permute-start
  13.7 0.1 select_reduce_fusion
  13.8 0.1 reduce_sum.31
  13.8 0.1 fusion.2
  14.0 2.0 %gather_fusion = bf16[8,64,2048]{2,1,0:T(8,128)(2,1)} fusion(bf16[4,64,2048]{2,1,0:T(8,128)(2,1)S(1)} %copy-done.4, s32[1024]{0:T(1024)S(1)} %pad_clamp_fusion.1), kind=kCustom, calls=%fused_computation | custom fusion | bytes 4194336 | tf_op jit(solution)/shard_map/jit(_take)/gather | solution.py:276
  16.0 5.3 %all-to-all-start = ((bf16[8,64,2048]{2,1,0:T(8,128)(2,1)}), bf16[8,64,2048]{2,1,0:T(8,128)(2,1)S(1)}, u32[]{:S(2)}, u32[]{:S(2)}) async-start(bf16[8,64,2048]{2,1,0:T(8,128)(2,1)} %gather_fusion), calls=%async_computation | async-start | bytes 4194304 | tf_op jit(solution)/shard_map/all_to_all | solution.py:279
  21.3 0.1 dynamic_slice.15
  21.4 0.1 broadcast_in_dim.53
  21.5 0.1 copy.8
  21.6 0.1 select_reduce_fusion.1
  21.8 0.1 copy.9
  21.9 0.1 reshape.34
  22.0 2.2 %copy-done.2 = bf16[256,8192]{1,0:T(8,128)(2,1)S(1)} copy-done((bf16[256,8192]{1,0:T(8,128)(2,1)S(1)}, bf16[256,8192]{1,0:T(8,128)(2,1)}, u32[]{:S(2)}) %copy-start.2) | copy-done | bytes 4194328
  24.2 21.2 %own_rows.1.refs_0_ = f32[1,256,2560]{2,1,0:T(8,128)} custom-call(s32[12]{0:T(128)S(1)} %pad_add_fusion.plan_ref, bf16[256,8192]{1,0:T(8,128)(2,1)S(1)} %copy-done.2, bf16[8192,2560]{1,0:T(8,128)(2,1)} %refs_3_.5, bf16[8192,2560]{1,0:T(8,128)(2,1)} %refs_3_.5, bf16[8192,2560]{1,0:T(8,128)(2,1)} %refs_3_.5, bf16[8192,2560]{1,0:T(8,128)(2,1)} %refs_3_.5), custom_call_target="tpu_custom_call" | custom-call | tf_op jit(solution)/shard_map/own_rows/pallas_call | solution.py:131
  45.4 1.6 collective-permute-start.4
  47.0 1.5 collective-permute-start.3
  48.5 5.7 %collective-permute-done.5.refs_3_ = bf16[256,2048]{1,0:T(8,128)(2,1)} collective-permute-done((bf16[256,2048]{1,0:T(8,128)(2,1)}, bf16[256,2048]{1,0:T(8,128)(2,1)}, u32[]{:S(2)}, u32[]{:S(2)}) %collective-permute-start.5) | collective-permute-done | bytes 1048608 | tf_op jit(solution)/shard_map/ppermute | solution.py:255
  54.1 2.1 %collective-permute-done.refs_1_ = bf16[256,2048]{1,0:T(8,128)(2,1)} collective-permute-done((bf16[256,2048]{1,0:T(8,128)(2,1)}, bf16[256,2048]{1,0:T(8,128)(2,1)}, u32[]{:S(2)}, u32[]{:S(2)}) %collective-permute-start) | collective-permute-done | bytes 1048608 | tf_op jit(solution)/shard_map/ppermute | solution.py:254
  56.2 1.5 collective-permute-start.6
  57.7 0.5 collective-permute-start.7
  58.2 17.3 %near_rows.1.refs_3_.refs_4_ = f32[2,256,2560]{2,1,0:T(8,128)} custom-call(s32[12]{0:T(128)S(1)} %pad_add_fusion.plan_ref, bf16[256,2048]{1,0:T(8,128)(2,1)} %collective-permute-done.1.refs_0_, bf16[256,2048]{1,0:T(8,128)(2,1)} %collective-permute-done.refs_1_, bf16[256,2048]{1,0:T(8,128)(2,1)} %collective-permute-done.2.refs_2_, ...), custom_call_target="tpu_custom_call" | custom-call | flops 64424509440 | bytes 283115520 | tf_op jit(solution)/shard_map/near_rows/pallas_call | solution.py:131
  75.6 2.2 %gather_fusion.1 = bf16[8,64,2560]{2,1,0:T(8,128)(2,1)} fusion(bf16[4,64,2560]{2,1,0:T(8,128)(2,1)S(1)} %copy-done, s32[1024]{0:T(1024)S(1)} %pad_clamp_fusion), kind=kCustom, calls=%fused_computation.1 | custom fusion | bytes 5242912 | tf_op jit(solution)/shard_map/jit(_take)/gather | solution.py:276
  77.8 4.9 %all-to-all-start.1 = ((bf16[8,64,2560]{2,1,0:T(8,128)(2,1)}), bf16[8,64,2560]{2,1,0:T(8,128)(2,1)}, u32[]{:S(2)}, u32[]{:S(2)}) async-start(bf16[8,64,2560]{2,1,0:T(8,128)(2,1)} %gather_fusion.1), calls=%async_computation.1 | async-start | bytes 5242880 | tf_op jit(solution)/shard_map/all_to_all | solution.py:279
  82.7 0.6 collective-permute-start.14
  83.3 1.6 collective-permute-start.15
  84.8 12.9 %near_rows_more.1.refs_3_.refs_4_ = f32[2,256,2560]{2,1,0:T(8,128)} custom-call(s32[12]{0:T(128)S(1)} %pad_add_fusion.plan_ref, bf16[256,2048]{1,0:T(8,128)(2,1)} %collective-permute-done.3.refs_0_.refs_1_, bf16[256,2048]{1,0:T(8,128)(2,1)} %collective-permute-done.4.refs_1_.refs_2_, bf16[8192,2560]{1,0:T(8,128)(2,1)} %refs_3_.5, ...), custom_call_target="tpu_custom_call" | custom-call | tf_op jit(solution)/shard_map/near_rows_more/pallas_call | solution.py:131
  97.7 3.4 %collective-permute-done.6.refs_1_ = bf16[256,2048]{1,0:T(8,128)(2,1)} collective-permute-done((bf16[256,2048]{1,0:T(8,128)(2,1)}, bf16[256,2048]{1,0:T(8,128)(2,1)}, u32[]{:S(2)}, u32[]{:S(2)}) %collective-permute-start.6) | collective-permute-done | bytes 1048608 | tf_op jit(solution)/shard_map/ppermute | solution.py:254
  101.2 3.7 %shrink_parts.1 = (f32[128,128]{1,0:T(8,128)S(1)}, f32[128,128]{1,0:T(8,128)S(1)}, f32[128,128]{1,0:T(8,128)S(1)}, f32[128,128]{1,0:T(8,128)S(1)}) custom-call(s32[12]{0:T(128)S(1)} %pad_add_fusion.plan_ref, bf16[256,8192]{1,0:T(8,128)(2,1)S(1)} %copy-done.3, bf16[256,2048]{1,0:T(8,128)(2,1)} %collective-permute-done.3.refs_0_.refs_1_, ...), custom_call_target="tpu_custom_call" | custom-call | flops 1073741824 | bytes 6291456 | tf_op jit(solution)/shard_map/shrink_parts/pallas_call | solution.py:229
  104.9 1.5 collective-permute-start.8
  106.4 0.5 collective-permute-start.9
  107.0 1.5 collective-permute-start.10
  108.5 13.0 %far_rows.1.refs_4_ = f32[1,256,2560]{2,1,0:T(8,128)} custom-call(s32[12]{0:T(128)S(1)} %pad_add_fusion.plan_ref, bf16[256,2048]{1,0:T(8,128)(2,1)} %collective-permute-done.7.refs_3_.refs_0_, bf16[256,2048]{1,0:T(8,128)(2,1)} %collective-permute-done.6.refs_1_, bf16[8192,2560]{1,0:T(8,128)(2,1)} %refs_3_.5, bf16[8192,2560]{1,0:T(8,128)(2,1)} %refs_3_.5), custom_call_target="tpu_custom_call" | custom-call | flops 21474836480 | bytes 94371840 | tf_op jit(solution)/shard_map/far_rows/pallas_call | solution.py:131
  121.5 2.7 %collective-permute-done.8 = f32[128,128]{1,0:T(8,128)S(1)} collective-permute-done((f32[128,128]{1,0:T(8,128)S(1)}, f32[128,128]{1,0:T(8,128)S(1)}, u32[]{:S(2)}, u32[]{:S(2)}) %collective-permute-start.8) | collective-permute-done | bytes 65568 | tf_op jit(solution)/shard_map/ppermute | solution.py:254
  124.2 0.5 collective-permute-done.10
  124.7 1.7 %collective-permute-start.17 = (bf16[128,128]{1,0:T(8,128)(2,1)S(1)}, bf16[128,128]{1,0:T(8,128)(2,1)S(1)}, u32[]{:S(2)}, u32[]{:S(2)}) collective-permute-start(bf16[128,128]{1,0:T(8,128)(2,1)S(1)} %add_convert_fusion.refs_2_), channel_id=1, source_target_pairs={{0,2},{1,3},{2,0},{3,1},{4,6},{5,7},{6,4},{7,5},{8,10},{9,11},{10,... | collective-permute-start | bytes 98312 | tf_op jit(solution)/shard_map/ppermute | solution.py:255
  126.4 1.5 collective-permute-start.16
  127.9 0.3 collective-permute-start.13
  128.3 1.7 %collective-permute-start.11 = (bf16[256,2048]{1,0:T(8,128)(2,1)}, bf16[256,2048]{1,0:T(8,128)(2,1)S(1)}, u32[]{:S(2)}, u32[]{:S(2)}) collective-permute-start(bf16[256,2048]{1,0:T(8,128)(2,1)} %collective-permute-done.refs_1_), channel_id=1, source_target_pairs={{0,2},{1,3},{2,0},{3,1},{4,6},{5,7},{6,4},{7,5},{8,10},{9,11},{10,... | collective-permute-start | bytes 3145736 | tf_op jit(solution)/shard_map/ppermute | solution.py:255
  129.9 1.5 collective-permute-start.12
  131.4 11.8 %near_rows_rest.1.refs_1_ = f32[2,256,2560]{2,1,0:T(8,128)} custom-call(s32[12]{0:T(128)S(1)} %pad_add_fusion.plan_ref, bf16[256,2048]{1,0:T(8,128)(2,1)S(1)} %collective-permute-done.14.refs_0_, bf16[256,2048]{1,0:T(8,128)(2,1)S(1)} %collective-permute-done.15.refs_1_, bf16[8192,2560]{1,0:T(8,128)(2,1)} %refs_3_.5, ...), custom_call_target="tpu_custom_call" | custom-call | flops 21474836480 | bytes 125829120 | tf_op jit(solution)/shard_map/near_rows_rest/pallas_call | solution.py:131
  143.3 8.9 %finish_rows.1.refs_8_ = bf16[1024,2560]{1,0:T(8,128)(2,1)} custom-call(s32[12]{0:T(128)S(1)} %pad_add_fusion.plan_ref, f32[1,256,2560]{2,1,0:T(8,128)} %own_rows.1.refs_0_, f32[2,256,2560]{2,1,0:T(8,128)} %near_rows_rest.1.refs_1_, bf16[128,128]{1,0:T(8,128)(2,1)S(1)} %add_convert_fusion.refs_2_, bf16[128,128]{1,0:T(8,128)(2,1)S(1)} %collective-permute-done.16.refs_3_, ...), custom_call_target="tpu_custom_call" | custom-call | flops 503316480 | bytes 11796480 | tf_op jit(solution)/shard_map/finish_rows/pallas_call | solution.py:174
  152.2 0.9 collective-permute-done.12.refs_1_
  153.1 12.8 %last_rows.1 = bf16[1024,2560]{1,0:T(8,128)(2,1)} custom-call(s32[12]{0:T(128)S(1)} %pad_add_fusion.plan_ref, bf16[256,2048]{1,0:T(8,128)(2,1)S(1)} %collective-permute-done.11.refs_0_, bf16[256,2048]{1,0:T(8,128)(2,1)S(1)} %collective-permute-done.12.refs_1_, bf16[8192,2560]{1,0:T(8,128)(2,1)} %refs_3_.5, ...), custom_call_target="tpu_custom_call", output_to_operand_aliasing={{}: (9, {})} | custom-call | flops 10737418240 | bytes 52428800 | tf_op jit(solution)/shard_map/last_rows/pallas_call | solution.py:131
  (34 shorter events, 0.3 us)
Async XLA Ops:
  0.0 75.6 %copy-start = (bf16[4,64,2560]{2,1,0:T(8,128)(2,1)S(1)}, bf16[4,64,2560]{2,1,0:T(8,128)(2,1)}, u32[]{:S(2)}) copy-start(bf16[4,64,2560]{2,1,0:T(8,128)(2,1)} %param.9) | copy-start | bytes 3932164
  4.3 9.4 %copy-start.5 = (s32[32]{0:T(128)S(1)}, s32[32]{0:T(128)}, u32[]{:S(2)}) copy-start(s32[32]{0:T(128)} %param.10) | copy-start | bytes 388
  4.3 9.4 %copy-start.6 = (s32[64]{0:T(128)S(1)}, s32[64]{0:T(128)}, u32[]{:S(2)}) copy-start(s32[64]{0:T(128)} %param.11) | copy-start | bytes 772
  4.3 9.7 %copy-start.4 = (bf16[4,64,2048]{2,1,0:T(8,128)(2,1)S(1)}, bf16[4,64,2048]{2,1,0:T(8,128)(2,1)}, u32[]{:S(2)}) copy-start(bf16[4,64,2048]{2,1,0:T(8,128)(2,1)} %param.8) | copy-start | bytes 3145732
  4.3 41.1 %collective-permute-start.2 = (bf16[256,2048]{1,0:T(8,128)(2,1)}, bf16[256,2048]{1,0:T(8,128)(2,1)}, u32[]{:S(2)}, u32[]{:S(2)}) collective-permute-start(bf16[256,2048]{1,0:T(8,128)(2,1)} %get-tuple-element.45), channel_id=1, source_target_pairs={{0,2},{1,3},{2,0},{3,1},{4,6},{5,7},{6,4},{7,5},{8,10},{9,11},{10,... | collective-permute-start | bytes 3145736 | tf_op jit(solution)/shard_map/ppermute | solution.py:255
  7.4 38.0 %collective-permute-start.1 = (bf16[256,2048]{1,0:T(8,128)(2,1)}, bf16[256,2048]{1,0:T(8,128)(2,1)}, u32[]{:S(2)}, u32[]{:S(2)}) collective-permute-start(bf16[256,2048]{1,0:T(8,128)(2,1)} %get-tuple-element.46), channel_id=1, source_target_pairs={{0,1},{1,0},{2,3},{3,2},{4,5},{5,4},{6,7},{7,6},{8,9},{9,8},{10,11... | collective-permute-start | bytes 3145736 | tf_op jit(solution)/shard_map/ppermute | solution.py:254
  13.0 41.1 %collective-permute-start.5 = (bf16[256,2048]{1,0:T(8,128)(2,1)}, bf16[256,2048]{1,0:T(8,128)(2,1)}, u32[]{:S(2)}, u32[]{:S(2)}) collective-permute-start(bf16[256,2048]{1,0:T(8,128)(2,1)} %get-tuple-element.28), channel_id=1, source_target_pairs={{0,2},{1,3},{2,0},{3,1},{4,6},{5,7},{6,4},{7,5},{8,10},{9,11},{10,... | collective-permute-start | bytes 3145736 | tf_op jit(solution)/shard_map/ppermute | solution.py:255
  13.5 42.7 %collective-permute-start = (bf16[256,2048]{1,0:T(8,128)(2,1)}, bf16[256,2048]{1,0:T(8,128)(2,1)}, u32[]{:S(2)}, u32[]{:S(2)}) collective-permute-start(bf16[256,2048]{1,0:T(8,128)(2,1)} %get-tuple-element.29), channel_id=1, source_target_pairs={{0,1},{1,0},{2,3},{3,2},{4,5},{5,4},{6,7},{7,6},{8,9},{9,8},{10,11... | collective-permute-start | bytes 3145736 | tf_op jit(solution)/shard_map/ppermute | solution.py:254
  16.0 59.6 %all-to-all-start = ((bf16[8,64,2048]{2,1,0:T(8,128)(2,1)}), bf16[8,64,2048]{2,1,0:T(8,128)(2,1)S(1)}, u32[]{:S(2)}, u32[]{:S(2)}) async-start(bf16[8,64,2048]{2,1,0:T(8,128)(2,1)} %gather_fusion), calls=%async_computation | async-start | bytes 4194304 | tf_op jit(solution)/shard_map/all_to_all | solution.py:279
  22.0 2.2 %copy-start.2 = (bf16[256,8192]{1,0:T(8,128)(2,1)S(1)}, bf16[256,8192]{1,0:T(8,128)(2,1)}, u32[]{:S(2)}) copy-start(bf16[256,8192]{1,0:T(8,128)(2,1)} %refs_0_.3) | copy-start | bytes 12582916
  45.4 37.3 %collective-permute-start.4 = (bf16[256,2048]{1,0:T(8,128)(2,1)}, bf16[256,2048]{1,0:T(8,128)(2,1)}, u32[]{:S(2)}, u32[]{:S(2)}) collective-permute-start(bf16[256,2048]{1,0:T(8,128)(2,1)} %get-tuple-element.29), channel_id=1, source_target_pairs={{0,2},{1,3},{2,0},{3,1},{4,6},{5,7},{6,4},{7,5},{8,10},{9,11},{10,... | collective-permute-start | bytes 3145736 | tf_op jit(solution)/shard_map/ppermute | solution.py:255
  47.0 35.7 %collective-permute-start.3 = (bf16[256,2048]{1,0:T(8,128)(2,1)}, bf16[256,2048]{1,0:T(8,128)(2,1)}, u32[]{:S(2)}, u32[]{:S(2)}) collective-permute-start(bf16[256,2048]{1,0:T(8,128)(2,1)} %get-tuple-element.28), channel_id=1, source_target_pairs={{0,1},{1,0},{2,3},{3,2},{4,5},{5,4},{6,7},{7,6},{8,9},{9,8},{10,11... | collective-permute-start | bytes 3145736 | tf_op jit(solution)/shard_map/ppermute | solution.py:254
  56.2 44.9 %collective-permute-start.6 = (bf16[256,2048]{1,0:T(8,128)(2,1)}, bf16[256,2048]{1,0:T(8,128)(2,1)}, u32[]{:S(2)}, u32[]{:S(2)}) collective-permute-start(bf16[256,2048]{1,0:T(8,128)(2,1)} %collective-permute-done.2.refs_2_), channel_id=1, source_target_pairs={{0,1},{1,0},{2,3},{3,2},{4,5},{5,4},{6,7},{7,6},{8,9},{9,8},{10,11... | collective-permute-start | bytes 3145736 | tf_op jit(solution)/shard_map/ppermute | solution.py:254
  57.7 43.5 %collective-permute-start.7 = (bf16[256,2048]{1,0:T(8,128)(2,1)}, bf16[256,2048]{1,0:T(8,128)(2,1)}, u32[]{:S(2)}, u32[]{:S(2)}) collective-permute-start(bf16[256,2048]{1,0:T(8,128)(2,1)} %collective-permute-done.1.refs_0_), channel_id=1, source_target_pairs={{0,2},{1,3},{2,0},{3,1},{4,6},{5,7},{6,4},{7,5},{8,10},{9,11},{10,... | collective-permute-start | bytes 3145736 | tf_op jit(solution)/shard_map/ppermute | solution.py:255
  77.8 65.5 %all-to-all-start.1 = ((bf16[8,64,2560]{2,1,0:T(8,128)(2,1)}), bf16[8,64,2560]{2,1,0:T(8,128)(2,1)}, u32[]{:S(2)}, u32[]{:S(2)}) async-start(bf16[8,64,2560]{2,1,0:T(8,128)(2,1)} %gather_fusion.1), calls=%async_computation.1 | async-start | bytes 5242880 | tf_op jit(solution)/shard_map/all_to_all | solution.py:279
  82.7 45.6 %collective-permute-start.14 = (bf16[256,2048]{1,0:T(8,128)(2,1)}, bf16[256,2048]{1,0:T(8,128)(2,1)S(1)}, u32[]{:S(2)}, u32[]{:S(2)}) collective-permute-start(bf16[256,2048]{1,0:T(8,128)(2,1)} %get-tuple-element.45), channel_id=1, source_target_pairs={{0,1},{1,0},{2,3},{3,2},{4,5},{5,4},{6,7},{7,6},{8,9},{9,8},{10,11... | collective-permute-start | bytes 3145736 | tf_op jit(solution)/shard_map/ppermute | solution.py:254
  83.3 46.7 %collective-permute-start.15 = (bf16[256,2048]{1,0:T(8,128)(2,1)}, bf16[256,2048]{1,0:T(8,128)(2,1)S(1)}, u32[]{:S(2)}, u32[]{:S(2)}) collective-permute-start(bf16[256,2048]{1,0:T(8,128)(2,1)} %get-tuple-element.46), channel_id=1, source_target_pairs={{0,2},{1,3},{2,0},{3,1},{4,6},{5,7},{6,4},{7,5},{8,10},{9,11},{10,... | collective-permute-start | bytes 3145736 | tf_op jit(solution)/shard_map/ppermute | solution.py:255
  84.8 16.4 %copy-start.3 = (bf16[256,8192]{1,0:T(8,128)(2,1)S(1)}, bf16[256,8192]{1,0:T(8,128)(2,1)}, u32[]{:S(2)}) copy-start(bf16[256,8192]{1,0:T(8,128)(2,1)} %refs_0_.3) | copy-start | bytes 12582916
  104.9 19.3 %collective-permute-start.8 = (f32[128,128]{1,0:T(8,128)S(1)}, f32[128,128]{1,0:T(8,128)S(1)}, u32[]{:S(2)}, u32[]{:S(2)}) collective-permute-start(f32[128,128]{1,0:T(8,128)S(1)} %get-tuple-element.37), channel_id=1, source_target_pairs={{0,1},{1,0},{2,3},{3,2},{4,5},{5,4},{6,7},{7,6},{8,9},{9,8},{10,11... | collective-permute-start | bytes 196616 | tf_op jit(solution)/shard_map/ppermute | solution.py:254
  106.4 17.8 %collective-permute-start.9 = (f32[128,128]{1,0:T(8,128)S(1)}, f32[128,128]{1,0:T(8,128)S(1)}, u32[]{:S(2)}, u32[]{:S(2)}) collective-permute-start(f32[128,128]{1,0:T(8,128)S(1)} %get-tuple-element.38), channel_id=1, source_target_pairs={{0,2},{1,3},{2,0},{3,1},{4,6},{5,7},{6,4},{7,5},{8,10},{9,11},{10,... | collective-permute-start | bytes 196616 | tf_op jit(solution)/shard_map/ppermute | solution.py:255
  107.0 17.7 %collective-permute-start.10 = (f32[128,128]{1,0:T(8,128)S(1)}, f32[128,128]{1,0:T(8,128)S(1)}, u32[]{:S(2)}, u32[]{:S(2)}) collective-permute-start(f32[128,128]{1,0:T(8,128)S(1)} %get-tuple-element.39), channel_id=1, source_target_pairs={{0,3},{1,2},{2,1},{3,0},{4,7},{5,6},{6,5},{7,4},{8,11},{9,10},{10,... | collective-permute-start | bytes 196616 | tf_op jit(solution)/shard_map/ppermute | solution.py:256
  124.7 18.6 %collective-permute-start.17 = (bf16[128,128]{1,0:T(8,128)(2,1)S(1)}, bf16[128,128]{1,0:T(8,128)(2,1)S(1)}, u32[]{:S(2)}, u32[]{:S(2)}) collective-permute-start(bf16[128,128]{1,0:T(8,128)(2,1)S(1)} %add_convert_fusion.refs_2_), channel_id=1, source_target_pairs={{0,2},{1,3},{2,0},{3,1},{4,6},{5,7},{6,4},{7,5},{8,10},{9,11},{10,... | collective-permute-start | bytes 98312 | tf_op jit(solution)/shard_map/ppermute | solution.py:255
  126.4 16.8 %collective-permute-start.16 = (bf16[128,128]{1,0:T(8,128)(2,1)S(1)}, bf16[128,128]{1,0:T(8,128)(2,1)S(1)}, u32[]{:S(2)}, u32[]{:S(2)}) collective-permute-start(bf16[128,128]{1,0:T(8,128)(2,1)S(1)} %add_convert_fusion.refs_2_), channel_id=1, source_target_pairs={{0,1},{1,0},{2,3},{3,2},{4,5},{5,4},{6,7},{7,6},{8,9},{9,8},{10,11... | collective-permute-start | bytes 98312 | tf_op jit(solution)/shard_map/ppermute | solution.py:254
  127.9 24.3 %collective-permute-start.13 = (bf16[128,128]{1,0:T(8,128)(2,1)S(1)}, bf16[128,128]{1,0:T(8,128)(2,1)S(1)}, u32[]{:S(2)}, u32[]{:S(2)}) collective-permute-start(bf16[128,128]{1,0:T(8,128)(2,1)S(1)} %add_convert_fusion.refs_2_), channel_id=1, source_target_pairs={{0,3},{1,2},{2,1},{3,0},{4,7},{5,6},{6,5},{7,4},{8,11},{9,10},{10,... | collective-permute-start | bytes 98312 | tf_op jit(solution)/shard_map/ppermute | solution.py:256
  128.3 23.9 %collective-permute-start.11 = (bf16[256,2048]{1,0:T(8,128)(2,1)}, bf16[256,2048]{1,0:T(8,128)(2,1)S(1)}, u32[]{:S(2)}, u32[]{:S(2)}) collective-permute-start(bf16[256,2048]{1,0:T(8,128)(2,1)} %collective-permute-done.refs_1_), channel_id=1, source_target_pairs={{0,2},{1,3},{2,0},{3,1},{4,6},{5,7},{6,4},{7,5},{8,10},{9,11},{10,... | collective-permute-start | bytes 3145736 | tf_op jit(solution)/shard_map/ppermute | solution.py:255
  129.9 23.2 %collective-permute-start.12 = (bf16[256,2048]{1,0:T(8,128)(2,1)}, bf16[256,2048]{1,0:T(8,128)(2,1)S(1)}, u32[]{:S(2)}, u32[]{:S(2)}) collective-permute-start(bf16[256,2048]{1,0:T(8,128)(2,1)} %collective-permute-done.5.refs_3_), channel_id=1, source_target_pairs={{0,1},{1,0},{2,3},{3,2},{4,5},{5,4},{6,7},{7,6},{8,9},{9,8},{10,11... | collective-permute-start | bytes 3145736 | tf_op jit(solution)/shard_map/ppermute | solution.py:254
  153.1 12.8 %copy-start.1 = (bf16[4,64,2560]{2,1,0:T(8,128)(2,1)S(1)}, bf16[4,64,2560]{2,1,0:T(8,128)(2,1)}, u32[]{:S(2)}) copy-start(bf16[4,64,2560]{2,1,0:T(8,128)(2,1)} %param.9) | copy-start | bytes 3932164

commit v6 on v5

--- a/solution.py
+++ b/solution.py
@@ -44,6 +44,36 @@
     if at is None:
         return ref[...]
     return ref[:, at[0] : at[1]] if isinstance(at, tuple) else ref[at]
+
+
+def cut_kernel(member_ref, tokens_ref, far_ref, own_ref, sems):
+    depth = far_ref.shape[1]
+    copies = []
+    for number, (out_ref, flip) in enumerate(((far_ref, 3), (own_ref, 0))):
+        start = pl.multiple_of((member_ref[0] ^ flip) * depth, depth)
+        copies.append(pltpu.make_async_copy(tokens_ref.at[:, pl.ds(start, depth)], out_ref, sems.at[number]))
+    for copy in copies:
+        copy.start()
+    for copy in copies:
+        copy.wait()
+
+
+def first_cuts(tokens, member):
+    rows, width = tokens.shape
+    shape = (rows, width // 4)
+    return pl.pallas_call(
+        cut_kernel,
+        grid_spec=pltpu.PrefetchScalarGridSpec(
+            num_scalar_prefetch=1,
+            grid=(1,),
+            in_specs=[pl.BlockSpec(memory_space=pl.ANY)],
+            out_specs=[pl.BlockSpec(memory_space=pltpu.VMEM)] * 2,
+            scratch_shapes=[pltpu.SemaphoreType.DMA((2,))],
+        ),
+        out_shape=[pltpu.VMEM(shape, tokens.dtype)] * 2,
+        cost_estimate=cost(0, 2 * tokens.size),
+        name="first_cuts",
+    )(member.astype(jnp.int32).reshape(1), tokens)
 
 
 def project_kernel(sets, weights_at, totals_at, update, plan_ref, *refs):
@@ -266,7 +296,7 @@
     def cut(j, *others):
         return part(tokens, after((member ^ 3 ^ j) * depth, *others), depth)
 
-    s0, s3 = cut(0), cut(3)
+    s0, s3 = first_cuts(tokens, member)
     x0, y3 = to_x(s0), to_y(s3)
     s1, s2 = cut(1, s0, s3), cut(2, s0, s3)
     x1, y2 = to_x(s1), to_y(s2)

time: 166 us -> 165 us (level)
  local copies, waits for them, and re-layouts: 15.4 us -> 11.1 us
  Pallas kernels: 102 us -> 105 us
    ppermute x8, waiting for transfers between devices: 5.67 us -> 12 us  [square(): to_y = lambda v: lax.ppermute(v, 'tp', [(i, i ^ 2) for i in range(4)])]
    ppermute x8, waiting for transfers between devices: 9.2 us -> 3.35 us  [square(): to_x = lambda v: lax.ppermute(v, 'tp', [(i, i ^ 1) for i in range(4)])]
    dynamic_slice x2 -> x1, local copies, waits for them, and re-layouts: 8.49 us -> 4.19 us  [part(): return lax.dynamic_slice(array, (0, start), (rows, size))]
    pallas_call x0 -> x1, Pallas kernels: none -> 3 us  [first_cuts(): pl.pallas_call(cut_kernel, grid_spec=pltpu.PrefetchScalarGridSpec(num_sca...]
    ppermute x8, starting transfers between devices: 9.63 us -> 7.39 us  [square(): to_x = lambda v: lax.ppermute(v, 'tp', [(i, i ^ 1) for i in range(4)])]
  transfers between devices with their start and end apart: 20 -> 20, of which waited for: 6 -> 7; matrix products, arithmetic and copies ran while one was open for 6% -> 6% of each run, Pallas kernels for 54% -> 54%
where the time goes in v6:
time: 165 us; the launch traced here: 164 us
  Pallas kernels  105 us (64%)
  starting transfers between devices  31.7 us (19%)
  waiting for transfers between devices  16.1 us (10%)
  local copies, waits for them, and re-layouts  11.1 us (7%)
    pallas_call x6, Pallas kernels, project(): pl.pallas_call(functools.partial(project_kernel, flat, weights_at, totals...  89.1 us
    ppermute x8, waiting for transfers between devices, square(): to_y = lambda v: lax.ppermute(v, 'tp', [(i, i ^ 2) for i in range(4)])  12 us
    ppermute x8, starting transfers between devices, square(): to_y = lambda v: lax.ppermute(v, 'tp', [(i, i ^ 2) for i in range(4)])  11.2 us
    all_to_all x2, starting transfers between devices, exchange(): lax.all_to_all(panels, 'grp', split_axis=0, concat_axis=0, tiled=True)  10.2 us
    pallas_call x1, Pallas kernels, finish(): pl.pallas_call(functools.partial(finish_kernel, 3), grid_spec=pltpu.Prefe...  8.94 us
    ppermute x8, starting transfers between devices, square(): to_x = lambda v: lax.ppermute(v, 'tp', [(i, i ^ 1) for i in range(4)])  7.39 us
    gather x2, local copies, waits for them, and re-layouts, chosen(): return jnp.take(panels, select, axis=0, mode='clip')  4.2 us
    dynamic_slice x1, local copies, waits for them, and re-layouts, part(): return lax.dynamic_slice(array, (0, start), (rows, size))  4.19 us
  transfers between devices with their start and end apart: 20, of which 7 were waited for; matrix products, arithmetic and copies ran while one was open for 6% of the time, Pallas kernels for 54%

profile of v6, /device:TPU:0, one launch (start us, length us, event | category | flops | bytes accessed | tf_op | source)
XLA Modules:
  0.0 164.3 jit_solution(4494593863449891150)
XLA Ops:
  0.0 3.0 %first_cuts.1 = (bf16[256,2048]{1,0:T(8,128)(2,1)}, bf16[256,2048]{1,0:T(8,128)(2,1)}) custom-call(s32[1]{0:T(128)} %bitcast.member_ref, bf16[256,8192]{1,0:T(8,128)(2,1)} %refs_0_.3), custom_call_target="tpu_custom_call" | custom-call | bytes 4194304 | tf_op jit(solution)/shard_map/first_cuts/pallas_call | solution.py:64
  3.1 3.0 %collective-permute-start.1 = (bf16[256,2048]{1,0:T(8,128)(2,1)}, bf16[256,2048]{1,0:T(8,128)(2,1)}, u32[]{:S(2)}, u32[]{:S(2)}) collective-permute-start(bf16[256,2048]{1,0:T(8,128)(2,1)} %get-tuple-element.50), channel_id=1, source_target_pairs={{0,1},{1,0},{2,3},{3,2},{4,5},{5,4},{6,7},{7,6},{8,9},{9,8},{10,11... | collective-permute-start | bytes 3145736 | tf_op jit(solution)/shard_map/ppermute | solution.py:284
  6.1 1.5 collective-permute-start.2
  7.6 4.2 %constant_dynamic-slice_fusion = (bf16[256,2048]{1,0:T(8,128)(2,1)}, bf16[256,2048]{1,0:T(8,128)(2,1)}) fusion(bf16[256,8192]{1,0:T(8,128)(2,1)} %refs_0_.3, s32[]{:T(128)S(6)} %select_n.42, s32[]{:T(128)S(6)} %select_n.41), kind=kLoop, calls=%fused_computation.25 | loop fusion | bytes 4194312 | tf_op jit(solution)/shard_map/dynamic_slice | solution.py:294
  11.8 0.5 collective-permute-start.5
  12.3 0.1 collective-permute-start
  12.4 0.1 select_reduce_fusion
  12.4 0.1 reduce_sum.31
  12.5 0.1 fusion.2
  12.7 2.0 %gather_fusion = bf16[8,64,2048]{2,1,0:T(8,128)(2,1)} fusion(bf16[4,64,2048]{2,1,0:T(8,128)(2,1)S(1)} %copy-done.4, s32[1024]{0:T(1024)S(1)} %pad_clamp_fusion.1), kind=kCustom, calls=%fused_computation | custom fusion | bytes 4194336 | tf_op jit(solution)/shard_map/jit(_take)/gather | solution.py:306
  14.7 5.3 %all-to-all-start = ((bf16[8,64,2048]{2,1,0:T(8,128)(2,1)}), bf16[8,64,2048]{2,1,0:T(8,128)(2,1)S(1)}, u32[]{:S(2)}, u32[]{:S(2)}) async-start(bf16[8,64,2048]{2,1,0:T(8,128)(2,1)} %gather_fusion), calls=%async_computation | async-start | bytes 4194304 | tf_op jit(solution)/shard_map/all_to_all | solution.py:309
  20.0 0.1 dynamic_slice.9
  20.1 0.1 broadcast_in_dim.53
  20.2 0.1 copy.8
  20.4 0.1 select_reduce_fusion.1
  20.5 0.1 copy.9
  20.6 0.1 reshape.37
  20.8 2.2 %copy-done.2 = bf16[256,8192]{1,0:T(8,128)(2,1)S(1)} copy-done((bf16[256,8192]{1,0:T(8,128)(2,1)S(1)}, bf16[256,8192]{1,0:T(8,128)(2,1)}, u32[]{:S(2)}) %copy-start.2) | copy-done | bytes 4194328
  23.0 21.2 %own_rows.1.refs_0_ = f32[1,256,2560]{2,1,0:T(8,128)} custom-call(s32[12]{0:T(128)S(1)} %pad_add_fusion.plan_ref, bf16[256,8192]{1,0:T(8,128)(2,1)S(1)} %copy-done.2, bf16[8192,2560]{1,0:T(8,128)(2,1)} %refs_3_.5, bf16[8192,2560]{1,0:T(8,128)(2,1)} %refs_3_.5, bf16[8192,2560]{1,0:T(8,128)(2,1)} %refs_3_.5, bf16[8192,2560]{1,0:T(8,128)(2,1)} %refs_3_.5), custom_call_target="tpu_custom_call" | custom-call | tf_op jit(solution)/shard_map/own_rows/pallas_call | solution.py:161
  44.1 1.6 collective-permute-start.4
  45.7 1.5 collective-permute-start.3
  47.2 7.7 %collective-permute-done.5.refs_3_ = bf16[256,2048]{1,0:T(8,128)(2,1)} collective-permute-done((bf16[256,2048]{1,0:T(8,128)(2,1)}, bf16[256,2048]{1,0:T(8,128)(2,1)}, u32[]{:S(2)}, u32[]{:S(2)}) %collective-permute-start.5) | collective-permute-done | bytes 1048608 | tf_op jit(solution)/shard_map/ppermute | solution.py:285
  55.0 2.0 %collective-permute-start.7 = (bf16[256,2048]{1,0:T(8,128)(2,1)}, bf16[256,2048]{1,0:T(8,128)(2,1)}, u32[]{:S(2)}, u32[]{:S(2)}) collective-permute-start(bf16[256,2048]{1,0:T(8,128)(2,1)} %collective-permute-done.1.refs_0_), channel_id=1, source_target_pairs={{0,2},{1,3},{2,0},{3,1},{4,6},{5,7},{6,4},{7,5},{8,10},{9,11},{10,... | collective-permute-start | bytes 3145736 | tf_op jit(solution)/shard_map/ppermute | solution.py:285
  57.0 17.3 %near_rows.1.refs_3_.refs_4_ = f32[2,256,2560]{2,1,0:T(8,128)} custom-call(s32[12]{0:T(128)S(1)} %pad_add_fusion.plan_ref, bf16[256,2048]{1,0:T(8,128)(2,1)} %collective-permute-done.1.refs_0_, bf16[256,2048]{1,0:T(8,128)(2,1)} %collective-permute-done.refs_1_, bf16[256,2048]{1,0:T(8,128)(2,1)} %collective-permute-done.2.refs_2_, ...), custom_call_target="tpu_custom_call" | custom-call | flops 64424509440 | bytes 283115520 | tf_op jit(solution)/shard_map/near_rows/pallas_call | solution.py:161
  74.3 2.2 %gather_fusion.1 = bf16[8,64,2560]{2,1,0:T(8,128)(2,1)} fusion(bf16[4,64,2560]{2,1,0:T(8,128)(2,1)S(1)} %copy-done, s32[1024]{0:T(1024)S(1)} %pad_clamp_fusion), kind=kCustom, calls=%fused_computation.1 | custom fusion | bytes 5242912 | tf_op jit(solution)/shard_map/jit(_take)/gather | solution.py:306
  76.5 4.9 %all-to-all-start.1 = ((bf16[8,64,2560]{2,1,0:T(8,128)(2,1)}), bf16[8,64,2560]{2,1,0:T(8,128)(2,1)}, u32[]{:S(2)}, u32[]{:S(2)}) async-start(bf16[8,64,2560]{2,1,0:T(8,128)(2,1)} %gather_fusion.1), calls=%async_computation.1 | async-start | bytes 5242880 | tf_op jit(solution)/shard_map/all_to_all | solution.py:309
  81.4 1.6 collective-permute-start.14
  83.0 0.5 collective-permute-start.15
  83.5 12.9 %near_rows_more.1.refs_3_.refs_4_ = f32[2,256,2560]{2,1,0:T(8,128)} custom-call(s32[12]{0:T(128)S(1)} %pad_add_fusion.plan_ref, bf16[256,2048]{1,0:T(8,128)(2,1)} %collective-permute-done.3.refs_0_.refs_1_, bf16[256,2048]{1,0:T(8,128)(2,1)} %collective-permute-done.4.refs_1_.refs_2_, bf16[8192,2560]{1,0:T(8,128)(2,1)} %refs_3_.5, ...), custom_call_target="tpu_custom_call" | custom-call | tf_op jit(solution)/shard_map/near_rows_more/pallas_call | solution.py:161
  96.4 1.3 collective-permute-done.6.refs_1_
  97.8 2.1 %collective-permute-done.7.refs_3_.refs_0_ = bf16[256,2048]{1,0:T(8,128)(2,1)} collective-permute-done((bf16[256,2048]{1,0:T(8,128)(2,1)}, bf16[256,2048]{1,0:T(8,128)(2,1)}, u32[]{:S(2)}, u32[]{:S(2)}) %collective-permute-start.7) | collective-permute-done | bytes 1048608 | tf_op jit(solution)/shard_map/ppermute | solution.py:285
  99.9 3.7 %shrink_parts.1 = (f32[128,128]{1,0:T(8,128)S(1)}, f32[128,128]{1,0:T(8,128)S(1)}, f32[128,128]{1,0:T(8,128)S(1)}, f32[128,128]{1,0:T(8,128)S(1)}) custom-call(s32[12]{0:T(128)S(1)} %pad_add_fusion.plan_ref, bf16[256,8192]{1,0:T(8,128)(2,1)S(1)} %copy-done.3, bf16[256,2048]{1,0:T(8,128)(2,1)} %collective-permute-done.3.refs_0_.refs_1_, ...), custom_call_target="tpu_custom_call" | custom-call | flops 1073741824 | bytes 6291456 | tf_op jit(solution)/shard_map/shrink_parts/pallas_call | solution.py:259
  103.6 0.1 collective-permute-start.8
  103.7 2.0 %collective-permute-start.9 = (f32[128,128]{1,0:T(8,128)S(1)}, f32[128,128]{1,0:T(8,128)S(1)}, u32[]{:S(2)}, u32[]{:S(2)}) collective-permute-start(f32[128,128]{1,0:T(8,128)S(1)} %get-tuple-element.42), channel_id=1, source_target_pairs={{0,2},{1,3},{2,0},{3,1},{4,6},{5,7},{6,4},{7,5},{8,10},{9,11},{10,... | collective-permute-start | bytes 196616 | tf_op jit(solution)/shard_map/ppermute | solution.py:285
  105.7 1.4 collective-permute-start.10
  107.1 13.0 %far_rows.1.refs_4_ = f32[1,256,2560]{2,1,0:T(8,128)} custom-call(s32[12]{0:T(128)S(1)} %pad_add_fusion.plan_ref, bf16[256,2048]{1,0:T(8,128)(2,1)} %collective-permute-done.7.refs_3_.refs_0_, bf16[256,2048]{1,0:T(8,128)(2,1)} %collective-permute-done.6.refs_1_, bf16[8192,2560]{1,0:T(8,128)(2,1)} %refs_3_.5, bf16[8192,2560]{1,0:T(8,128)(2,1)} %refs_3_.5), custom_call_target="tpu_custom_call" | custom-call | flops 21474836480 | bytes 94371840 | tf_op jit(solution)/shard_map/far_rows/pallas_call | solution.py:161
  120.2 1.3 collective-permute-done.8
  121.4 2.2 %collective-permute-done.9 = f32[128,128]{1,0:T(8,128)S(1)} collective-permute-done((f32[128,128]{1,0:T(8,128)S(1)}, f32[128,128]{1,0:T(8,128)S(1)}, u32[]{:S(2)}, u32[]{:S(2)}) %collective-permute-start.9) | collective-permute-done | bytes 65568 | tf_op jit(solution)/shard_map/ppermute | solution.py:285
  123.6 1.6 collective-permute-start.17
  125.2 0.5 collective-permute-start.16
  125.7 1.4 collective-permute-start.13
  127.2 1.5 collective-permute-start.11
  128.7 0.5 collective-permute-start.12
  129.2 11.8 %near_rows_rest.1.refs_1_ = f32[2,256,2560]{2,1,0:T(8,128)} custom-call(s32[12]{0:T(128)S(1)} %pad_add_fusion.plan_ref, bf16[256,2048]{1,0:T(8,128)(2,1)S(1)} %collective-permute-done.14.refs_0_, bf16[256,2048]{1,0:T(8,128)(2,1)S(1)} %collective-permute-done.15.refs_1_, bf16[8192,2560]{1,0:T(8,128)(2,1)} %refs_3_.5, ...), custom_call_target="tpu_custom_call" | custom-call | flops 21474836480 | bytes 125829120 | tf_op jit(solution)/shard_map/near_rows_rest/pallas_call | solution.py:161
  141.1 0.7 all-to-all-done.1.refs_5_.refs_6_.refs_7_
  141.8 8.9 %finish_rows.1.refs_8_ = bf16[1024,2560]{1,0:T(8,128)(2,1)} custom-call(s32[12]{0:T(128)S(1)} %pad_add_fusion.plan_ref, f32[1,256,2560]{2,1,0:T(8,128)} %own_rows.1.refs_0_, f32[2,256,2560]{2,1,0:T(8,128)} %near_rows_rest.1.refs_1_, bf16[128,128]{1,0:T(8,128)(2,1)S(1)} %add_convert_fusion.refs_2_, bf16[128,128]{1,0:T(8,128)(2,1)S(1)} %collective-permute-done.16.refs_3_, ...), custom_call_target="tpu_custom_call" | custom-call | flops 503316480 | bytes 11796480 | tf_op jit(solution)/shard_map/finish_rows/pallas_call | solution.py:204
  150.8 0.7 collective-permute-done.12.refs_1_
  151.5 12.8 %last_rows.1 = bf16[1024,2560]{1,0:T(8,128)(2,1)} custom-call(s32[12]{0:T(128)S(1)} %pad_add_fusion.plan_ref, bf16[256,2048]{1,0:T(8,128)(2,1)S(1)} %collective-permute-done.11.refs_0_, bf16[256,2048]{1,0:T(8,128)(2,1)S(1)} %collective-permute-done.12.refs_1_, bf16[8192,2560]{1,0:T(8,128)(2,1)} %refs_3_.5, ...), custom_call_target="tpu_custom_call", output_to_operand_aliasing={{}: (9, {})} | custom-call | flops 10737418240 | bytes 52428800 | tf_op jit(solution)/shard_map/last_rows/pallas_call | solution.py:161
  (34 shorter events, 0.3 us)
Async XLA Ops:
  0.0 74.3 %copy-start = (bf16[4,64,2560]{2,1,0:T(8,128)(2,1)S(1)}, bf16[4,64,2560]{2,1,0:T(8,128)(2,1)}, u32[]{:S(2)}) copy-start(bf16[4,64,2560]{2,1,0:T(8,128)(2,1)} %param.9) | copy-start | bytes 3932164
  3.0 9.3 %copy-start.5 = (s32[32]{0:T(128)S(1)}, s32[32]{0:T(128)}, u32[]{:S(2)}) copy-start(s32[32]{0:T(128)} %param.10) | copy-start | bytes 388
  3.0 9.3 %copy-start.6 = (s32[64]{0:T(128)S(1)}, s32[64]{0:T(128)}, u32[]{:S(2)}) copy-start(s32[64]{0:T(128)} %param.11) | copy-start | bytes 772
  3.0 9.6 %copy-start.4 = (bf16[4,64,2048]{2,1,0:T(8,128)(2,1)S(1)}, bf16[4,64,2048]{2,1,0:T(8,128)(2,1)}, u32[]{:S(2)}) copy-start(bf16[4,64,2048]{2,1,0:T(8,128)(2,1)} %param.8) | copy-start | bytes 3145732
  3.1 41.1 %collective-permute-start.1 = (bf16[256,2048]{1,0:T(8,128)(2,1)}, bf16[256,2048]{1,0:T(8,128)(2,1)}, u32[]{:S(2)}, u32[]{:S(2)}) collective-permute-start(bf16[256,2048]{1,0:T(8,128)(2,1)} %get-tuple-element.50), channel_id=1, source_target_pairs={{0,1},{1,0},{2,3},{3,2},{4,5},{5,4},{6,7},{7,6},{8,9},{9,8},{10,11... | collective-permute-start | bytes 3145736 | tf_op jit(solution)/shard_map/ppermute | solution.py:284
  6.1 38.1 %collective-permute-start.2 = (bf16[256,2048]{1,0:T(8,128)(2,1)}, bf16[256,2048]{1,0:T(8,128)(2,1)}, u32[]{:S(2)}, u32[]{:S(2)}) collective-permute-start(bf16[256,2048]{1,0:T(8,128)(2,1)} %get-tuple-element.49), channel_id=1, source_target_pairs={{0,2},{1,3},{2,0},{3,1},{4,6},{5,7},{6,4},{7,5},{8,10},{9,11},{10,... | collective-permute-start | bytes 3145736 | tf_op jit(solution)/shard_map/ppermute | solution.py:285
  11.8 43.2 %collective-permute-start.5 = (bf16[256,2048]{1,0:T(8,128)(2,1)}, bf16[256,2048]{1,0:T(8,128)(2,1)}, u32[]{:S(2)}, u32[]{:S(2)}) collective-permute-start(bf16[256,2048]{1,0:T(8,128)(2,1)} %get-tuple-element.32), channel_id=1, source_target_pairs={{0,2},{1,3},{2,0},{3,1},{4,6},{5,7},{6,4},{7,5},{8,10},{9,11},{10,... | collective-permute-start | bytes 3145736 | tf_op jit(solution)/shard_map/ppermute | solution.py:285
  12.3 42.7 %collective-permute-start = (bf16[256,2048]{1,0:T(8,128)(2,1)}, bf16[256,2048]{1,0:T(8,128)(2,1)}, u32[]{:S(2)}, u32[]{:S(2)}) collective-permute-start(bf16[256,2048]{1,0:T(8,128)(2,1)} %get-tuple-element.33), channel_id=1, source_target_pairs={{0,1},{1,0},{2,3},{3,2},{4,5},{5,4},{6,7},{7,6},{8,9},{9,8},{10,11... | collective-permute-start | bytes 3145736 | tf_op jit(solution)/shard_map/ppermute | solution.py:284
  14.7 59.6 %all-to-all-start = ((bf16[8,64,2048]{2,1,0:T(8,128)(2,1)}), bf16[8,64,2048]{2,1,0:T(8,128)(2,1)S(1)}, u32[]{:S(2)}, u32[]{:S(2)}) async-start(bf16[8,64,2048]{2,1,0:T(8,128)(2,1)} %gather_fusion), calls=%async_computation | async-start | bytes 4194304 | tf_op jit(solution)/shard_map/all_to_all | solution.py:309
  20.8 2.2 %copy-start.2 = (bf16[256,8192]{1,0:T(8,128)(2,1)S(1)}, bf16[256,8192]{1,0:T(8,128)(2,1)}, u32[]{:S(2)}) copy-start(bf16[256,8192]{1,0:T(8,128)(2,1)} %refs_0_.3) | copy-start | bytes 12582916
  44.1 37.3 %collective-permute-start.4 = (bf16[256,2048]{1,0:T(8,128)(2,1)}, bf16[256,2048]{1,0:T(8,128)(2,1)}, u32[]{:S(2)}, u32[]{:S(2)}) collective-permute-start(bf16[256,2048]{1,0:T(8,128)(2,1)} %get-tuple-element.33), channel_id=1, source_target_pairs={{0,2},{1,3},{2,0},{3,1},{4,6},{5,7},{6,4},{7,5},{8,10},{9,11},{10,... | collective-permute-start | bytes 3145736 | tf_op jit(solution)/shard_map/ppermute | solution.py:285
  45.7 35.7 %collective-permute-start.3 = (bf16[256,2048]{1,0:T(8,128)(2,1)}, bf16[256,2048]{1,0:T(8,128)(2,1)}, u32[]{:S(2)}, u32[]{:S(2)}) collective-permute-start(bf16[256,2048]{1,0:T(8,128)(2,1)} %get-tuple-element.32), channel_id=1, source_target_pairs={{0,1},{1,0},{2,3},{3,2},{4,5},{5,4},{6,7},{7,6},{8,9},{9,8},{10,11... | collective-permute-start | bytes 3145736 | tf_op jit(solution)/shard_map/ppermute | solution.py:284
  54.9 42.8 %collective-permute-start.6 = (bf16[256,2048]{1,0:T(8,128)(2,1)}, bf16[256,2048]{1,0:T(8,128)(2,1)}, u32[]{:S(2)}, u32[]{:S(2)}) collective-permute-start(bf16[256,2048]{1,0:T(8,128)(2,1)} %collective-permute-done.2.refs_2_), channel_id=1, source_target_pairs={{0,1},{1,0},{2,3},{3,2},{4,5},{5,4},{6,7},{7,6},{8,9},{9,8},{10,11... | collective-permute-start | bytes 3145736 | tf_op jit(solution)/shard_map/ppermute | solution.py:284
  55.0 44.9 %collective-permute-start.7 = (bf16[256,2048]{1,0:T(8,128)(2,1)}, bf16[256,2048]{1,0:T(8,128)(2,1)}, u32[]{:S(2)}, u32[]{:S(2)}) collective-permute-start(bf16[256,2048]{1,0:T(8,128)(2,1)} %collective-permute-done.1.refs_0_), channel_id=1, source_target_pairs={{0,2},{1,3},{2,0},{3,1},{4,6},{5,7},{6,4},{7,5},{8,10},{9,11},{10,... | collective-permute-start | bytes 3145736 | tf_op jit(solution)/shard_map/ppermute | solution.py:285
  76.5 65.3 %all-to-all-start.1 = ((bf16[8,64,2560]{2,1,0:T(8,128)(2,1)}), bf16[8,64,2560]{2,1,0:T(8,128)(2,1)}, u32[]{:S(2)}, u32[]{:S(2)}) async-start(bf16[8,64,2560]{2,1,0:T(8,128)(2,1)} %gather_fusion.1), calls=%async_computation.1 | async-start | bytes 5242880 | tf_op jit(solution)/shard_map/all_to_all | solution.py:309
  81.4 45.7 %collective-permute-start.14 = (bf16[256,2048]{1,0:T(8,128)(2,1)}, bf16[256,2048]{1,0:T(8,128)(2,1)S(1)}, u32[]{:S(2)}, u32[]{:S(2)}) collective-permute-start(bf16[256,2048]{1,0:T(8,128)(2,1)} %get-tuple-element.49), channel_id=1, source_target_pairs={{0,1},{1,0},{2,3},{3,2},{4,5},{5,4},{6,7},{7,6},{8,9},{9,8},{10,11... | collective-permute-start | bytes 3145736 | tf_op jit(solution)/shard_map/ppermute | solution.py:284
  83.0 45.7 %collective-permute-start.15 = (bf16[256,2048]{1,0:T(8,128)(2,1)}, bf16[256,2048]{1,0:T(8,128)(2,1)S(1)}, u32[]{:S(2)}, u32[]{:S(2)}) collective-permute-start(bf16[256,2048]{1,0:T(8,128)(2,1)} %get-tuple-element.50), channel_id=1, source_target_pairs={{0,2},{1,3},{2,0},{3,1},{4,6},{5,7},{6,4},{7,5},{8,10},{9,11},{10,... | collective-permute-start | bytes 3145736 | tf_op jit(solution)/shard_map/ppermute | solution.py:285
  83.5 16.4 %copy-start.3 = (bf16[256,8192]{1,0:T(8,128)(2,1)S(1)}, bf16[256,8192]{1,0:T(8,128)(2,1)}, u32[]{:S(2)}) copy-start(bf16[256,8192]{1,0:T(8,128)(2,1)} %refs_0_.3) | copy-start | bytes 12582916
  103.6 17.8 %collective-permute-start.8 = (f32[128,128]{1,0:T(8,128)S(1)}, f32[128,128]{1,0:T(8,128)S(1)}, u32[]{:S(2)}, u32[]{:S(2)}) collective-permute-start(f32[128,128]{1,0:T(8,128)S(1)} %get-tuple-element.41), channel_id=1, source_target_pairs={{0,1},{1,0},{2,3},{3,2},{4,5},{5,4},{6,7},{7,6},{8,9},{9,8},{10,11... | collective-permute-start | bytes 196616 | tf_op jit(solution)/shard_map/ppermute | solution.py:284
  103.7 19.9 %collective-permute-start.9 = (f32[128,128]{1,0:T(8,128)S(1)}, f32[128,128]{1,0:T(8,128)S(1)}, u32[]{:S(2)}, u32[]{:S(2)}) collective-permute-start(f32[128,128]{1,0:T(8,128)S(1)} %get-tuple-element.42), channel_id=1, source_target_pairs={{0,2},{1,3},{2,0},{3,1},{4,6},{5,7},{6,4},{7,5},{8,10},{9,11},{10,... | collective-permute-start | bytes 196616 | tf_op jit(solution)/shard_map/ppermute | solution.py:285
  105.7 17.9 %collective-permute-start.10 = (f32[128,128]{1,0:T(8,128)S(1)}, f32[128,128]{1,0:T(8,128)S(1)}, u32[]{:S(2)}, u32[]{:S(2)}) collective-permute-start(f32[128,128]{1,0:T(8,128)S(1)} %get-tuple-element.43), channel_id=1, source_target_pairs={{0,3},{1,2},{2,1},{3,0},{4,7},{5,6},{6,5},{7,4},{8,11},{9,10},{10,... | collective-permute-start | bytes 196616 | tf_op jit(solution)/shard_map/ppermute | solution.py:286
  123.6 17.5 %collective-permute-start.17 = (bf16[128,128]{1,0:T(8,128)(2,1)S(1)}, bf16[128,128]{1,0:T(8,128)(2,1)S(1)}, u32[]{:S(2)}, u32[]{:S(2)}) collective-permute-start(bf16[128,128]{1,0:T(8,128)(2,1)S(1)} %add_convert_fusion.refs_2_), channel_id=1, source_target_pairs={{0,2},{1,3},{2,0},{3,1},{4,6},{5,7},{6,4},{7,5},{8,10},{9,11},{10,... | collective-permute-start | bytes 98312 | tf_op jit(solution)/shard_map/ppermute | solution.py:285
  125.2 15.9 %collective-permute-start.16 = (bf16[128,128]{1,0:T(8,128)(2,1)S(1)}, bf16[128,128]{1,0:T(8,128)(2,1)S(1)}, u32[]{:S(2)}, u32[]{:S(2)}) collective-permute-start(bf16[128,128]{1,0:T(8,128)(2,1)S(1)} %add_convert_fusion.refs_2_), channel_id=1, source_target_pairs={{0,1},{1,0},{2,3},{3,2},{4,5},{5,4},{6,7},{7,6},{8,9},{9,8},{10,11... | collective-permute-start | bytes 98312 | tf_op jit(solution)/shard_map/ppermute | solution.py:284
  125.7 25.0 %collective-permute-start.13 = (bf16[128,128]{1,0:T(8,128)(2,1)S(1)}, bf16[128,128]{1,0:T(8,128)(2,1)S(1)}, u32[]{:S(2)}, u32[]{:S(2)}) collective-permute-start(bf16[128,128]{1,0:T(8,128)(2,1)S(1)} %add_convert_fusion.refs_2_), channel_id=1, source_target_pairs={{0,3},{1,2},{2,1},{3,0},{4,7},{5,6},{6,5},{7,4},{8,11},{9,10},{10,... | collective-permute-start | bytes 98312 | tf_op jit(solution)/shard_map/ppermute | solution.py:286
  127.2 23.6 %collective-permute-start.11 = (bf16[256,2048]{1,0:T(8,128)(2,1)}, bf16[256,2048]{1,0:T(8,128)(2,1)S(1)}, u32[]{:S(2)}, u32[]{:S(2)}) collective-permute-start(bf16[256,2048]{1,0:T(8,128)(2,1)} %collective-permute-done.refs_1_), channel_id=1, source_target_pairs={{0,2},{1,3},{2,0},{3,1},{4,6},{5,7},{6,4},{7,5},{8,10},{9,11},{10,... | collective-permute-start | bytes 3145736 | tf_op jit(solution)/shard_map/ppermute | solution.py:285
  128.7 22.8 %collective-permute-start.12 = (bf16[256,2048]{1,0:T(8,128)(2,1)}, bf16[256,2048]{1,0:T(8,128)(2,1)S(1)}, u32[]{:S(2)}, u32[]{:S(2)}) collective-permute-start(bf16[256,2048]{1,0:T(8,128)(2,1)} %collective-permute-done.5.refs_3_), channel_id=1, source_target_pairs={{0,1},{1,0},{2,3},{3,2},{4,5},{5,4},{6,7},{7,6},{8,9},{9,8},{10,11... | collective-permute-start | bytes 3145736 | tf_op jit(solution)/shard_map/ppermute | solution.py:284
  151.5 12.8 %copy-start.1 = (bf16[4,64,2560]{2,1,0:T(8,128)(2,1)S(1)}, bf16[4,64,2560]{2,1,0:T(8,128)(2,1)}, u32[]{:S(2)}) copy-start(bf16[4,64,2560]{2,1,0:T(8,128)(2,1)} %param.9) | copy-start | bytes 3932164

commit v7 on v6

--- a/solution.py
+++ b/solution.py
@@ -41,9 +41,7 @@
 
 
 def view(ref, at):
-    if at is None:
-        return ref[...]
-    return ref[:, at[0] : at[1]] if isinstance(at, tuple) else ref[at]
+    return ref[...] if at is None else ref[:, at[0] : at[1]]
 
 
 def cut_kernel(member_ref, tokens_ref, far_ref, own_ref, sems):
@@ -409,7 +407,7 @@
     offsets = slot_numbers % loaded_here
     owned_here = owners.reshape(group_count, -1) == group
     select_slot = jnp.sum(jnp.where(owned_here, offsets.reshape(group_count, -1), 0), axis=1)
-    fits = lax.axis_size("tp") == 4 and tokens.shape[0] % BLOCK == 0
+    fits = lax.axis_size("tp") == 4 and tokens.shape[0] == 2 * BLOCK
     way = square if fits else general
     return way(tokens, frozen_weight, down_weight, up_weight, owners, select_slot)
 

time: 165 us -> 165 us (level)
  no operation moved by 1% of the time
where the time goes in v7:
time: 165 us; the launch traced here: 164 us
  Pallas kernels  105 us (64%)
  starting transfers between devices  31.7 us (19%)
  waiting for transfers between devices  16.1 us (10%)
  local copies, waits for them, and re-layouts  11.1 us (7%)
    pallas_call x6, Pallas kernels, project(): pl.pallas_call(functools.partial(project_kernel, flat, weights_at, totals...  89.1 us
    ppermute x8, waiting for transfers between devices, square(): to_y = lambda v: lax.ppermute(v, 'tp', [(i, i ^ 2) for i in range(4)])  12 us
    ppermute x8, starting transfers between devices, square(): to_y = lambda v: lax.ppermute(v, 'tp', [(i, i ^ 2) for i in range(4)])  11.2 us
    all_to_all x2, starting transfers between devices, exchange(): lax.all_to_all(panels, 'grp', split_axis=0, concat_axis=0, tiled=True)  10.2 us
    pallas_call x1, Pallas kernels, finish(): pl.pallas_call(functools.partial(finish_kernel, 3), grid_spec=pltpu.Prefe...  8.91 us
    ppermute x8, starting transfers between devices, square(): to_x = lambda v: lax.ppermute(v, 'tp', [(i, i ^ 1) for i in range(4)])  7.39 us
    gather x2, local copies, waits for them, and re-layouts, chosen(): return jnp.take(panels, select, axis=0, mode='clip')  4.2 us
    dynamic_slice x1, local copies, waits for them, and re-layouts, part(): return lax.dynamic_slice(array, (0, start), (rows, size))  4.19 us
  transfers between devices with their start and end apart: 20, of which 7 were waited for; matrix products, arithmetic and copies ran while one was open for 6% of the time, Pallas kernels for 54%

profile of v7, /device:TPU:0, one launch (start us, length us, event | category | flops | bytes accessed | tf_op | source)
XLA Modules:
  0.0 164.3 jit_solution(4494593863449891150)
XLA Ops:
  0.0 3.0 %first_cuts.1 = (bf16[256,2048]{1,0:T(8,128)(2,1)}, bf16[256,2048]{1,0:T(8,128)(2,1)}) custom-call(s32[1]{0:T(128)} %bitcast.member_ref, bf16[256,8192]{1,0:T(8,128)(2,1)} %refs_0_.3), custom_call_target="tpu_custom_call" | custom-call | bytes 4194304 | tf_op jit(solution)/shard_map/first_cuts/pallas_call | solution.py:62
  3.1 3.0 %collective-permute-start.1 = (bf16[256,2048]{1,0:T(8,128)(2,1)}, bf16[256,2048]{1,0:T(8,128)(2,1)}, u32[]{:S(2)}, u32[]{:S(2)}) collective-permute-start(bf16[256,2048]{1,0:T(8,128)(2,1)} %get-tuple-element.50), channel_id=1, source_target_pairs={{0,1},{1,0},{2,3},{3,2},{4,5},{5,4},{6,7},{7,6},{8,9},{9,8},{10,11... | collective-permute-start | bytes 3145736 | tf_op jit(solution)/shard_map/ppermute | solution.py:282
  6.1 1.5 collective-permute-start.2
  7.6 4.2 %constant_dynamic-slice_fusion = (bf16[256,2048]{1,0:T(8,128)(2,1)}, bf16[256,2048]{1,0:T(8,128)(2,1)}) fusion(bf16[256,8192]{1,0:T(8,128)(2,1)} %refs_0_.3, s32[]{:T(128)S(6)} %select_n.42, s32[]{:T(128)S(6)} %select_n.41), kind=kLoop, calls=%fused_computation.25 | loop fusion | bytes 4194312 | tf_op jit(solution)/shard_map/dynamic_slice | solution.py:292
  11.8 0.5 collective-permute-start.5
  12.3 0.1 collective-permute-start
  12.4 0.1 select_reduce_fusion
  12.4 0.1 reduce_sum.31
  12.5 0.1 fusion.2
  12.7 2.0 %gather_fusion = bf16[8,64,2048]{2,1,0:T(8,128)(2,1)} fusion(bf16[4,64,2048]{2,1,0:T(8,128)(2,1)S(1)} %copy-done.4, s32[1024]{0:T(1024)S(1)} %pad_clamp_fusion.1), kind=kCustom, calls=%fused_computation | custom fusion | bytes 4194336 | tf_op jit(solution)/shard_map/jit(_take)/gather | solution.py:304
  14.7 5.3 %all-to-all-start = ((bf16[8,64,2048]{2,1,0:T(8,128)(2,1)}), bf16[8,64,2048]{2,1,0:T(8,128)(2,1)S(1)}, u32[]{:S(2)}, u32[]{:S(2)}) async-start(bf16[8,64,2048]{2,1,0:T(8,128)(2,1)} %gather_fusion), calls=%async_computation | async-start | bytes 4194304 | tf_op jit(solution)/shard_map/all_to_all | solution.py:307
  20.0 0.1 dynamic_slice.9
  20.1 0.1 broadcast_in_dim.53
  20.2 0.1 copy.8
  20.4 0.1 select_reduce_fusion.1
  20.5 0.1 copy.9
  20.6 0.1 reshape.37
  20.8 2.2 %copy-done.2 = bf16[256,8192]{1,0:T(8,128)(2,1)S(1)} copy-done((bf16[256,8192]{1,0:T(8,128)(2,1)S(1)}, bf16[256,8192]{1,0:T(8,128)(2,1)}, u32[]{:S(2)}) %copy-start.2) | copy-done | bytes 4194328
  23.0 21.2 %own_rows.1.refs_0_ = f32[1,256,2560]{2,1,0:T(8,128)} custom-call(s32[12]{0:T(128)S(1)} %pad_add_fusion.plan_ref, bf16[256,8192]{1,0:T(8,128)(2,1)S(1)} %copy-done.2, bf16[8192,2560]{1,0:T(8,128)(2,1)} %refs_3_.5, bf16[8192,2560]{1,0:T(8,128)(2,1)} %refs_3_.5, bf16[8192,2560]{1,0:T(8,128)(2,1)} %refs_3_.5, bf16[8192,2560]{1,0:T(8,128)(2,1)} %refs_3_.5), custom_call_target="tpu_custom_call" | custom-call | tf_op jit(solution)/shard_map/own_rows/pallas_call | solution.py:159
  44.1 1.6 collective-permute-start.4
  45.7 1.5 collective-permute-start.3
  47.2 7.7 %collective-permute-done.5.refs_3_ = bf16[256,2048]{1,0:T(8,128)(2,1)} collective-permute-done((bf16[256,2048]{1,0:T(8,128)(2,1)}, bf16[256,2048]{1,0:T(8,128)(2,1)}, u32[]{:S(2)}, u32[]{:S(2)}) %collective-permute-start.5) | collective-permute-done | bytes 1048608 | tf_op jit(solution)/shard_map/ppermute | solution.py:283
  55.0 2.0 %collective-permute-start.7 = (bf16[256,2048]{1,0:T(8,128)(2,1)}, bf16[256,2048]{1,0:T(8,128)(2,1)}, u32[]{:S(2)}, u32[]{:S(2)}) collective-permute-start(bf16[256,2048]{1,0:T(8,128)(2,1)} %collective-permute-done.1.refs_0_), channel_id=1, source_target_pairs={{0,2},{1,3},{2,0},{3,1},{4,6},{5,7},{6,4},{7,5},{8,10},{9,11},{10,... | collective-permute-start | bytes 3145736 | tf_op jit(solution)/shard_map/ppermute | solution.py:283
  57.0 17.3 %near_rows.1.refs_3_.refs_4_ = f32[2,256,2560]{2,1,0:T(8,128)} custom-call(s32[12]{0:T(128)S(1)} %pad_add_fusion.plan_ref, bf16[256,2048]{1,0:T(8,128)(2,1)} %collective-permute-done.1.refs_0_, bf16[256,2048]{1,0:T(8,128)(2,1)} %collective-permute-done.refs_1_, bf16[256,2048]{1,0:T(8,128)(2,1)} %collective-permute-done.2.refs_2_, ...), custom_call_target="tpu_custom_call" | custom-call | flops 64424509440 | bytes 283115520 | tf_op jit(solution)/shard_map/near_rows/pallas_call | solution.py:159
  74.3 2.2 %gather_fusion.1 = bf16[8,64,2560]{2,1,0:T(8,128)(2,1)} fusion(bf16[4,64,2560]{2,1,0:T(8,128)(2,1)S(1)} %copy-done, s32[1024]{0:T(1024)S(1)} %pad_clamp_fusion), kind=kCustom, calls=%fused_computation.1 | custom fusion | bytes 5242912 | tf_op jit(solution)/shard_map/jit(_take)/gather | solution.py:304
  76.5 4.9 %all-to-all-start.1 = ((bf16[8,64,2560]{2,1,0:T(8,128)(2,1)}), bf16[8,64,2560]{2,1,0:T(8,128)(2,1)}, u32[]{:S(2)}, u32[]{:S(2)}) async-start(bf16[8,64,2560]{2,1,0:T(8,128)(2,1)} %gather_fusion.1), calls=%async_computation.1 | async-start | bytes 5242880 | tf_op jit(solution)/shard_map/all_to_all | solution.py:307
  81.4 1.6 collective-permute-start.14
  83.0 0.5 collective-permute-start.15
  83.5 12.9 %near_rows_more.1.refs_3_.refs_4_ = f32[2,256,2560]{2,1,0:T(8,128)} custom-call(s32[12]{0:T(128)S(1)} %pad_add_fusion.plan_ref, bf16[256,2048]{1,0:T(8,128)(2,1)} %collective-permute-done.3.refs_0_.refs_1_, bf16[256,2048]{1,0:T(8,128)(2,1)} %collective-permute-done.4.refs_1_.refs_2_, bf16[8192,2560]{1,0:T(8,128)(2,1)} %refs_3_.5, ...), custom_call_target="tpu_custom_call" | custom-call | tf_op jit(solution)/shard_map/near_rows_more/pallas_call | solution.py:159
  96.4 1.3 collective-permute-done.6.refs_1_
  97.8 2.1 %collective-permute-done.7.refs_3_.refs_0_ = bf16[256,2048]{1,0:T(8,128)(2,1)} collective-permute-done((bf16[256,2048]{1,0:T(8,128)(2,1)}, bf16[256,2048]{1,0:T(8,128)(2,1)}, u32[]{:S(2)}, u32[]{:S(2)}) %collective-permute-start.7) | collective-permute-done | bytes 1048608 | tf_op jit(solution)/shard_map/ppermute | solution.py:283
  99.9 3.7 %shrink_parts.1 = (f32[128,128]{1,0:T(8,128)S(1)}, f32[128,128]{1,0:T(8,128)S(1)}, f32[128,128]{1,0:T(8,128)S(1)}, f32[128,128]{1,0:T(8,128)S(1)}) custom-call(s32[12]{0:T(128)S(1)} %pad_add_fusion.plan_ref, bf16[256,8192]{1,0:T(8,128)(2,1)S(1)} %copy-done.3, bf16[256,2048]{1,0:T(8,128)(2,1)} %collective-permute-done.3.refs_0_.refs_1_, ...), custom_call_target="tpu_custom_call" | custom-call | flops 1073741824 | bytes 6291456 | tf_op jit(solution)/shard_map/shrink_parts/pallas_call | solution.py:257
  103.6 0.1 collective-permute-start.8
  103.7 2.0 %collective-permute-start.9 = (f32[128,128]{1,0:T(8,128)S(1)}, f32[128,128]{1,0:T(8,128)S(1)}, u32[]{:S(2)}, u32[]{:S(2)}) collective-permute-start(f32[128,128]{1,0:T(8,128)S(1)} %get-tuple-element.42), channel_id=1, source_target_pairs={{0,2},{1,3},{2,0},{3,1},{4,6},{5,7},{6,4},{7,5},{8,10},{9,11},{10,... | collective-permute-start | bytes 196616 | tf_op jit(solution)/shard_map/ppermute | solution.py:283
  105.7 1.4 collective-permute-start.10
  107.1 13.0 %far_rows.1.refs_4_ = f32[1,256,2560]{2,1,0:T(8,128)} custom-call(s32[12]{0:T(128)S(1)} %pad_add_fusion.plan_ref, bf16[256,2048]{1,0:T(8,128)(2,1)} %collective-permute-done.7.refs_3_.refs_0_, bf16[256,2048]{1,0:T(8,128)(2,1)} %collective-permute-done.6.refs_1_, bf16[8192,2560]{1,0:T(8,128)(2,1)} %refs_3_.5, bf16[8192,2560]{1,0:T(8,128)(2,1)} %refs_3_.5), custom_call_target="tpu_custom_call" | custom-call | flops 21474836480 | bytes 94371840 | tf_op jit(solution)/shard_map/far_rows/pallas_call | solution.py:159
  120.2 1.3 collective-permute-done.8
  121.4 2.2 %collective-permute-done.9 = f32[128,128]{1,0:T(8,128)S(1)} collective-permute-done((f32[128,128]{1,0:T(8,128)S(1)}, f32[128,128]{1,0:T(8,128)S(1)}, u32[]{:S(2)}, u32[]{:S(2)}) %collective-permute-start.9) | collective-permute-done | bytes 65568 | tf_op jit(solution)/shard_map/ppermute | solution.py:283
  123.6 1.6 collective-permute-start.17
  125.2 0.5 collective-permute-start.16
  125.7 1.4 collective-permute-start.13
  127.2 1.5 collective-permute-start.11
  128.7 0.5 collective-permute-start.12
  129.2 11.8 %near_rows_rest.1.refs_1_ = f32[2,256,2560]{2,1,0:T(8,128)} custom-call(s32[12]{0:T(128)S(1)} %pad_add_fusion.plan_ref, bf16[256,2048]{1,0:T(8,128)(2,1)S(1)} %collective-permute-done.14.refs_0_, bf16[256,2048]{1,0:T(8,128)(2,1)S(1)} %collective-permute-done.15.refs_1_, bf16[8192,2560]{1,0:T(8,128)(2,1)} %refs_3_.5, ...), custom_call_target="tpu_custom_call" | custom-call | flops 21474836480 | bytes 125829120 | tf_op jit(solution)/shard_map/near_rows_rest/pallas_call | solution.py:159
  141.1 0.7 all-to-all-done.1.refs_5_.refs_6_.refs_7_
  141.8 8.9 %finish_rows.1.refs_8_ = bf16[1024,2560]{1,0:T(8,128)(2,1)} custom-call(s32[12]{0:T(128)S(1)} %pad_add_fusion.plan_ref, f32[1,256,2560]{2,1,0:T(8,128)} %own_rows.1.refs_0_, f32[2,256,2560]{2,1,0:T(8,128)} %near_rows_rest.1.refs_1_, bf16[128,128]{1,0:T(8,128)(2,1)S(1)} %add_convert_fusion.refs_2_, bf16[128,128]{1,0:T(8,128)(2,1)S(1)} %collective-permute-done.16.refs_3_, ...), custom_call_target="tpu_custom_call" | custom-call | flops 503316480 | bytes 11796480 | tf_op jit(solution)/shard_map/finish_rows/pallas_call | solution.py:202
  150.7 0.8 collective-permute-done.12.refs_1_
  151.5 12.8 %last_rows.1 = bf16[1024,2560]{1,0:T(8,128)(2,1)} custom-call(s32[12]{0:T(128)S(1)} %pad_add_fusion.plan_ref, bf16[256,2048]{1,0:T(8,128)(2,1)S(1)} %collective-permute-done.11.refs_0_, bf16[256,2048]{1,0:T(8,128)(2,1)S(1)} %collective-permute-done.12.refs_1_, bf16[8192,2560]{1,0:T(8,128)(2,1)} %refs_3_.5, ...), custom_call_target="tpu_custom_call", output_to_operand_aliasing={{}: (9, {})} | custom-call | flops 10737418240 | bytes 52428800 | tf_op jit(solution)/shard_map/last_rows/pallas_call | solution.py:159
  (34 shorter events, 0.3 us)
Async XLA Ops:
  0.0 74.3 %copy-start = (bf16[4,64,2560]{2,1,0:T(8,128)(2,1)S(1)}, bf16[4,64,2560]{2,1,0:T(8,128)(2,1)}, u32[]{:S(2)}) copy-start(bf16[4,64,2560]{2,1,0:T(8,128)(2,1)} %param.9) | copy-start | bytes 3932164
  3.0 9.3 %copy-start.5 = (s32[32]{0:T(128)S(1)}, s32[32]{0:T(128)}, u32[]{:S(2)}) copy-start(s32[32]{0:T(128)} %param.10) | copy-start | bytes 388
  3.0 9.3 %copy-start.6 = (s32[64]{0:T(128)S(1)}, s32[64]{0:T(128)}, u32[]{:S(2)}) copy-start(s32[64]{0:T(128)} %param.11) | copy-start | bytes 772
  3.0 9.6 %copy-start.4 = (bf16[4,64,2048]{2,1,0:T(8,128)(2,1)S(1)}, bf16[4,64,2048]{2,1,0:T(8,128)(2,1)}, u32[]{:S(2)}) copy-start(bf16[4,64,2048]{2,1,0:T(8,128)(2,1)} %param.8) | copy-start | bytes 3145732
  3.1 41.1 %collective-permute-start.1 = (bf16[256,2048]{1,0:T(8,128)(2,1)}, bf16[256,2048]{1,0:T(8,128)(2,1)}, u32[]{:S(2)}, u32[]{:S(2)}) collective-permute-start(bf16[256,2048]{1,0:T(8,128)(2,1)} %get-tuple-element.50), channel_id=1, source_target_pairs={{0,1},{1,0},{2,3},{3,2},{4,5},{5,4},{6,7},{7,6},{8,9},{9,8},{10,11... | collective-permute-start | bytes 3145736 | tf_op jit(solution)/shard_map/ppermute | solution.py:282
  6.1 38.1 %collective-permute-start.2 = (bf16[256,2048]{1,0:T(8,128)(2,1)}, bf16[256,2048]{1,0:T(8,128)(2,1)}, u32[]{:S(2)}, u32[]{:S(2)}) collective-permute-start(bf16[256,2048]{1,0:T(8,128)(2,1)} %get-tuple-element.49), channel_id=1, source_target_pairs={{0,2},{1,3},{2,0},{3,1},{4,6},{5,7},{6,4},{7,5},{8,10},{9,11},{10,... | collective-permute-start | bytes 3145736 | tf_op jit(solution)/shard_map/ppermute | solution.py:283
  11.8 43.2 %collective-permute-start.5 = (bf16[256,2048]{1,0:T(8,128)(2,1)}, bf16[256,2048]{1,0:T(8,128)(2,1)}, u32[]{:S(2)}, u32[]{:S(2)}) collective-permute-start(bf16[256,2048]{1,0:T(8,128)(2,1)} %get-tuple-element.32), channel_id=1, source_target_pairs={{0,2},{1,3},{2,0},{3,1},{4,6},{5,7},{6,4},{7,5},{8,10},{9,11},{10,... | collective-permute-start | bytes 3145736 | tf_op jit(solution)/shard_map/ppermute | solution.py:283
  12.3 42.7 %collective-permute-start = (bf16[256,2048]{1,0:T(8,128)(2,1)}, bf16[256,2048]{1,0:T(8,128)(2,1)}, u32[]{:S(2)}, u32[]{:S(2)}) collective-permute-start(bf16[256,2048]{1,0:T(8,128)(2,1)} %get-tuple-element.33), channel_id=1, source_target_pairs={{0,1},{1,0},{2,3},{3,2},{4,5},{5,4},{6,7},{7,6},{8,9},{9,8},{10,11... | collective-permute-start | bytes 3145736 | tf_op jit(solution)/shard_map/ppermute | solution.py:282
  14.7 59.6 %all-to-all-start = ((bf16[8,64,2048]{2,1,0:T(8,128)(2,1)}), bf16[8,64,2048]{2,1,0:T(8,128)(2,1)S(1)}, u32[]{:S(2)}, u32[]{:S(2)}) async-start(bf16[8,64,2048]{2,1,0:T(8,128)(2,1)} %gather_fusion), calls=%async_computation | async-start | bytes 4194304 | tf_op jit(solution)/shard_map/all_to_all | solution.py:307
  20.8 2.2 %copy-start.2 = (bf16[256,8192]{1,0:T(8,128)(2,1)S(1)}, bf16[256,8192]{1,0:T(8,128)(2,1)}, u32[]{:S(2)}) copy-start(bf16[256,8192]{1,0:T(8,128)(2,1)} %refs_0_.3) | copy-start | bytes 12582916
  44.1 37.3 %collective-permute-start.4 = (bf16[256,2048]{1,0:T(8,128)(2,1)}, bf16[256,2048]{1,0:T(8,128)(2,1)}, u32[]{:S(2)}, u32[]{:S(2)}) collective-permute-start(bf16[256,2048]{1,0:T(8,128)(2,1)} %get-tuple-element.33), channel_id=1, source_target_pairs={{0,2},{1,3},{2,0},{3,1},{4,6},{5,7},{6,4},{7,5},{8,10},{9,11},{10,... | collective-permute-start | bytes 3145736 | tf_op jit(solution)/shard_map/ppermute | solution.py:283
  45.7 35.7 %collective-permute-start.3 = (bf16[256,2048]{1,0:T(8,128)(2,1)}, bf16[256,2048]{1,0:T(8,128)(2,1)}, u32[]{:S(2)}, u32[]{:S(2)}) collective-permute-start(bf16[256,2048]{1,0:T(8,128)(2,1)} %get-tuple-element.32), channel_id=1, source_target_pairs={{0,1},{1,0},{2,3},{3,2},{4,5},{5,4},{6,7},{7,6},{8,9},{9,8},{10,11... | collective-permute-start | bytes 3145736 | tf_op jit(solution)/shard_map/ppermute | solution.py:282
  54.9 42.8 %collective-permute-start.6 = (bf16[256,2048]{1,0:T(8,128)(2,1)}, bf16[256,2048]{1,0:T(8,128)(2,1)}, u32[]{:S(2)}, u32[]{:S(2)}) collective-permute-start(bf16[256,2048]{1,0:T(8,128)(2,1)} %collective-permute-done.2.refs_2_), channel_id=1, source_target_pairs={{0,1},{1,0},{2,3},{3,2},{4,5},{5,4},{6,7},{7,6},{8,9},{9,8},{10,11... | collective-permute-start | bytes 3145736 | tf_op jit(solution)/shard_map/ppermute | solution.py:282
  55.0 44.9 %collective-permute-start.7 = (bf16[256,2048]{1,0:T(8,128)(2,1)}, bf16[256,2048]{1,0:T(8,128)(2,1)}, u32[]{:S(2)}, u32[]{:S(2)}) collective-permute-start(bf16[256,2048]{1,0:T(8,128)(2,1)} %collective-permute-done.1.refs_0_), channel_id=1, source_target_pairs={{0,2},{1,3},{2,0},{3,1},{4,6},{5,7},{6,4},{7,5},{8,10},{9,11},{10,... | collective-permute-start | bytes 3145736 | tf_op jit(solution)/shard_map/ppermute | solution.py:283
  76.5 65.3 %all-to-all-start.1 = ((bf16[8,64,2560]{2,1,0:T(8,128)(2,1)}), bf16[8,64,2560]{2,1,0:T(8,128)(2,1)}, u32[]{:S(2)}, u32[]{:S(2)}) async-start(bf16[8,64,2560]{2,1,0:T(8,128)(2,1)} %gather_fusion.1), calls=%async_computation.1 | async-start | bytes 5242880 | tf_op jit(solution)/shard_map/all_to_all | solution.py:307
  81.4 45.7 %collective-permute-start.14 = (bf16[256,2048]{1,0:T(8,128)(2,1)}, bf16[256,2048]{1,0:T(8,128)(2,1)S(1)}, u32[]{:S(2)}, u32[]{:S(2)}) collective-permute-start(bf16[256,2048]{1,0:T(8,128)(2,1)} %get-tuple-element.49), channel_id=1, source_target_pairs={{0,1},{1,0},{2,3},{3,2},{4,5},{5,4},{6,7},{7,6},{8,9},{9,8},{10,11... | collective-permute-start | bytes 3145736 | tf_op jit(solution)/shard_map/ppermute | solution.py:282
  83.0 45.7 %collective-permute-start.15 = (bf16[256,2048]{1,0:T(8,128)(2,1)}, bf16[256,2048]{1,0:T(8,128)(2,1)S(1)}, u32[]{:S(2)}, u32[]{:S(2)}) collective-permute-start(bf16[256,2048]{1,0:T(8,128)(2,1)} %get-tuple-element.50), channel_id=1, source_target_pairs={{0,2},{1,3},{2,0},{3,1},{4,6},{5,7},{6,4},{7,5},{8,10},{9,11},{10,... | collective-permute-start | bytes 3145736 | tf_op jit(solution)/shard_map/ppermute | solution.py:283
  83.5 16.4 %copy-start.3 = (bf16[256,8192]{1,0:T(8,128)(2,1)S(1)}, bf16[256,8192]{1,0:T(8,128)(2,1)}, u32[]{:S(2)}) copy-start(bf16[256,8192]{1,0:T(8,128)(2,1)} %refs_0_.3) | copy-start | bytes 12582916
  103.6 17.8 %collective-permute-start.8 = (f32[128,128]{1,0:T(8,128)S(1)}, f32[128,128]{1,0:T(8,128)S(1)}, u32[]{:S(2)}, u32[]{:S(2)}) collective-permute-start(f32[128,128]{1,0:T(8,128)S(1)} %get-tuple-element.41), channel_id=1, source_target_pairs={{0,1},{1,0},{2,3},{3,2},{4,5},{5,4},{6,7},{7,6},{8,9},{9,8},{10,11... | collective-permute-start | bytes 196616 | tf_op jit(solution)/shard_map/ppermute | solution.py:282
  103.7 19.9 %collective-permute-start.9 = (f32[128,128]{1,0:T(8,128)S(1)}, f32[128,128]{1,0:T(8,128)S(1)}, u32[]{:S(2)}, u32[]{:S(2)}) collective-permute-start(f32[128,128]{1,0:T(8,128)S(1)} %get-tuple-element.42), channel_id=1, source_target_pairs={{0,2},{1,3},{2,0},{3,1},{4,6},{5,7},{6,4},{7,5},{8,10},{9,11},{10,... | collective-permute-start | bytes 196616 | tf_op jit(solution)/shard_map/ppermute | solution.py:283
  105.7 17.9 %collective-permute-start.10 = (f32[128,128]{1,0:T(8,128)S(1)}, f32[128,128]{1,0:T(8,128)S(1)}, u32[]{:S(2)}, u32[]{:S(2)}) collective-permute-start(f32[128,128]{1,0:T(8,128)S(1)} %get-tuple-element.43), channel_id=1, source_target_pairs={{0,3},{1,2},{2,1},{3,0},{4,7},{5,6},{6,5},{7,4},{8,11},{9,10},{10,... | collective-permute-start | bytes 196616 | tf_op jit(solution)/shard_map/ppermute | solution.py:284
  123.6 17.5 %collective-permute-start.17 = (bf16[128,128]{1,0:T(8,128)(2,1)S(1)}, bf16[128,128]{1,0:T(8,128)(2,1)S(1)}, u32[]{:S(2)}, u32[]{:S(2)}) collective-permute-start(bf16[128,128]{1,0:T(8,128)(2,1)S(1)} %add_convert_fusion.refs_2_), channel_id=1, source_target_pairs={{0,2},{1,3},{2,0},{3,1},{4,6},{5,7},{6,4},{7,5},{8,10},{9,11},{10,... | collective-permute-start | bytes 98312 | tf_op jit(solution)/shard_map/ppermute | solution.py:283
  125.2 15.9 %collective-permute-start.16 = (bf16[128,128]{1,0:T(8,128)(2,1)S(1)}, bf16[128,128]{1,0:T(8,128)(2,1)S(1)}, u32[]{:S(2)}, u32[]{:S(2)}) collective-permute-start(bf16[128,128]{1,0:T(8,128)(2,1)S(1)} %add_convert_fusion.refs_2_), channel_id=1, source_target_pairs={{0,1},{1,0},{2,3},{3,2},{4,5},{5,4},{6,7},{7,6},{8,9},{9,8},{10,11... | collective-permute-start | bytes 98312 | tf_op jit(solution)/shard_map/ppermute | solution.py:282
  125.7 25.0 %collective-permute-start.13 = (bf16[128,128]{1,0:T(8,128)(2,1)S(1)}, bf16[128,128]{1,0:T(8,128)(2,1)S(1)}, u32[]{:S(2)}, u32[]{:S(2)}) collective-permute-start(bf16[128,128]{1,0:T(8,128)(2,1)S(1)} %add_convert_fusion.refs_2_), channel_id=1, source_target_pairs={{0,3},{1,2},{2,1},{3,0},{4,7},{5,6},{6,5},{7,4},{8,11},{9,10},{10,... | collective-permute-start | bytes 98312 | tf_op jit(solution)/shard_map/ppermute | solution.py:284
  127.2 23.6 %collective-permute-start.11 = (bf16[256,2048]{1,0:T(8,128)(2,1)}, bf16[256,2048]{1,0:T(8,128)(2,1)S(1)}, u32[]{:S(2)}, u32[]{:S(2)}) collective-permute-start(bf16[256,2048]{1,0:T(8,128)(2,1)} %collective-permute-done.refs_1_), channel_id=1, source_target_pairs={{0,2},{1,3},{2,0},{3,1},{4,6},{5,7},{6,4},{7,5},{8,10},{9,11},{10,... | collective-permute-start | bytes 3145736 | tf_op jit(solution)/shard_map/ppermute | solution.py:283
  128.7 22.8 %collective-permute-start.12 = (bf16[256,2048]{1,0:T(8,128)(2,1)}, bf16[256,2048]{1,0:T(8,128)(2,1)S(1)}, u32[]{:S(2)}, u32[]{:S(2)}) collective-permute-start(bf16[256,2048]{1,0:T(8,128)(2,1)} %collective-permute-done.5.refs_3_), channel_id=1, source_target_pairs={{0,1},{1,0},{2,3},{3,2},{4,5},{5,4},{6,7},{7,6},{8,9},{9,8},{10,11... | collective-permute-start | bytes 3145736 | tf_op jit(solution)/shard_map/ppermute | solution.py:282
  151.5 12.8 %copy-start.1 = (bf16[4,64,2560]{2,1,0:T(8,128)(2,1)S(1)}, bf16[4,64,2560]{2,1,0:T(8,128)(2,1)}, u32[]{:S(2)}) copy-start(bf16[4,64,2560]{2,1,0:T(8,128)(2,1)} %param.9) | copy-start | bytes 3932164

commit v8 on v7

--- a/solution.py
+++ b/solution.py
@@ -44,10 +44,10 @@
     return ref[...] if at is None else ref[:, at[0] : at[1]]
 
 
-def cut_kernel(member_ref, tokens_ref, far_ref, own_ref, sems):
-    depth = far_ref.shape[1]
+def cut_kernel(flips, member_ref, tokens_ref, one_ref, two_ref, sems):
+    depth = one_ref.shape[1]
     copies = []
-    for number, (out_ref, flip) in enumerate(((far_ref, 3), (own_ref, 0))):
+    for number, (out_ref, flip) in enumerate(zip((one_ref, two_ref), flips)):
         start = pl.multiple_of((member_ref[0] ^ flip) * depth, depth)
         copies.append(pltpu.make_async_copy(tokens_ref.at[:, pl.ds(start, depth)], out_ref, sems.at[number]))
     for copy in copies:
@@ -56,11 +56,11 @@
         copy.wait()
 
 
-def first_cuts(tokens, member):
+def cuts(tokens, member, flips):
     rows, width = tokens.shape
     shape = (rows, width // 4)
     return pl.pallas_call(
-        cut_kernel,
+        functools.partial(cut_kernel, flips),
         grid_spec=pltpu.PrefetchScalarGridSpec(
             num_scalar_prefetch=1,
             grid=(1,),
@@ -70,7 +70,7 @@
         ),
         out_shape=[pltpu.VMEM(shape, tokens.dtype)] * 2,
         cost_estimate=cost(0, 2 * tokens.size),
-        name="first_cuts",
+        name="cuts",
     )(member.astype(jnp.int32).reshape(1), tokens)
 
 
@@ -288,15 +288,9 @@
     mine = jnp.sum(jnp.where((members[:, None] == jnp.arange(4))[:, :, None], mine[None], 0), axis=1)
     plan = jnp.concatenate([members, mine.reshape(-1)]).astype(jnp.int32)
 
-    def part(array, start, size):
-        return lax.dynamic_slice(array, (0, start), (rows, size))
-
-    def cut(j, *others):
-        return part(tokens, after((member ^ 3 ^ j) * depth, *others), depth)
-
-    s0, s3 = first_cuts(tokens, member)
+    s0, s3 = cuts(tokens, member, (3, 0))
     x0, y3 = to_x(s0), to_y(s3)
-    s1, s2 = cut(1, s0, s3), cut(2, s0, s3)
+    s1, s2 = cuts(tokens, after(member, s0, s3), (2, 1))
     x1, y2 = to_x(s1), to_y(s2)
     x2, y1 = to_x(after(s2, x0, y3)), to_y(after(s1, x0, y3))
 

time: 165 us -> 165 us (level)
  Pallas kernels: 105 us -> 108 us
  local copies, waits for them, and re-layouts: 11.1 us -> 8.18 us
    ppermute x8, waiting for transfers between devices: 12 us -> 6.37 us  [square(): to_y = lambda v: lax.ppermute(v, 'tp', [(i, i ^ 2) for i in range(4)])]
    ppermute x8, waiting for transfers between devices: 3.38 us -> 8.74 us  [square(): to_x = lambda v: lax.ppermute(v, 'tp', [(i, i ^ 1) for i in range(4)])]
    dynamic_slice x1 -> x0, local copies, waits for them, and re-layouts: 4.19 us -> none  [part(): return lax.dynamic_slice(array, (0, start), (rows, size))]
    pallas_call x1 -> x2, Pallas kernels: 3 us -> 5.87 us  [cuts(): pl.pallas_call(functools.partial(cut_kernel, flips), grid_spec=pltpu.Pref...]
  transfers between devices with their start and end apart: 20 -> 20, of which waited for: 7 -> 8; matrix products, arithmetic and copies ran while one was open for 6% -> 4% of each run, Pallas kernels for 54% -> 56%
where the time goes in v8:
time: 165 us; the launch traced here: 164 us
  Pallas kernels  108 us (65%)
  starting transfers between devices  31.8 us (19%)
  waiting for transfers between devices  15.7 us (10%)
  local copies, waits for them, and re-layouts  8.18 us (5%)
    pallas_call x6, Pallas kernels, project(): pl.pallas_call(functools.partial(project_kernel, flat, weights_at, totals...  89.5 us
    ppermute x8, starting transfers between devices, square(): to_y = lambda v: lax.ppermute(v, 'tp', [(i, i ^ 2) for i in range(4)])  10.7 us
    all_to_all x2, starting transfers between devices, exchange(): lax.all_to_all(panels, 'grp', split_axis=0, concat_axis=0, tiled=True)  10.2 us
    pallas_call x1, Pallas kernels, finish(): pl.pallas_call(functools.partial(finish_kernel, 3), grid_spec=pltpu.Prefe...  8.91 us
    ppermute x8, waiting for transfers between devices, square(): to_x = lambda v: lax.ppermute(v, 'tp', [(i, i ^ 1) for i in range(4)])  8.74 us
    ppermute x8, starting transfers between devices, square(): to_x = lambda v: lax.ppermute(v, 'tp', [(i, i ^ 1) for i in range(4)])  7.93 us
    ppermute x8, waiting for transfers between devices, square(): to_y = lambda v: lax.ppermute(v, 'tp', [(i, i ^ 2) for i in range(4)])  6.37 us
    pallas_call x2, Pallas kernels, cuts(): pl.pallas_call(functools.partial(cut_kernel, flips), grid_spec=pltpu.Pref...  5.87 us
  transfers between devices with their start and end apart: 20, of which 8 were waited for; matrix products, arithmetic and copies ran while one was open for 4% of the time, Pallas kernels for 56%

profile of v8, /device:TPU:0, one launch (start us, length us, event | category | flops | bytes accessed | tf_op | source)
XLA Modules:
  0.0 164.3 jit_solution(6281575565114357876)
XLA Ops:
  0.0 3.0 %cuts.2 = (bf16[256,2048]{1,0:T(8,128)(2,1)}, bf16[256,2048]{1,0:T(8,128)(2,1)}) custom-call(s32[1]{0:T(128)} %bitcast.member_ref, bf16[256,8192]{1,0:T(8,128)(2,1)} %refs_0_.3), custom_call_target="tpu_custom_call" | custom-call | bytes 4194304 | tf_op jit(solution)/shard_map/cuts/pallas_call | solution.py:62
  3.0 3.0 %collective-permute-start.1 = (bf16[256,2048]{1,0:T(8,128)(2,1)}, bf16[256,2048]{1,0:T(8,128)(2,1)}, u32[]{:S(2)}, u32[]{:S(2)}) collective-permute-start(bf16[256,2048]{1,0:T(8,128)(2,1)} %get-tuple-element.52), channel_id=1, source_target_pairs={{0,1},{1,0},{2,3},{3,2},{4,5},{5,4},{6,7},{7,6},{8,9},{9,8},{10,11... | collective-permute-start | bytes 3145736 | tf_op jit(solution)/shard_map/ppermute | solution.py:282
  6.0 1.5 collective-permute-start.2
  7.6 2.9 %cuts.3 = (bf16[256,2048]{1,0:T(8,128)(2,1)}, bf16[256,2048]{1,0:T(8,128)(2,1)}) custom-call(s32[1]{0:T(128)} %bitcast.1.member_ref, bf16[256,8192]{1,0:T(8,128)(2,1)} %refs_0_.3), custom_call_target="tpu_custom_call" | custom-call | bytes 4194304 | tf_op jit(solution)/shard_map/cuts/pallas_call | solution.py:62
  10.4 0.6 collective-permute-start
  11.1 0.1 select_reduce_fusion
  11.2 0.1 reduce_sum.31
  11.3 0.1 fusion.2
  11.4 3.2 %gather_fusion = bf16[8,64,2048]{2,1,0:T(8,128)(2,1)} fusion(bf16[4,64,2048]{2,1,0:T(8,128)(2,1)} %param.8, s32[1024]{0:T(1024)S(1)} %pad_clamp_fusion.1), kind=kCustom, calls=%fused_computation | custom fusion | bytes 4194336 | tf_op jit(solution)/shard_map/jit(_take)/gather | solution.py:298
  14.6 5.3 %all-to-all-start = ((bf16[8,64,2048]{2,1,0:T(8,128)(2,1)}), bf16[8,64,2048]{2,1,0:T(8,128)(2,1)S(1)}, u32[]{:S(2)}, u32[]{:S(2)}) async-start(bf16[8,64,2048]{2,1,0:T(8,128)(2,1)} %gather_fusion), calls=%async_computation | async-start | bytes 4194304 | tf_op jit(solution)/shard_map/all_to_all | solution.py:301
  20.0 0.1 dynamic_slice.3
  20.1 0.1 broadcast_in_dim.53
  20.1 0.1 copy.8
  20.3 0.1 select_reduce_fusion.1
  20.5 0.1 copy.9
  20.6 0.1 reshape.40
  20.7 2.2 %copy-done.2 = bf16[256,8192]{1,0:T(8,128)(2,1)S(1)} copy-done((bf16[256,8192]{1,0:T(8,128)(2,1)S(1)}, bf16[256,8192]{1,0:T(8,128)(2,1)}, u32[]{:S(2)}) %copy-start.2) | copy-done | bytes 4194328
  22.9 21.4 %own_rows.1.refs_0_ = f32[1,256,2560]{2,1,0:T(8,128)} custom-call(s32[12]{0:T(128)S(1)} %pad_add_fusion.plan_ref, bf16[256,8192]{1,0:T(8,128)(2,1)S(1)} %copy-done.2, bf16[8192,2560]{1,0:T(8,128)(2,1)} %refs_3_.5, bf16[8192,2560]{1,0:T(8,128)(2,1)} %refs_3_.5, bf16[8192,2560]{1,0:T(8,128)(2,1)} %refs_3_.5, bf16[8192,2560]{1,0:T(8,128)(2,1)} %refs_3_.5), custom_call_target="tpu_custom_call" | custom-call | tf_op jit(solution)/shard_map/own_rows/pallas_call | solution.py:159
  44.4 1.6 collective-permute-start.3
  45.9 1.5 collective-permute-start.4
  47.4 5.4 %collective-permute-done.refs_1_ = bf16[256,2048]{1,0:T(8,128)(2,1)} collective-permute-done((bf16[256,2048]{1,0:T(8,128)(2,1)}, bf16[256,2048]{1,0:T(8,128)(2,1)}, u32[]{:S(2)}, u32[]{:S(2)}) %collective-permute-start) | collective-permute-done | bytes 1048608 | tf_op jit(solution)/shard_map/ppermute | solution.py:282
  52.8 2.1 %collective-permute-done.5.refs_3_ = bf16[256,2048]{1,0:T(8,128)(2,1)} collective-permute-done((bf16[256,2048]{1,0:T(8,128)(2,1)}, bf16[256,2048]{1,0:T(8,128)(2,1)}, u32[]{:S(2)}, u32[]{:S(2)}) %collective-permute-start.5) | collective-permute-done | bytes 1048608 | tf_op jit(solution)/shard_map/ppermute | solution.py:283
  55.0 2.0 %collective-permute-start.7 = (bf16[256,2048]{1,0:T(8,128)(2,1)}, bf16[256,2048]{1,0:T(8,128)(2,1)}, u32[]{:S(2)}, u32[]{:S(2)}) collective-permute-start(bf16[256,2048]{1,0:T(8,128)(2,1)} %collective-permute-done.1.refs_0_), channel_id=1, source_target_pairs={{0,2},{1,3},{2,0},{3,1},{4,6},{5,7},{6,4},{7,5},{8,10},{9,11},{10,... | collective-permute-start | bytes 3145736 | tf_op jit(solution)/shard_map/ppermute | solution.py:283
  57.0 17.3 %near_rows.1.refs_3_.refs_4_ = f32[2,256,2560]{2,1,0:T(8,128)} custom-call(s32[12]{0:T(128)S(1)} %pad_add_fusion.plan_ref, bf16[256,2048]{1,0:T(8,128)(2,1)} %collective-permute-done.1.refs_0_, bf16[256,2048]{1,0:T(8,128)(2,1)} %collective-permute-done.refs_1_, bf16[256,2048]{1,0:T(8,128)(2,1)} %collective-permute-done.2.refs_2_, ...), custom_call_target="tpu_custom_call" | custom-call | flops 64424509440 | bytes 283115520 | tf_op jit(solution)/shard_map/near_rows/pallas_call | solution.py:159
  74.3 2.2 %gather_fusion.1 = bf16[8,64,2560]{2,1,0:T(8,128)(2,1)} fusion(bf16[4,64,2560]{2,1,0:T(8,128)(2,1)S(1)} %copy-done, s32[1024]{0:T(1024)S(1)} %pad_clamp_fusion), kind=kCustom, calls=%fused_computation.1 | custom fusion | bytes 5242912 | tf_op jit(solution)/shard_map/jit(_take)/gather | solution.py:298
  76.5 4.9 %all-to-all-start.1 = ((bf16[8,64,2560]{2,1,0:T(8,128)(2,1)}), bf16[8,64,2560]{2,1,0:T(8,128)(2,1)}, u32[]{:S(2)}, u32[]{:S(2)}) async-start(bf16[8,64,2560]{2,1,0:T(8,128)(2,1)} %gather_fusion.1), calls=%async_computation.1 | async-start | bytes 5242880 | tf_op jit(solution)/shard_map/all_to_all | solution.py:301
  81.4 1.6 collective-permute-start.14
  83.0 0.5 collective-permute-start.15
  83.5 12.9 %near_rows_more.1.refs_3_.refs_4_ = f32[2,256,2560]{2,1,0:T(8,128)} custom-call(s32[12]{0:T(128)S(1)} %pad_add_fusion.plan_ref, bf16[256,2048]{1,0:T(8,128)(2,1)} %collective-permute-done.3.refs_0_.refs_1_, bf16[256,2048]{1,0:T(8,128)(2,1)} %collective-permute-done.4.refs_1_.refs_2_, bf16[8192,2560]{1,0:T(8,128)(2,1)} %refs_3_.5, ...), custom_call_target="tpu_custom_call" | custom-call | tf_op jit(solution)/shard_map/near_rows_more/pallas_call | solution.py:159
  96.4 1.4 collective-permute-done.6.refs_1_
  97.8 2.1 %collective-permute-done.7.refs_3_.refs_0_ = bf16[256,2048]{1,0:T(8,128)(2,1)} collective-permute-done((bf16[256,2048]{1,0:T(8,128)(2,1)}, bf16[256,2048]{1,0:T(8,128)(2,1)}, u32[]{:S(2)}, u32[]{:S(2)}) %collective-permute-start.7) | collective-permute-done | bytes 1048608 | tf_op jit(solution)/shard_map/ppermute | solution.py:283
  99.9 3.7 %shrink_parts.1 = (f32[128,128]{1,0:T(8,128)S(1)}, f32[128,128]{1,0:T(8,128)S(1)}, f32[128,128]{1,0:T(8,128)S(1)}, f32[128,128]{1,0:T(8,128)S(1)}) custom-call(s32[12]{0:T(128)S(1)} %pad_add_fusion.plan_ref, bf16[256,8192]{1,0:T(8,128)(2,1)S(1)} %copy-done.3, bf16[256,2048]{1,0:T(8,128)(2,1)} %collective-permute-done.3.refs_0_.refs_1_, ...), custom_call_target="tpu_custom_call" | custom-call | flops 1073741824 | bytes 6291456 | tf_op jit(solution)/shard_map/shrink_parts/pallas_call | solution.py:257
  103.6 0.1 collective-permute-start.8
  103.7 2.0 %collective-permute-start.9 = (f32[128,128]{1,0:T(8,128)S(1)}, f32[128,128]{1,0:T(8,128)S(1)}, u32[]{:S(2)}, u32[]{:S(2)}) collective-permute-start(f32[128,128]{1,0:T(8,128)S(1)} %get-tuple-element.44), channel_id=1, source_target_pairs={{0,2},{1,3},{2,0},{3,1},{4,6},{5,7},{6,4},{7,5},{8,10},{9,11},{10,... | collective-permute-start | bytes 196616 | tf_op jit(solution)/shard_map/ppermute | solution.py:283
  105.7 1.4 collective-permute-start.10
  107.1 13.0 %far_rows.1.refs_4_ = f32[1,256,2560]{2,1,0:T(8,128)} custom-call(s32[12]{0:T(128)S(1)} %pad_add_fusion.plan_ref, bf16[256,2048]{1,0:T(8,128)(2,1)} %collective-permute-done.7.refs_3_.refs_0_, bf16[256,2048]{1,0:T(8,128)(2,1)} %collective-permute-done.6.refs_1_, bf16[8192,2560]{1,0:T(8,128)(2,1)} %refs_3_.5, bf16[8192,2560]{1,0:T(8,128)(2,1)} %refs_3_.5), custom_call_target="tpu_custom_call" | custom-call | flops 21474836480 | bytes 94371840 | tf_op jit(solution)/shard_map/far_rows/pallas_call | solution.py:159
  120.2 1.3 collective-permute-done.8
  121.4 2.2 %collective-permute-done.9 = f32[128,128]{1,0:T(8,128)S(1)} collective-permute-done((f32[128,128]{1,0:T(8,128)S(1)}, f32[128,128]{1,0:T(8,128)S(1)}, u32[]{:S(2)}, u32[]{:S(2)}) %collective-permute-start.9) | collective-permute-done | bytes 65568 | tf_op jit(solution)/shard_map/ppermute | solution.py:283
  123.6 1.6 collective-permute-start.17
  125.2 0.5 collective-permute-start.16
  125.7 1.4 collective-permute-start.13
  127.2 1.5 collective-permute-start.11
  128.7 0.5 collective-permute-start.12
  129.2 12.0 %near_rows_rest.1.refs_1_ = f32[2,256,2560]{2,1,0:T(8,128)} custom-call(s32[12]{0:T(128)S(1)} %pad_add_fusion.plan_ref, bf16[256,2048]{1,0:T(8,128)(2,1)S(1)} %collective-permute-done.14.refs_0_, bf16[256,2048]{1,0:T(8,128)(2,1)S(1)} %collective-permute-done.15.refs_1_, bf16[8192,2560]{1,0:T(8,128)(2,1)} %refs_3_.5, ...), custom_call_target="tpu_custom_call" | custom-call | flops 21474836480 | bytes 125829120 | tf_op jit(solution)/shard_map/near_rows_rest/pallas_call | solution.py:159
  141.2 0.6 all-to-all-done.1.refs_5_.refs_6_.refs_7_
  141.8 8.9 %finish_rows.1.refs_8_ = bf16[1024,2560]{1,0:T(8,128)(2,1)} custom-call(s32[12]{0:T(128)S(1)} %pad_add_fusion.plan_ref, f32[1,256,2560]{2,1,0:T(8,128)} %own_rows.1.refs_0_, f32[2,256,2560]{2,1,0:T(8,128)} %near_rows_rest.1.refs_1_, bf16[128,128]{1,0:T(8,128)(2,1)S(1)} %add_convert_fusion.refs_2_, bf16[128,128]{1,0:T(8,128)(2,1)S(1)} %collective-permute-done.16.refs_3_, ...), custom_call_target="tpu_custom_call" | custom-call | flops 503316480 | bytes 11796480 | tf_op jit(solution)/shard_map/finish_rows/pallas_call | solution.py:202
  150.7 0.7 collective-permute-done.12.refs_1_
  151.5 12.8 %last_rows.1 = bf16[1024,2560]{1,0:T(8,128)(2,1)} custom-call(s32[12]{0:T(128)S(1)} %pad_add_fusion.plan_ref, bf16[256,2048]{1,0:T(8,128)(2,1)S(1)} %collective-permute-done.11.refs_0_, bf16[256,2048]{1,0:T(8,128)(2,1)S(1)} %collective-permute-done.12.refs_1_, bf16[8192,2560]{1,0:T(8,128)(2,1)} %refs_3_.5, ...), custom_call_target="tpu_custom_call", output_to_operand_aliasing={{}: (9, {})} | custom-call | flops 10737418240 | bytes 52428800 | tf_op jit(solution)/shard_map/last_rows/pallas_call | solution.py:159
  (32 shorter events, 0.4 us)
Async XLA Ops:
  0.0 74.3 %copy-start = (bf16[4,64,2560]{2,1,0:T(8,128)(2,1)S(1)}, bf16[4,64,2560]{2,1,0:T(8,128)(2,1)}, u32[]{:S(2)}) copy-start(bf16[4,64,2560]{2,1,0:T(8,128)(2,1)} %param.9) | copy-start | bytes 3932164
  3.0 8.1 %copy-start.4 = (s32[32]{0:T(128)S(1)}, s32[32]{0:T(128)}, u32[]{:S(2)}) copy-start(s32[32]{0:T(128)} %param.10) | copy-start | bytes 388
  3.0 8.1 %copy-start.5 = (s32[64]{0:T(128)S(1)}, s32[64]{0:T(128)}, u32[]{:S(2)}) copy-start(s32[64]{0:T(128)} %param.11) | copy-start | bytes 772
  3.0 41.3 %collective-permute-start.1 = (bf16[256,2048]{1,0:T(8,128)(2,1)}, bf16[256,2048]{1,0:T(8,128)(2,1)}, u32[]{:S(2)}, u32[]{:S(2)}) collective-permute-start(bf16[256,2048]{1,0:T(8,128)(2,1)} %get-tuple-element.52), channel_id=1, source_target_pairs={{0,1},{1,0},{2,3},{3,2},{4,5},{5,4},{6,7},{7,6},{8,9},{9,8},{10,11... | collective-permute-start | bytes 3145736 | tf_op jit(solution)/shard_map/ppermute | solution.py:282
  6.0 38.3 %collective-permute-start.2 = (bf16[256,2048]{1,0:T(8,128)(2,1)}, bf16[256,2048]{1,0:T(8,128)(2,1)}, u32[]{:S(2)}, u32[]{:S(2)}) collective-permute-start(bf16[256,2048]{1,0:T(8,128)(2,1)} %get-tuple-element.51), channel_id=1, source_target_pairs={{0,2},{1,3},{2,0},{3,1},{4,6},{5,7},{6,4},{7,5},{8,10},{9,11},{10,... | collective-permute-start | bytes 3145736 | tf_op jit(solution)/shard_map/ppermute | solution.py:283
  10.4 42.4 %collective-permute-start = (bf16[256,2048]{1,0:T(8,128)(2,1)}, bf16[256,2048]{1,0:T(8,128)(2,1)}, u32[]{:S(2)}, u32[]{:S(2)}) collective-permute-start(bf16[256,2048]{1,0:T(8,128)(2,1)} %get-tuple-element.35), channel_id=1, source_target_pairs={{0,1},{1,0},{2,3},{3,2},{4,5},{5,4},{6,7},{7,6},{8,9},{9,8},{10,11... | collective-permute-start | bytes 3145736 | tf_op jit(solution)/shard_map/ppermute | solution.py:282
  11.0 43.9 %collective-permute-start.5 = (bf16[256,2048]{1,0:T(8,128)(2,1)}, bf16[256,2048]{1,0:T(8,128)(2,1)}, u32[]{:S(2)}, u32[]{:S(2)}) collective-permute-start(bf16[256,2048]{1,0:T(8,128)(2,1)} %get-tuple-element.34), channel_id=1, source_target_pairs={{0,2},{1,3},{2,0},{3,1},{4,6},{5,7},{6,4},{7,5},{8,10},{9,11},{10,... | collective-permute-start | bytes 3145736 | tf_op jit(solution)/shard_map/ppermute | solution.py:283
  14.6 59.7 %all-to-all-start = ((bf16[8,64,2048]{2,1,0:T(8,128)(2,1)}), bf16[8,64,2048]{2,1,0:T(8,128)(2,1)S(1)}, u32[]{:S(2)}, u32[]{:S(2)}) async-start(bf16[8,64,2048]{2,1,0:T(8,128)(2,1)} %gather_fusion), calls=%async_computation | async-start | bytes 4194304 | tf_op jit(solution)/shard_map/all_to_all | solution.py:301
  20.7 2.2 %copy-start.2 = (bf16[256,8192]{1,0:T(8,128)(2,1)S(1)}, bf16[256,8192]{1,0:T(8,128)(2,1)}, u32[]{:S(2)}) copy-start(bf16[256,8192]{1,0:T(8,128)(2,1)} %refs_0_.3) | copy-start | bytes 12582916
  44.4 37.0 %collective-permute-start.3 = (bf16[256,2048]{1,0:T(8,128)(2,1)}, bf16[256,2048]{1,0:T(8,128)(2,1)}, u32[]{:S(2)}, u32[]{:S(2)}) collective-permute-start(bf16[256,2048]{1,0:T(8,128)(2,1)} %get-tuple-element.34), channel_id=1, source_target_pairs={{0,1},{1,0},{2,3},{3,2},{4,5},{5,4},{6,7},{7,6},{8,9},{9,8},{10,11... | collective-permute-start | bytes 3145736 | tf_op jit(solution)/shard_map/ppermute | solution.py:282
  45.9 35.5 %collective-permute-start.4 = (bf16[256,2048]{1,0:T(8,128)(2,1)}, bf16[256,2048]{1,0:T(8,128)(2,1)}, u32[]{:S(2)}, u32[]{:S(2)}) collective-permute-start(bf16[256,2048]{1,0:T(8,128)(2,1)} %get-tuple-element.35), channel_id=1, source_target_pairs={{0,2},{1,3},{2,0},{3,1},{4,6},{5,7},{6,4},{7,5},{8,10},{9,11},{10,... | collective-permute-start | bytes 3145736 | tf_op jit(solution)/shard_map/ppermute | solution.py:283
  54.9 42.8 %collective-permute-start.6 = (bf16[256,2048]{1,0:T(8,128)(2,1)}, bf16[256,2048]{1,0:T(8,128)(2,1)}, u32[]{:S(2)}, u32[]{:S(2)}) collective-permute-start(bf16[256,2048]{1,0:T(8,128)(2,1)} %collective-permute-done.2.refs_2_), channel_id=1, source_target_pairs={{0,1},{1,0},{2,3},{3,2},{4,5},{5,4},{6,7},{7,6},{8,9},{9,8},{10,11... | collective-permute-start | bytes 3145736 | tf_op jit(solution)/shard_map/ppermute | solution.py:282
  55.0 44.9 %collective-permute-start.7 = (bf16[256,2048]{1,0:T(8,128)(2,1)}, bf16[256,2048]{1,0:T(8,128)(2,1)}, u32[]{:S(2)}, u32[]{:S(2)}) collective-permute-start(bf16[256,2048]{1,0:T(8,128)(2,1)} %collective-permute-done.1.refs_0_), channel_id=1, source_target_pairs={{0,2},{1,3},{2,0},{3,1},{4,6},{5,7},{6,4},{7,5},{8,10},{9,11},{10,... | collective-permute-start | bytes 3145736 | tf_op jit(solution)/shard_map/ppermute | solution.py:283
  76.5 65.3 %all-to-all-start.1 = ((bf16[8,64,2560]{2,1,0:T(8,128)(2,1)}), bf16[8,64,2560]{2,1,0:T(8,128)(2,1)}, u32[]{:S(2)}, u32[]{:S(2)}) async-start(bf16[8,64,2560]{2,1,0:T(8,128)(2,1)} %gather_fusion.1), calls=%async_computation.1 | async-start | bytes 5242880 | tf_op jit(solution)/shard_map/all_to_all | solution.py:301
  81.4 45.7 %collective-permute-start.14 = (bf16[256,2048]{1,0:T(8,128)(2,1)}, bf16[256,2048]{1,0:T(8,128)(2,1)S(1)}, u32[]{:S(2)}, u32[]{:S(2)}) collective-permute-start(bf16[256,2048]{1,0:T(8,128)(2,1)} %get-tuple-element.51), channel_id=1, source_target_pairs={{0,1},{1,0},{2,3},{3,2},{4,5},{5,4},{6,7},{7,6},{8,9},{9,8},{10,11... | collective-permute-start | bytes 3145736 | tf_op jit(solution)/shard_map/ppermute | solution.py:282
  83.0 45.7 %collective-permute-start.15 = (bf16[256,2048]{1,0:T(8,128)(2,1)}, bf16[256,2048]{1,0:T(8,128)(2,1)S(1)}, u32[]{:S(2)}, u32[]{:S(2)}) collective-permute-start(bf16[256,2048]{1,0:T(8,128)(2,1)} %get-tuple-element.52), channel_id=1, source_target_pairs={{0,2},{1,3},{2,0},{3,1},{4,6},{5,7},{6,4},{7,5},{8,10},{9,11},{10,... | collective-permute-start | bytes 3145736 | tf_op jit(solution)/shard_map/ppermute | solution.py:283
  83.5 16.4 %copy-start.3 = (bf16[256,8192]{1,0:T(8,128)(2,1)S(1)}, bf16[256,8192]{1,0:T(8,128)(2,1)}, u32[]{:S(2)}) copy-start(bf16[256,8192]{1,0:T(8,128)(2,1)} %refs_0_.3) | copy-start | bytes 12582916
  103.6 17.8 %collective-permute-start.8 = (f32[128,128]{1,0:T(8,128)S(1)}, f32[128,128]{1,0:T(8,128)S(1)}, u32[]{:S(2)}, u32[]{:S(2)}) collective-permute-start(f32[128,128]{1,0:T(8,128)S(1)} %get-tuple-element.43), channel_id=1, source_target_pairs={{0,1},{1,0},{2,3},{3,2},{4,5},{5,4},{6,7},{7,6},{8,9},{9,8},{10,11... | collective-permute-start | bytes 196616 | tf_op jit(solution)/shard_map/ppermute | solution.py:282
  103.7 19.9 %collective-permute-start.9 = (f32[128,128]{1,0:T(8,128)S(1)}, f32[128,128]{1,0:T(8,128)S(1)}, u32[]{:S(2)}, u32[]{:S(2)}) collective-permute-start(f32[128,128]{1,0:T(8,128)S(1)} %get-tuple-element.44), channel_id=1, source_target_pairs={{0,2},{1,3},{2,0},{3,1},{4,6},{5,7},{6,4},{7,5},{8,10},{9,11},{10,... | collective-permute-start | bytes 196616 | tf_op jit(solution)/shard_map/ppermute | solution.py:283
  105.7 17.9 %collective-permute-start.10 = (f32[128,128]{1,0:T(8,128)S(1)}, f32[128,128]{1,0:T(8,128)S(1)}, u32[]{:S(2)}, u32[]{:S(2)}) collective-permute-start(f32[128,128]{1,0:T(8,128)S(1)} %get-tuple-element.45), channel_id=1, source_target_pairs={{0,3},{1,2},{2,1},{3,0},{4,7},{5,6},{6,5},{7,4},{8,11},{9,10},{10,... | collective-permute-start | bytes 196616 | tf_op jit(solution)/shard_map/ppermute | solution.py:284
  123.6 17.6 %collective-permute-start.17 = (bf16[128,128]{1,0:T(8,128)(2,1)S(1)}, bf16[128,128]{1,0:T(8,128)(2,1)S(1)}, u32[]{:S(2)}, u32[]{:S(2)}) collective-permute-start(bf16[128,128]{1,0:T(8,128)(2,1)S(1)} %add_convert_fusion.refs_2_), channel_id=1, source_target_pairs={{0,2},{1,3},{2,0},{3,1},{4,6},{5,7},{6,4},{7,5},{8,10},{9,11},{10,... | collective-permute-start | bytes 98312 | tf_op jit(solution)/shard_map/ppermute | solution.py:283
  125.2 16.0 %collective-permute-start.16 = (bf16[128,128]{1,0:T(8,128)(2,1)S(1)}, bf16[128,128]{1,0:T(8,128)(2,1)S(1)}, u32[]{:S(2)}, u32[]{:S(2)}) collective-permute-start(bf16[128,128]{1,0:T(8,128)(2,1)S(1)} %add_convert_fusion.refs_2_), channel_id=1, source_target_pairs={{0,1},{1,0},{2,3},{3,2},{4,5},{5,4},{6,7},{7,6},{8,9},{9,8},{10,11... | collective-permute-start | bytes 98312 | tf_op jit(solution)/shard_map/ppermute | solution.py:282
  125.7 25.0 %collective-permute-start.13 = (bf16[128,128]{1,0:T(8,128)(2,1)S(1)}, bf16[128,128]{1,0:T(8,128)(2,1)S(1)}, u32[]{:S(2)}, u32[]{:S(2)}) collective-permute-start(bf16[128,128]{1,0:T(8,128)(2,1)S(1)} %add_convert_fusion.refs_2_), channel_id=1, source_target_pairs={{0,3},{1,2},{2,1},{3,0},{4,7},{5,6},{6,5},{7,4},{8,11},{9,10},{10,... | collective-permute-start | bytes 98312 | tf_op jit(solution)/shard_map/ppermute | solution.py:284
  127.2 23.6 %collective-permute-start.11 = (bf16[256,2048]{1,0:T(8,128)(2,1)}, bf16[256,2048]{1,0:T(8,128)(2,1)S(1)}, u32[]{:S(2)}, u32[]{:S(2)}) collective-permute-start(bf16[256,2048]{1,0:T(8,128)(2,1)} %collective-permute-done.refs_1_), channel_id=1, source_target_pairs={{0,2},{1,3},{2,0},{3,1},{4,6},{5,7},{6,4},{7,5},{8,10},{9,11},{10,... | collective-permute-start | bytes 3145736 | tf_op jit(solution)/shard_map/ppermute | solution.py:283
  128.7 22.8 %collective-permute-start.12 = (bf16[256,2048]{1,0:T(8,128)(2,1)}, bf16[256,2048]{1,0:T(8,128)(2,1)S(1)}, u32[]{:S(2)}, u32[]{:S(2)}) collective-permute-start(bf16[256,2048]{1,0:T(8,128)(2,1)} %collective-permute-done.5.refs_3_), channel_id=1, source_target_pairs={{0,1},{1,0},{2,3},{3,2},{4,5},{5,4},{6,7},{7,6},{8,9},{9,8},{10,11... | collective-permute-start | bytes 3145736 | tf_op jit(solution)/shard_map/ppermute | solution.py:282
  151.5 12.8 %copy-start.1 = (bf16[4,64,2560]{2,1,0:T(8,128)(2,1)S(1)}, bf16[4,64,2560]{2,1,0:T(8,128)(2,1)}, u32[]{:S(2)}) copy-start(bf16[4,64,2560]{2,1,0:T(8,128)(2,1)} %param.9) | copy-start | bytes 3932164

commit v9 on v7

--- a/solution.py
+++ b/solution.py
@@ -10,7 +10,7 @@
 BLOCK = 128
 MIB = 1 << 20
 PANELS_AT = 4
-VMEM_BYTES = 24 * MIB
+VMEM_BYTES = 36 * MIB
 
 adapter_scale = 0.5
 

time: 165 us -> 165 us (level)
  no operation moved by 1% of the time
where the time goes in v9:
time: 165 us; the launch traced here: 164 us
  Pallas kernels  105 us (64%)
  starting transfers between devices  31.7 us (19%)
  waiting for transfers between devices  16.1 us (10%)
  local copies, waits for them, and re-layouts  11.1 us (7%)
    pallas_call x6, Pallas kernels, project(): pl.pallas_call(functools.partial(project_kernel, flat, weights_at, totals...  89.1 us
    ppermute x8, waiting for transfers between devices, square(): to_y = lambda v: lax.ppermute(v, 'tp', [(i, i ^ 2) for i in range(4)])  12 us
    ppermute x8, starting transfers between devices, square(): to_y = lambda v: lax.ppermute(v, 'tp', [(i, i ^ 2) for i in range(4)])  11.2 us
    all_to_all x2, starting transfers between devices, exchange(): lax.all_to_all(panels, 'grp', split_axis=0, concat_axis=0, tiled=True)  10.2 us
    pallas_call x1, Pallas kernels, finish(): pl.pallas_call(functools.partial(finish_kernel, 3), grid_spec=pltpu.Prefe...  8.91 us
    ppermute x8, starting transfers between devices, square(): to_x = lambda v: lax.ppermute(v, 'tp', [(i, i ^ 1) for i in range(4)])  7.39 us
    gather x2, local copies, waits for them, and re-layouts, chosen(): return jnp.take(panels, select, axis=0, mode='clip')  4.2 us
    dynamic_slice x1, local copies, waits for them, and re-layouts, part(): return lax.dynamic_slice(array, (0, start), (rows, size))  4.19 us
  transfers between devices with their start and end apart: 20, of which 7 were waited for; matrix products, arithmetic and copies ran while one was open for 6% of the time, Pallas kernels for 54%

profile of v9, /device:TPU:0, one launch (start us, length us, event | category | flops | bytes accessed | tf_op | source)
XLA Modules:
  0.0 164.3 jit_solution(6075173837567474031)
XLA Ops:
  0.0 3.0 %first_cuts.1 = (bf16[256,2048]{1,0:T(8,128)(2,1)}, bf16[256,2048]{1,0:T(8,128)(2,1)}) custom-call(s32[1]{0:T(128)} %bitcast.member_ref, bf16[256,8192]{1,0:T(8,128)(2,1)} %refs_0_.3), custom_call_target="tpu_custom_call" | custom-call | bytes 4194304 | tf_op jit(solution)/shard_map/first_cuts/pallas_call | solution.py:62
  3.1 3.0 %collective-permute-start.1 = (bf16[256,2048]{1,0:T(8,128)(2,1)}, bf16[256,2048]{1,0:T(8,128)(2,1)}, u32[]{:S(2)}, u32[]{:S(2)}) collective-permute-start(bf16[256,2048]{1,0:T(8,128)(2,1)} %get-tuple-element.50), channel_id=1, source_target_pairs={{0,1},{1,0},{2,3},{3,2},{4,5},{5,4},{6,7},{7,6},{8,9},{9,8},{10,11... | collective-permute-start | bytes 3145736 | tf_op jit(solution)/shard_map/ppermute | solution.py:282
  6.1 1.5 collective-permute-start.2
  7.6 4.2 %constant_dynamic-slice_fusion = (bf16[256,2048]{1,0:T(8,128)(2,1)}, bf16[256,2048]{1,0:T(8,128)(2,1)}) fusion(bf16[256,8192]{1,0:T(8,128)(2,1)} %refs_0_.3, s32[]{:T(128)S(6)} %select_n.42, s32[]{:T(128)S(6)} %select_n.41), kind=kLoop, calls=%fused_computation.25 | loop fusion | bytes 4194312 | tf_op jit(solution)/shard_map/dynamic_slice | solution.py:292
  11.8 0.5 collective-permute-start.5
  12.3 0.1 collective-permute-start
  12.4 0.1 select_reduce_fusion
  12.4 0.1 reduce_sum.31
  12.5 0.1 fusion.2
  12.7 2.0 %gather_fusion = bf16[8,64,2048]{2,1,0:T(8,128)(2,1)} fusion(bf16[4,64,2048]{2,1,0:T(8,128)(2,1)S(1)} %copy-done.4, s32[1024]{0:T(1024)S(1)} %pad_clamp_fusion.1), kind=kCustom, calls=%fused_computation | custom fusion | bytes 4194336 | tf_op jit(solution)/shard_map/jit(_take)/gather | solution.py:304
  14.7 5.3 %all-to-all-start = ((bf16[8,64,2048]{2,1,0:T(8,128)(2,1)}), bf16[8,64,2048]{2,1,0:T(8,128)(2,1)S(1)}, u32[]{:S(2)}, u32[]{:S(2)}) async-start(bf16[8,64,2048]{2,1,0:T(8,128)(2,1)} %gather_fusion), calls=%async_computation | async-start | bytes 4194304 | tf_op jit(solution)/shard_map/all_to_all | solution.py:307
  20.0 0.1 dynamic_slice.9
  20.1 0.1 broadcast_in_dim.53
  20.2 0.1 copy.8
  20.4 0.1 select_reduce_fusion.1
  20.5 0.1 copy.9
  20.6 0.1 reshape.37
  20.8 2.2 %copy-done.2 = bf16[256,8192]{1,0:T(8,128)(2,1)S(1)} copy-done((bf16[256,8192]{1,0:T(8,128)(2,1)S(1)}, bf16[256,8192]{1,0:T(8,128)(2,1)}, u32[]{:S(2)}) %copy-start.2) | copy-done | bytes 4194328
  23.0 21.2 %own_rows.1.refs_0_ = f32[1,256,2560]{2,1,0:T(8,128)} custom-call(s32[12]{0:T(128)S(1)} %pad_add_fusion.plan_ref, bf16[256,8192]{1,0:T(8,128)(2,1)S(1)} %copy-done.2, bf16[8192,2560]{1,0:T(8,128)(2,1)} %refs_3_.5, bf16[8192,2560]{1,0:T(8,128)(2,1)} %refs_3_.5, bf16[8192,2560]{1,0:T(8,128)(2,1)} %refs_3_.5, bf16[8192,2560]{1,0:T(8,128)(2,1)} %refs_3_.5), custom_call_target="tpu_custom_call" | custom-call | tf_op jit(solution)/shard_map/own_rows/pallas_call | solution.py:159
  44.1 1.6 collective-permute-start.4
  45.7 1.5 collective-permute-start.3
  47.2 7.7 %collective-permute-done.5.refs_3_ = bf16[256,2048]{1,0:T(8,128)(2,1)} collective-permute-done((bf16[256,2048]{1,0:T(8,128)(2,1)}, bf16[256,2048]{1,0:T(8,128)(2,1)}, u32[]{:S(2)}, u32[]{:S(2)}) %collective-permute-start.5) | collective-permute-done | bytes 1048608 | tf_op jit(solution)/shard_map/ppermute | solution.py:283
  55.0 2.0 %collective-permute-start.7 = (bf16[256,2048]{1,0:T(8,128)(2,1)}, bf16[256,2048]{1,0:T(8,128)(2,1)}, u32[]{:S(2)}, u32[]{:S(2)}) collective-permute-start(bf16[256,2048]{1,0:T(8,128)(2,1)} %collective-permute-done.1.refs_0_), channel_id=1, source_target_pairs={{0,2},{1,3},{2,0},{3,1},{4,6},{5,7},{6,4},{7,5},{8,10},{9,11},{10,... | collective-permute-start | bytes 3145736 | tf_op jit(solution)/shard_map/ppermute | solution.py:283
  57.0 17.3 %near_rows.1.refs_3_.refs_4_ = f32[2,256,2560]{2,1,0:T(8,128)} custom-call(s32[12]{0:T(128)S(1)} %pad_add_fusion.plan_ref, bf16[256,2048]{1,0:T(8,128)(2,1)} %collective-permute-done.1.refs_0_, bf16[256,2048]{1,0:T(8,128)(2,1)} %collective-permute-done.refs_1_, bf16[256,2048]{1,0:T(8,128)(2,1)} %collective-permute-done.2.refs_2_, ...), custom_call_target="tpu_custom_call" | custom-call | flops 64424509440 | bytes 283115520 | tf_op jit(solution)/shard_map/near_rows/pallas_call | solution.py:159
  74.3 2.2 %gather_fusion.1 = bf16[8,64,2560]{2,1,0:T(8,128)(2,1)} fusion(bf16[4,64,2560]{2,1,0:T(8,128)(2,1)S(1)} %copy-done, s32[1024]{0:T(1024)S(1)} %pad_clamp_fusion), kind=kCustom, calls=%fused_computation.1 | custom fusion | bytes 5242912 | tf_op jit(solution)/shard_map/jit(_take)/gather | solution.py:304
  76.5 4.9 %all-to-all-start.1 = ((bf16[8,64,2560]{2,1,0:T(8,128)(2,1)}), bf16[8,64,2560]{2,1,0:T(8,128)(2,1)}, u32[]{:S(2)}, u32[]{:S(2)}) async-start(bf16[8,64,2560]{2,1,0:T(8,128)(2,1)} %gather_fusion.1), calls=%async_computation.1 | async-start | bytes 5242880 | tf_op jit(solution)/shard_map/all_to_all | solution.py:307
  81.4 1.6 collective-permute-start.14
  83.0 0.5 collective-permute-start.15
  83.5 12.9 %near_rows_more.1.refs_3_.refs_4_ = f32[2,256,2560]{2,1,0:T(8,128)} custom-call(s32[12]{0:T(128)S(1)} %pad_add_fusion.plan_ref, bf16[256,2048]{1,0:T(8,128)(2,1)} %collective-permute-done.3.refs_0_.refs_1_, bf16[256,2048]{1,0:T(8,128)(2,1)} %collective-permute-done.4.refs_1_.refs_2_, bf16[8192,2560]{1,0:T(8,128)(2,1)} %refs_3_.5, ...), custom_call_target="tpu_custom_call" | custom-call | tf_op jit(solution)/shard_map/near_rows_more/pallas_call | solution.py:159
  96.4 1.3 collective-permute-done.6.refs_1_
  97.8 2.1 %collective-permute-done.7.refs_3_.refs_0_ = bf16[256,2048]{1,0:T(8,128)(2,1)} collective-permute-done((bf16[256,2048]{1,0:T(8,128)(2,1)}, bf16[256,2048]{1,0:T(8,128)(2,1)}, u32[]{:S(2)}, u32[]{:S(2)}) %collective-permute-start.7) | collective-permute-done | bytes 1048608 | tf_op jit(solution)/shard_map/ppermute | solution.py:283
  99.9 3.7 %shrink_parts.1 = (f32[128,128]{1,0:T(8,128)S(1)}, f32[128,128]{1,0:T(8,128)S(1)}, f32[128,128]{1,0:T(8,128)S(1)}, f32[128,128]{1,0:T(8,128)S(1)}) custom-call(s32[12]{0:T(128)S(1)} %pad_add_fusion.plan_ref, bf16[256,8192]{1,0:T(8,128)(2,1)S(1)} %copy-done.3, bf16[256,2048]{1,0:T(8,128)(2,1)} %collective-permute-done.3.refs_0_.refs_1_, ...), custom_call_target="tpu_custom_call" | custom-call | flops 1073741824 | bytes 6291456 | tf_op jit(solution)/shard_map/shrink_parts/pallas_call | solution.py:257
  103.6 0.1 collective-permute-start.8
  103.7 2.0 %collective-permute-start.9 = (f32[128,128]{1,0:T(8,128)S(1)}, f32[128,128]{1,0:T(8,128)S(1)}, u32[]{:S(2)}, u32[]{:S(2)}) collective-permute-start(f32[128,128]{1,0:T(8,128)S(1)} %get-tuple-element.42), channel_id=1, source_target_pairs={{0,2},{1,3},{2,0},{3,1},{4,6},{5,7},{6,4},{7,5},{8,10},{9,11},{10,... | collective-permute-start | bytes 196616 | tf_op jit(solution)/shard_map/ppermute | solution.py:283
  105.7 1.4 collective-permute-start.10
  107.1 13.0 %far_rows.1.refs_4_ = f32[1,256,2560]{2,1,0:T(8,128)} custom-call(s32[12]{0:T(128)S(1)} %pad_add_fusion.plan_ref, bf16[256,2048]{1,0:T(8,128)(2,1)} %collective-permute-done.7.refs_3_.refs_0_, bf16[256,2048]{1,0:T(8,128)(2,1)} %collective-permute-done.6.refs_1_, bf16[8192,2560]{1,0:T(8,128)(2,1)} %refs_3_.5, bf16[8192,2560]{1,0:T(8,128)(2,1)} %refs_3_.5), custom_call_target="tpu_custom_call" | custom-call | flops 21474836480 | bytes 94371840 | tf_op jit(solution)/shard_map/far_rows/pallas_call | solution.py:159
  120.2 1.3 collective-permute-done.8
  121.4 2.2 %collective-permute-done.9 = f32[128,128]{1,0:T(8,128)S(1)} collective-permute-done((f32[128,128]{1,0:T(8,128)S(1)}, f32[128,128]{1,0:T(8,128)S(1)}, u32[]{:S(2)}, u32[]{:S(2)}) %collective-permute-start.9) | collective-permute-done | bytes 65568 | tf_op jit(solution)/shard_map/ppermute | solution.py:283
  123.6 1.6 collective-permute-start.17
  125.2 0.5 collective-permute-start.16
  125.7 1.4 collective-permute-start.13
  127.2 1.5 collective-permute-start.11
  128.7 0.5 collective-permute-start.12
  129.2 11.8 %near_rows_rest.1.refs_1_ = f32[2,256,2560]{2,1,0:T(8,128)} custom-call(s32[12]{0:T(128)S(1)} %pad_add_fusion.plan_ref, bf16[256,2048]{1,0:T(8,128)(2,1)S(1)} %collective-permute-done.14.refs_0_, bf16[256,2048]{1,0:T(8,128)(2,1)S(1)} %collective-permute-done.15.refs_1_, bf16[8192,2560]{1,0:T(8,128)(2,1)} %refs_3_.5, ...), custom_call_target="tpu_custom_call" | custom-call | flops 21474836480 | bytes 125829120 | tf_op jit(solution)/shard_map/near_rows_rest/pallas_call | solution.py:159
  141.1 0.7 all-to-all-done.1.refs_5_.refs_6_.refs_7_
  141.8 8.9 %finish_rows.1.refs_8_ = bf16[1024,2560]{1,0:T(8,128)(2,1)} custom-call(s32[12]{0:T(128)S(1)} %pad_add_fusion.plan_ref, f32[1,256,2560]{2,1,0:T(8,128)} %own_rows.1.refs_0_, f32[2,256,2560]{2,1,0:T(8,128)} %near_rows_rest.1.refs_1_, bf16[128,128]{1,0:T(8,128)(2,1)S(1)} %add_convert_fusion.refs_2_, bf16[128,128]{1,0:T(8,128)(2,1)S(1)} %collective-permute-done.16.refs_3_, ...), custom_call_target="tpu_custom_call" | custom-call | flops 503316480 | bytes 11796480 | tf_op jit(solution)/shard_map/finish_rows/pallas_call | solution.py:202
  150.7 0.8 collective-permute-done.12.refs_1_
  151.5 12.8 %last_rows.1 = bf16[1024,2560]{1,0:T(8,128)(2,1)} custom-call(s32[12]{0:T(128)S(1)} %pad_add_fusion.plan_ref, bf16[256,2048]{1,0:T(8,128)(2,1)S(1)} %collective-permute-done.11.refs_0_, bf16[256,2048]{1,0:T(8,128)(2,1)S(1)} %collective-permute-done.12.refs_1_, bf16[8192,2560]{1,0:T(8,128)(2,1)} %refs_3_.5, ...), custom_call_target="tpu_custom_call", output_to_operand_aliasing={{}: (9, {})} | custom-call | flops 10737418240 | bytes 52428800 | tf_op jit(solution)/shard_map/last_rows/pallas_call | solution.py:159
  (34 shorter events, 0.3 us)
Async XLA Ops:
  0.0 74.3 %copy-start = (bf16[4,64,2560]{2,1,0:T(8,128)(2,1)S(1)}, bf16[4,64,2560]{2,1,0:T(8,128)(2,1)}, u32[]{:S(2)}) copy-start(bf16[4,64,2560]{2,1,0:T(8,128)(2,1)} %param.9) | copy-start | bytes 3932164
  3.0 9.3 %copy-start.5 = (s32[32]{0:T(128)S(1)}, s32[32]{0:T(128)}, u32[]{:S(2)}) copy-start(s32[32]{0:T(128)} %param.10) | copy-start | bytes 388
  3.0 9.3 %copy-start.6 = (s32[64]{0:T(128)S(1)}, s32[64]{0:T(128)}, u32[]{:S(2)}) copy-start(s32[64]{0:T(128)} %param.11) | copy-start | bytes 772
  3.0 9.6 %copy-start.4 = (bf16[4,64,2048]{2,1,0:T(8,128)(2,1)S(1)}, bf16[4,64,2048]{2,1,0:T(8,128)(2,1)}, u32[]{:S(2)}) copy-start(bf16[4,64,2048]{2,1,0:T(8,128)(2,1)} %param.8) | copy-start | bytes 3145732
  3.1 41.1 %collective-permute-start.1 = (bf16[256,2048]{1,0:T(8,128)(2,1)}, bf16[256,2048]{1,0:T(8,128)(2,1)}, u32[]{:S(2)}, u32[]{:S(2)}) collective-permute-start(bf16[256,2048]{1,0:T(8,128)(2,1)} %get-tuple-element.50), channel_id=1, source_target_pairs={{0,1},{1,0},{2,3},{3,2},{4,5},{5,4},{6,7},{7,6},{8,9},{9,8},{10,11... | collective-permute-start | bytes 3145736 | tf_op jit(solution)/shard_map/ppermute | solution.py:282
  6.1 38.1 %collective-permute-start.2 = (bf16[256,2048]{1,0:T(8,128)(2,1)}, bf16[256,2048]{1,0:T(8,128)(2,1)}, u32[]{:S(2)}, u32[]{:S(2)}) collective-permute-start(bf16[256,2048]{1,0:T(8,128)(2,1)} %get-tuple-element.49), channel_id=1, source_target_pairs={{0,2},{1,3},{2,0},{3,1},{4,6},{5,7},{6,4},{7,5},{8,10},{9,11},{10,... | collective-permute-start | bytes 3145736 | tf_op jit(solution)/shard_map/ppermute | solution.py:283
  11.8 43.2 %collective-permute-start.5 = (bf16[256,2048]{1,0:T(8,128)(2,1)}, bf16[256,2048]{1,0:T(8,128)(2,1)}, u32[]{:S(2)}, u32[]{:S(2)}) collective-permute-start(bf16[256,2048]{1,0:T(8,128)(2,1)} %get-tuple-element.32), channel_id=1, source_target_pairs={{0,2},{1,3},{2,0},{3,1},{4,6},{5,7},{6,4},{7,5},{8,10},{9,11},{10,... | collective-permute-start | bytes 3145736 | tf_op jit(solution)/shard_map/ppermute | solution.py:283
  12.3 42.7 %collective-permute-start = (bf16[256,2048]{1,0:T(8,128)(2,1)}, bf16[256,2048]{1,0:T(8,128)(2,1)}, u32[]{:S(2)}, u32[]{:S(2)}) collective-permute-start(bf16[256,2048]{1,0:T(8,128)(2,1)} %get-tuple-element.33), channel_id=1, source_target_pairs={{0,1},{1,0},{2,3},{3,2},{4,5},{5,4},{6,7},{7,6},{8,9},{9,8},{10,11... | collective-permute-start | bytes 3145736 | tf_op jit(solution)/shard_map/ppermute | solution.py:282
  14.7 59.6 %all-to-all-start = ((bf16[8,64,2048]{2,1,0:T(8,128)(2,1)}), bf16[8,64,2048]{2,1,0:T(8,128)(2,1)S(1)}, u32[]{:S(2)}, u32[]{:S(2)}) async-start(bf16[8,64,2048]{2,1,0:T(8,128)(2,1)} %gather_fusion), calls=%async_computation | async-start | bytes 4194304 | tf_op jit(solution)/shard_map/all_to_all | solution.py:307
  20.8 2.2 %copy-start.2 = (bf16[256,8192]{1,0:T(8,128)(2,1)S(1)}, bf16[256,8192]{1,0:T(8,128)(2,1)}, u32[]{:S(2)}) copy-start(bf16[256,8192]{1,0:T(8,128)(2,1)} %refs_0_.3) | copy-start | bytes 12582916
  44.1 37.3 %collective-permute-start.4 = (bf16[256,2048]{1,0:T(8,128)(2,1)}, bf16[256,2048]{1,0:T(8,128)(2,1)}, u32[]{:S(2)}, u32[]{:S(2)}) collective-permute-start(bf16[256,2048]{1,0:T(8,128)(2,1)} %get-tuple-element.33), channel_id=1, source_target_pairs={{0,2},{1,3},{2,0},{3,1},{4,6},{5,7},{6,4},{7,5},{8,10},{9,11},{10,... | collective-permute-start | bytes 3145736 | tf_op jit(solution)/shard_map/ppermute | solution.py:283
  45.7 35.7 %collective-permute-start.3 = (bf16[256,2048]{1,0:T(8,128)(2,1)}, bf16[256,2048]{1,0:T(8,128)(2,1)}, u32[]{:S(2)}, u32[]{:S(2)}) collective-permute-start(bf16[256,2048]{1,0:T(8,128)(2,1)} %get-tuple-element.32), channel_id=1, source_target_pairs={{0,1},{1,0},{2,3},{3,2},{4,5},{5,4},{6,7},{7,6},{8,9},{9,8},{10,11... | collective-permute-start | bytes 3145736 | tf_op jit(solution)/shard_map/ppermute | solution.py:282
  54.9 42.8 %collective-permute-start.6 = (bf16[256,2048]{1,0:T(8,128)(2,1)}, bf16[256,2048]{1,0:T(8,128)(2,1)}, u32[]{:S(2)}, u32[]{:S(2)}) collective-permute-start(bf16[256,2048]{1,0:T(8,128)(2,1)} %collective-permute-done.2.refs_2_), channel_id=1, source_target_pairs={{0,1},{1,0},{2,3},{3,2},{4,5},{5,4},{6,7},{7,6},{8,9},{9,8},{10,11... | collective-permute-start | bytes 3145736 | tf_op jit(solution)/shard_map/ppermute | solution.py:282
  55.0 44.9 %collective-permute-start.7 = (bf16[256,2048]{1,0:T(8,128)(2,1)}, bf16[256,2048]{1,0:T(8,128)(2,1)}, u32[]{:S(2)}, u32[]{:S(2)}) collective-permute-start(bf16[256,2048]{1,0:T(8,128)(2,1)} %collective-permute-done.1.refs_0_), channel_id=1, source_target_pairs={{0,2},{1,3},{2,0},{3,1},{4,6},{5,7},{6,4},{7,5},{8,10},{9,11},{10,... | collective-permute-start | bytes 3145736 | tf_op jit(solution)/shard_map/ppermute | solution.py:283
  76.5 65.3 %all-to-all-start.1 = ((bf16[8,64,2560]{2,1,0:T(8,128)(2,1)}), bf16[8,64,2560]{2,1,0:T(8,128)(2,1)}, u32[]{:S(2)}, u32[]{:S(2)}) async-start(bf16[8,64,2560]{2,1,0:T(8,128)(2,1)} %gather_fusion.1), calls=%async_computation.1 | async-start | bytes 5242880 | tf_op jit(solution)/shard_map/all_to_all | solution.py:307
  81.4 45.7 %collective-permute-start.14 = (bf16[256,2048]{1,0:T(8,128)(2,1)}, bf16[256,2048]{1,0:T(8,128)(2,1)S(1)}, u32[]{:S(2)}, u32[]{:S(2)}) collective-permute-start(bf16[256,2048]{1,0:T(8,128)(2,1)} %get-tuple-element.49), channel_id=1, source_target_pairs={{0,1},{1,0},{2,3},{3,2},{4,5},{5,4},{6,7},{7,6},{8,9},{9,8},{10,11... | collective-permute-start | bytes 3145736 | tf_op jit(solution)/shard_map/ppermute | solution.py:282
  83.0 45.7 %collective-permute-start.15 = (bf16[256,2048]{1,0:T(8,128)(2,1)}, bf16[256,2048]{1,0:T(8,128)(2,1)S(1)}, u32[]{:S(2)}, u32[]{:S(2)}) collective-permute-start(bf16[256,2048]{1,0:T(8,128)(2,1)} %get-tuple-element.50), channel_id=1, source_target_pairs={{0,2},{1,3},{2,0},{3,1},{4,6},{5,7},{6,4},{7,5},{8,10},{9,11},{10,... | collective-permute-start | bytes 3145736 | tf_op jit(solution)/shard_map/ppermute | solution.py:283
  83.5 16.4 %copy-start.3 = (bf16[256,8192]{1,0:T(8,128)(2,1)S(1)}, bf16[256,8192]{1,0:T(8,128)(2,1)}, u32[]{:S(2)}) copy-start(bf16[256,8192]{1,0:T(8,128)(2,1)} %refs_0_.3) | copy-start | bytes 12582916
  103.6 17.8 %collective-permute-start.8 = (f32[128,128]{1,0:T(8,128)S(1)}, f32[128,128]{1,0:T(8,128)S(1)}, u32[]{:S(2)}, u32[]{:S(2)}) collective-permute-start(f32[128,128]{1,0:T(8,128)S(1)} %get-tuple-element.41), channel_id=1, source_target_pairs={{0,1},{1,0},{2,3},{3,2},{4,5},{5,4},{6,7},{7,6},{8,9},{9,8},{10,11... | collective-permute-start | bytes 196616 | tf_op jit(solution)/shard_map/ppermute | solution.py:282
  103.7 19.9 %collective-permute-start.9 = (f32[128,128]{1,0:T(8,128)S(1)}, f32[128,128]{1,0:T(8,128)S(1)}, u32[]{:S(2)}, u32[]{:S(2)}) collective-permute-start(f32[128,128]{1,0:T(8,128)S(1)} %get-tuple-element.42), channel_id=1, source_target_pairs={{0,2},{1,3},{2,0},{3,1},{4,6},{5,7},{6,4},{7,5},{8,10},{9,11},{10,... | collective-permute-start | bytes 196616 | tf_op jit(solution)/shard_map/ppermute | solution.py:283
  105.7 17.9 %collective-permute-start.10 = (f32[128,128]{1,0:T(8,128)S(1)}, f32[128,128]{1,0:T(8,128)S(1)}, u32[]{:S(2)}, u32[]{:S(2)}) collective-permute-start(f32[128,128]{1,0:T(8,128)S(1)} %get-tuple-element.43), channel_id=1, source_target_pairs={{0,3},{1,2},{2,1},{3,0},{4,7},{5,6},{6,5},{7,4},{8,11},{9,10},{10,... | collective-permute-start | bytes 196616 | tf_op jit(solution)/shard_map/ppermute | solution.py:284
  123.6 17.5 %collective-permute-start.17 = (bf16[128,128]{1,0:T(8,128)(2,1)S(1)}, bf16[128,128]{1,0:T(8,128)(2,1)S(1)}, u32[]{:S(2)}, u32[]{:S(2)}) collective-permute-start(bf16[128,128]{1,0:T(8,128)(2,1)S(1)} %add_convert_fusion.refs_2_), channel_id=1, source_target_pairs={{0,2},{1,3},{2,0},{3,1},{4,6},{5,7},{6,4},{7,5},{8,10},{9,11},{10,... | collective-permute-start | bytes 98312 | tf_op jit(solution)/shard_map/ppermute | solution.py:283
  125.2 15.9 %collective-permute-start.16 = (bf16[128,128]{1,0:T(8,128)(2,1)S(1)}, bf16[128,128]{1,0:T(8,128)(2,1)S(1)}, u32[]{:S(2)}, u32[]{:S(2)}) collective-permute-start(bf16[128,128]{1,0:T(8,128)(2,1)S(1)} %add_convert_fusion.refs_2_), channel_id=1, source_target_pairs={{0,1},{1,0},{2,3},{3,2},{4,5},{5,4},{6,7},{7,6},{8,9},{9,8},{10,11... | collective-permute-start | bytes 98312 | tf_op jit(solution)/shard_map/ppermute | solution.py:282
  125.7 25.0 %collective-permute-start.13 = (bf16[128,128]{1,0:T(8,128)(2,1)S(1)}, bf16[128,128]{1,0:T(8,128)(2,1)S(1)}, u32[]{:S(2)}, u32[]{:S(2)}) collective-permute-start(bf16[128,128]{1,0:T(8,128)(2,1)S(1)} %add_convert_fusion.refs_2_), channel_id=1, source_target_pairs={{0,3},{1,2},{2,1},{3,0},{4,7},{5,6},{6,5},{7,4},{8,11},{9,10},{10,... | collective-permute-start | bytes 98312 | tf_op jit(solution)/shard_map/ppermute | solution.py:284
  127.2 23.6 %collective-permute-start.11 = (bf16[256,2048]{1,0:T(8,128)(2,1)}, bf16[256,2048]{1,0:T(8,128)(2,1)S(1)}, u32[]{:S(2)}, u32[]{:S(2)}) collective-permute-start(bf16[256,2048]{1,0:T(8,128)(2,1)} %collective-permute-done.refs_1_), channel_id=1, source_target_pairs={{0,2},{1,3},{2,0},{3,1},{4,6},{5,7},{6,4},{7,5},{8,10},{9,11},{10,... | collective-permute-start | bytes 3145736 | tf_op jit(solution)/shard_map/ppermute | solution.py:283
  128.7 22.8 %collective-permute-start.12 = (bf16[256,2048]{1,0:T(8,128)(2,1)}, bf16[256,2048]{1,0:T(8,128)(2,1)S(1)}, u32[]{:S(2)}, u32[]{:S(2)}) collective-permute-start(bf16[256,2048]{1,0:T(8,128)(2,1)} %collective-permute-done.5.refs_3_), channel_id=1, source_target_pairs={{0,1},{1,0},{2,3},{3,2},{4,5},{5,4},{6,7},{7,6},{8,9},{9,8},{10,11... | collective-permute-start | bytes 3145736 | tf_op jit(solution)/shard_map/ppermute | solution.py:282
  151.5 12.8 %copy-start.1 = (bf16[4,64,2560]{2,1,0:T(8,128)(2,1)S(1)}, bf16[4,64,2560]{2,1,0:T(8,128)(2,1)}, u32[]{:S(2)}) copy-start(bf16[4,64,2560]{2,1,0:T(8,128)(2,1)} %param.9) | copy-start | bytes 3932164
